TPU v7x, 512 devices: a whole 4x8x8 slice. The times are simulated.
512 devices in a mesh: src: 16 (over y_lo, z), row: 32 (over x, y_hi, core).
Axes of the slice: x: 4, y: 8 (y_hi: 4, y_lo: 2; y = y_hi * 2 + y_lo), z: 8, core: 2. Of those that a mesh axis runs over, the one named last changes fastest.
Arguments:
- rhs_panels: bfloat16 [5, 2048, 2048], P(None, 'row', 'src'), may hold values from -6 to 6
- coupling: bfloat16 [10, 2048, 2048], P(None, 'row'), may hold values from -0.0625 to 0.0625
- block_inverse: bfloat16 [5, 2048, 2048], P(None, 'row'), as said below
- quadrupoles: int32 [16, 1024, 4], replicated, may hold values from 0 to 2047
- misfit: float32 [16, 1024], replicated, may hold values from -0.046875 to 0.046875
Outputs:
- potential: float32 [5, 2048, 2048], P(None, 'row', 'src')
- gradient: float32 [16, 5, 2048], P(None, None, ('row', 'src'))
Inputs may be any that keep to these rules, and one draw needn't show every extreme that they name: Every block of block_inverse is symmetric positive definite.
All inputs are finite; a program needn't handle non-finite values.
Results may differ from a plain program's by a relative error of at most 0.025.
Values may be sent and summed in bfloat16 or wider, within the bound.
No kernel may reach another device: no remote copies, remote signals or barrier semaphores. Data moves between devices by JAX's collectives and lax.ppermute only.
A program may use at most 64 MiB of HBM per device.

v0:
```python
import jax
import jax.numpy as jnp
from jax import lax
from jax.sharding import PartitionSpec as P


def pair_index(later, earlier):
    return later * (later - 1) // 2 + earlier


def contract_rows(left, right):
    return lax.dot_general(
        left, right, (((0,), (0,)), ((), ())), preferred_element_type=jnp.float32
    )


def shards(rhs_panels, coupling, block_inverse, quadrupoles, misfit):
    panels = rhs_panels.shape[0]
    local_width = rhs_panels.shape[2]
    gathered_u = []
    for panel in range(panels):
        total = rhs_panels[panel].astype(jnp.float32)
        for earlier in range(panel):
            total = total - jnp.dot(
                coupling[pair_index(panel, earlier)],
                gathered_u[earlier],
                preferred_element_type=jnp.float32,
            )
        gathered_u.append(lax.all_gather(total.astype(jnp.bfloat16), "row", axis=0, tiled=True))
    solved = [None] * panels
    rounded = [None] * panels
    for panel in reversed(range(panels)):
        total = jnp.dot(block_inverse[panel], gathered_u[panel], preferred_element_type=jnp.float32)
        if panel < panels - 1:

            def coupling_term(start, count, panel=panel):
                term = jnp.zeros((count, local_width), jnp.float32)
                for later in range(panel + 1, panels):
                    piece = coupling[pair_index(later, panel)]
                    term = term + contract_rows(piece, rounded[later])
                return term

            total = total - lax.psum_scatter(
                coupling_term(jnp.int32(0), total.shape[0] * lax.axis_size("row")).astype(
                    jnp.bfloat16
                ),
                "row",
                scatter_dimension=0,
                tiled=True,
            ).astype(jnp.float32)
        solved[panel] = total
        rounded[panel] = total.astype(jnp.bfloat16)
    potential = jnp.stack(solved)
    transposed = lax.all_to_all(jnp.stack(rounded), "src", split_axis=1, concat_axis=2, tiled=True)
    node_rows = transposed.shape[1]
    flat = transposed.reshape(panels * node_rows, transposed.shape[2])
    frames, measures = misfit.shape
    columns = quadrupoles.reshape(frames * measures, 4)

    def picked(which):
        return jnp.take(flat, columns[:, which], axis=1).astype(jnp.float32)

    source_diff = picked(0) - picked(1)
    measure_diff = picked(2) - picked(3)
    product = (source_diff * measure_diff).reshape(panels * node_rows, frames, measures)
    gradient = jnp.einsum("rfm,fm->fr", product, misfit, precision=lax.Precision.HIGHEST)
    return (potential, gradient.reshape(frames, panels, node_rows))


def solution(mesh):
    return jax.shard_map(
        shards,
        mesh=mesh,
        in_specs=(P(None, "row", "src"), P(None, "row", None), P(None, "row", None), P(), P()),
        out_specs=(P(None, "row", "src"), P(None, None, ("row", "src"))),
        check_vma=False,
    )
```

profile of v0, /device:TPU:1, one launch (start us, length us, event | category | flops | bytes accessed | tf_op | source)
XLA Modules:
  0.0 898.8 jit_solution(17615877792495668269)
XLA Ops:
  8.1 48.3 %all-gather = bf16[1,2048,128]{2,1,0:T(8,128)(2,1)S(1)} all-gather(bf16[1,64,128]{2,1,0:T(8,128)(2,1)S(1)} %slice.83), channel_id=2, replica_groups=mesh['src'=16,'row'=32] {'row'}, dimensions={1}, use_global_device_ids=true | all-gather | bytes 540672 | tf_op jit(solution)/shard_map/all_gather | solution.py:29
  56.4 1.2 fusion.16
  57.6 1.2 convolution_subtract_fusion.2
  58.7 1.2 convolution_subtract_fusion.1
  59.9 1.2 convolution_subtract_fusion
  61.1 41.8 %all_gather.16 = bf16[2048,128]{1,0:T(8,128)(2,1)S(1)} all-gather(bf16[64,128]{1,0:T(8,128)(2,1)S(1)} %fusion.16), channel_id=1, replica_groups=mesh['src'=16,'row'=32] {'row'}, dimensions={0}, use_global_device_ids=true | all-gather | bytes 540672 | tf_op jit(solution)/shard_map/all_gather | solution.py:29
  103.6 41.9 %all_gather.17 = bf16[2048,128]{1,0:T(8,128)(2,1)S(1)} all-gather(bf16[64,128]{1,0:T(8,128)(2,1)S(1)} %fusion.17), channel_id=1, replica_groups=mesh['src'=16,'row'=32] {'row'}, dimensions={0}, use_global_device_ids=true | all-gather | bytes 540672 | tf_op jit(solution)/shard_map/all_gather | solution.py:29
  146.0 41.6 %all_gather.18 = bf16[2048,128]{1,0:T(8,128)(2,1)S(1)} all-gather(bf16[64,128]{1,0:T(8,128)(2,1)S(1)} %fusion.18), channel_id=1, replica_groups=mesh['src'=16,'row'=32] {'row'}, dimensions={0}, use_global_device_ids=true | all-gather | bytes 540672 | tf_op jit(solution)/shard_map/all_gather | solution.py:29
  187.8 42.0 %all_gather.19 = bf16[2048,128]{1,0:T(8,128)(2,1)S(1)} all-gather(bf16[64,128]{1,0:T(8,128)(2,1)S(1)} %fusion.19), channel_id=1, replica_groups=mesh['src'=16,'row'=32] {'row'}, dimensions={0}, use_global_device_ids=true | all-gather | bytes 540672 | tf_op jit(solution)/shard_map/all_gather | solution.py:29
  231.8 2.2 fusion.88
  234.0 89.4 %reduce-scatter.5.cloned.1.call-done = bf16[64,128]{1,0:T(8,128)(2,1)} async-done(((bf16[2048,128]{1,0:T(8,128)(2,1)}), bf16[64,128]{1,0:T(8,128)(2,1)}) %reduce-scatter.5.cloned.1.call-update) | async-done | bytes 16400 | tf_op jit(solution)/shard_map/reduce_scatter | solution.py:43
  323.4 1.5 fusion.89
  325.5 1.3 fusion.36
  326.9 2.1 fusion.6
  329.1 94.2 %reduce-scatter.7.cloned.1.call-done = bf16[64,128]{1,0:T(8,128)(2,1)} async-done(((bf16[2048,128]{1,0:T(8,128)(2,1)}), bf16[64,128]{1,0:T(8,128)(2,1)}) %reduce-scatter.7.cloned.1.call-update) | async-done | bytes 16400 | tf_op jit(solution)/shard_map/reduce_scatter | solution.py:43
  424.3 1.3 fusion.44
  425.6 1.3 convolution_add_fusion.4
  426.9 2.1 fusion.5
  429.2 94.3 %reduce-scatter.9.cloned.1.call-done = bf16[64,128]{1,0:T(8,128)(2,1)} async-done(((bf16[2048,128]{1,0:T(8,128)(2,1)}), bf16[64,128]{1,0:T(8,128)(2,1)}) %reduce-scatter.9.cloned.1.call-update) | async-done | bytes 16400 | tf_op jit(solution)/shard_map/reduce_scatter | solution.py:43
  524.4 1.3 fusion.50
  525.7 1.3 convolution_add_fusion.2
  527.0 1.3 convolution_add_fusion.1
  528.4 2.1 fusion.4
  530.6 94.3 %reduce-scatter.11.cloned.1.call-done = bf16[64,128]{1,0:T(8,128)(2,1)} async-done(((bf16[2048,128]{1,0:T(8,128)(2,1)}), bf16[64,128]{1,0:T(8,128)(2,1)}) %reduce-scatter.11.cloned.1.call-update) | async-done | bytes 16400 | tf_op jit(solution)/shard_map/reduce_scatter | solution.py:43
  626.7 7.3 all-to-all-start
  634.0 7.4 all-to-all-done
  641.8 57.4 %gather_fusion.3 = bf16[16384,20]{1,0:T(8,128)(2,1)} fusion(bf16[20,2048]{0,1:T(8,128)(2,1)S(1)} %copy.47, s32[16384]{0:T(1024)S(1)} %fusion.84), kind=kCustom, calls=%fused_computation.3.clone | custom fusion | bytes 1376256 | tf_op jit(solution)/shard_map/jit(_take)/gather | solution.py:61
  699.2 57.4 %gather_fusion.2 = bf16[16384,20]{1,0:T(8,128)(2,1)} fusion(bf16[20,2048]{0,1:T(8,128)(2,1)S(1)} %copy.47, s32[16384]{0:T(1024)S(1)} %fusion.83), kind=kCustom, calls=%fused_computation.2.clone | custom fusion | bytes 1376256 | tf_op jit(solution)/shard_map/jit(_take)/gather | solution.py:61
  756.5 57.4 %gather_fusion.1 = bf16[16384,20]{1,0:T(8,128)(2,1)} fusion(bf16[20,2048]{0,1:T(8,128)(2,1)S(1)} %copy.47, s32[16384]{0:T(1024)S(1)} %fusion.82), kind=kCustom, calls=%fused_computation.1.clone | custom fusion | bytes 1376256 | tf_op jit(solution)/shard_map/jit(_take)/gather | solution.py:61
  813.9 57.4 %gather_fusion = bf16[16384,20]{1,0:T(8,128)(2,1)} fusion(bf16[20,2048]{0,1:T(8,128)(2,1)S(1)} %copy.47, s32[16384]{0:T(1024)S(1)} %fusion.81), kind=kCustom, calls=%fused_computation.clone | custom fusion | bytes 1376256 | tf_op jit(solution)/shard_map/jit(_take)/gather | solution.py:61
  871.3 15.6 %subtract_multiply_fusion = f32[20,16384]{0,1:T(8,128)S(1)} fusion(bf16[16384,20]{1,0:T(8,128)(2,1)} %gather_fusion.3, bf16[16384,20]{1,0:T(8,128)(2,1)} %gather_fusion.2, bf16[16384,20]{1,0:T(8,128)(2,1)} %gather_fusion.1, bf16[16384,20]{1,0:T(8,128)(2,1)} %gather_fusion, pred[16384]{0:T(1024)(128)(4,1)S(1)} %get-tuple-element.13, ...), kind=kLoop, calls=%fused_computation.4 | loop fusion | flops 3604480 | bytes 3997696 | tf_op jit(solution)/shard_map/mul | solution.py:65
  887.0 4.5 fusion.79
  (64 shorter events, 10.0 us)
Async XLA Ops:
  7.2 879.8 %copy-start = (f32[16,1024]{1,0:T(8,128)S(1)}, f32[16,1024]{1,0:T(8,128)}, u32[]{:S(2)}) copy-start(f32[16,1024]{1,0:T(8,128)} %param.11) | copy-start | bytes 196612
  7.2 316.2 %reduce-scatter.5.cloned.1.call-start = ((), (), s32[]{:S(2)}) async-start(), calls=%async_computation.5 | async-start | bytes 540672 | tf_op jit(solution)/shard_map/reduce_scatter | solution.py:43
  7.2 95.7 %copy-start.1 = (bf16[10,64,2048]{2,1,0:T(8,128)(2,1)S(1)}, bf16[10,64,2048]{2,1,0:T(8,128)(2,1)}, u32[]{:S(2)}) copy-start(bf16[10,64,2048]{2,1,0:T(8,128)(2,1)} %param.8) | copy-start | bytes 7864324
  103.3 126.4 %copy-start.2 = (bf16[5,64,2048]{2,1,0:T(8,128)(2,1)S(1)}, bf16[5,64,2048]{2,1,0:T(8,128)(2,1)}, u32[]{:S(2)}) copy-start(bf16[5,64,2048]{2,1,0:T(8,128)(2,1)} %param.9) | copy-start | bytes 3932164
  231.8 191.6 %reduce-scatter.7.cloned.1.call-start = ((), (), s32[]{:S(2)}) async-start(), calls=%async_computation.6 | async-start | bytes 540672 | tf_op jit(solution)/shard_map/reduce_scatter | solution.py:43
  324.9 0.6 copy-start.6
  324.9 4.1 copy-start.5
  324.9 4.1 copy-start.4
  326.8 98.8 %copy-start.7 = (bf16[64,128]{1,0:T(8,128)(2,1)S(1)}, bf16[64,128]{1,0:T(8,128)(2,1)}, u32[]{:S(2)}) copy-start(bf16[64,128]{1,0:T(8,128)(2,1)} %copy-done.6) | copy-start | bytes 49156
  329.0 194.5 %reduce-scatter.9.cloned.1.call-start = ((), (), s32[]{:S(2)}) async-start(), calls=%async_computation.7 | async-start | bytes 540672 | tf_op jit(solution)/shard_map/reduce_scatter | solution.py:43
  429.1 195.9 %reduce-scatter.11.cloned.1.call-start = ((), (), s32[]{:S(2)}) async-start(), calls=%async_computation.8 | async-start | bytes 540672 | tf_op jit(solution)/shard_map/reduce_scatter | solution.py:43
  527.0 3.5 copy-start.3
  528.4 105.6 %copy-start.9 = (f32[64,128]{1,0:T(8,128)S(1)}, f32[64,128]{1,0:T(8,128)}, u32[]{:S(2)}) copy-start(f32[64,128]{1,0:T(8,128)} %get-tuple-element.10) | copy-start | bytes 98308
  528.4 105.6 %copy-start.8 = (f32[128,64]{0,1:T(8,128)S(1)}, f32[128,64]{0,1:T(8,128)}, u32[]{:S(2)}) copy-start(f32[128,64]{0,1:T(8,128)} %get-tuple-element.8) | copy-start | bytes 98308
  626.7 14.7 %all-to-all-start = ((bf16[5,64,128]{2,0,1:T(8,128)(2,1)}), bf16[5,64,128]{2,0,1:T(8,128)(2,1)S(1)}, u32[]{:S(2)}, u32[]{:S(2)}) async-start(bf16[5,64,128]{2,0,1:T(8,128)(2,1)} %copy.45), calls=%async_computation.4 | async-start | bytes 262144 | tf_op jit(solution)/shard_map/all_to_all | solution.py:54
  634.0 65.2 %copy-start.10 = (f32[5,64,128]{2,1,0:T(8,128)}, f32[5,64,128]{2,1,0:T(8,128)S(1)}, u32[]{:S(2)}) copy-start(f32[5,64,128]{2,1,0:T(8,128)S(1)} %bitcast_dynamic-update-slice_fusion) | copy-start | bytes 491524
Sparse Core Ops, SparseCore 0:
  231.9 91.4 reduce-scatter.4
  329.1 94.2 reduce-scatter.6
  429.2 94.2 reduce-scatter.8
  530.6 94.2 reduce-scatter.10
where the time goes:
time: 901 us; the launch traced here: 899 us
  waiting for transfers between devices  380 us (42%)
  local copies, waits for them, and re-layouts  235 us (26%)
  blocking collectives  215 us (24%)
  matrix products  31.1 us (3%)
  other arithmetic  15.8 us (2%)
  between operations  14.2 us (2%)
    reduce_scatter x4, waiting for transfers between devices, shards(): lax.psum_scatter(coupling_term(jnp.int32(0), total.shape[0] * lax.axis_si...  372 us
    gather x4, local copies, waits for them, and re-layouts, picked(): return jnp.take(flat, columns[:, which], axis=1).astype(jnp.float32)  230 us
    all_gather x5, blocking collectives, shards(): lax.all_gather(total.astype(jnp.bfloat16), 'row', axis=0, tiled=True)  215 us
  transfers between devices with their start and end apart: 5, of which 5 were waited for; matrix products, arithmetic and copies ran while one was open for 0% of the time, Pallas kernels for 0%

commit v1 on v0

v1 whole, which is shorter than its diff:
```python
import jax
import jax.numpy as jnp
from jax import lax
from jax.sharding import PartitionSpec as P

BF = jnp.bfloat16
F32 = jnp.float32


def pair_index(later, earlier):
    return later * (later - 1) // 2 + earlier


def dot(left, right, left_dim, right_dim):
    return lax.dot_general(
        left, right, (((left_dim,), (right_dim,)), ((), ())), preferred_element_type=F32
    )


def shards(rhs_panels, coupling, block_inverse, quadrupoles, misfit):
    panels, rows, width = rhs_panels.shape
    size = coupling.shape[2]
    chips = lax.axis_size("row") // 2
    half = width // 2
    core = lax.axis_index("row") % 2
    pairs = [(2 * p + c, 2 * p + 1 - c) for p in range(chips) for c in range(2)]
    same_core = [[2 * p + c for p in range(chips)] for c in range(2)]

    def swap(value):
        return lax.ppermute(value, "row", pairs)

    def in_order(mine, other, axis):
        return jnp.where(
            core == 0,
            jnp.concatenate([mine, other], axis=axis),
            jnp.concatenate([other, mine], axis=axis),
        )

    def exchange(blocks):
        return lax.all_to_all(
            blocks, "row", split_axis=0, concat_axis=0, tiled=True, axis_index_groups=same_core
        )

    def gather(value):
        got = exchange(jnp.broadcast_to(value[None], (chips,) + value.shape))
        return jnp.transpose(got, (1, 0, 2)).reshape(value.shape[0], size)

    flipped = jnp.transpose(rhs_panels, (0, 2, 1))
    keep = lax.dynamic_slice_in_dim(flipped, core * half, half, axis=1)
    send = lax.dynamic_slice_in_dim(flipped, (1 - core) * half, half, axis=1)
    rhs = in_order(keep, swap(send), 2)

    other_coupling = swap(coupling)
    other_inverse = swap(block_inverse)
    stacked = []
    for panel in range(panels):
        blocks = [
            in_order(coupling[i], other_coupling[i], 0)
            for i in (pair_index(later, panel) for later in range(panel + 1, panels))
        ]
        blocks.append(in_order(block_inverse[panel], other_inverse[panel], 0))
        stacked.append(jnp.concatenate(blocks, axis=0))

    tall = 2 * rows
    totals = [rhs[panel].astype(F32) for panel in range(panels)]
    for panel in range(panels):
        full = gather(totals[panel].astype(BF))
        out = dot(full, stacked[panel], 1, 1)
        for at, later in enumerate(range(panel + 1, panels)):
            totals[later] = totals[later] - out[:, at * tall : (at + 1) * tall]
        totals[panel] = out[:, (panels - 1 - panel) * tall :]

    solved = [None] * panels
    rounded = [None] * panels
    for panel in reversed(range(panels)):
        total = totals[panel]
        if panel < panels - 1:
            later = jnp.concatenate(rounded[panel + 1 :], axis=1)
            part = dot(later, stacked[panel][: later.shape[1]], 1, 0).astype(BF)
            part = jnp.transpose(part.reshape(half, chips, tall), (1, 0, 2))
            total = total - jnp.sum(exchange(part).astype(F32), axis=0)
        solved[panel] = total
        rounded[panel] = total.astype(BF)

    solved = jnp.stack(solved)
    keep = lax.dynamic_slice_in_dim(solved, core * rows, rows, axis=2)
    send = lax.dynamic_slice_in_dim(solved, (1 - core) * rows, rows, axis=2)
    potential = jnp.transpose(in_order(keep, swap(send), 1), (0, 2, 1))

    groups = lax.axis_size("src")
    nodes = potential.astype(BF).reshape(panels * rows, width)
    nodes = lax.all_to_all(
        jnp.broadcast_to(nodes[None], (groups,) + nodes.shape),
        "src",
        split_axis=0,
        concat_axis=0,
        tiled=True,
    )
    nodes = jnp.transpose(nodes, (1, 0, 2)).reshape(panels * rows, groups * width)
    frames, measures = misfit.shape
    share = frames // groups
    first = lax.axis_index("src") * share
    quads = lax.dynamic_slice_in_dim(quadrupoles, first, share, axis=0).reshape(share * measures, 4)
    weights = lax.dynamic_slice_in_dim(misfit, first, share, axis=0).reshape(1, share * measures)
    sources = lax.broadcasted_iota(jnp.int32, (groups * width, share * measures), 0)

    def difference(plus, minus):
        hot = (sources == quads[None, :, plus]).astype(BF)
        hot = hot - (sources == quads[None, :, minus]).astype(BF)
        return dot(nodes, hot, 1, 0)

    product = difference(0, 1) * difference(2, 3) * weights
    mine = jnp.sum(product.reshape(panels, groups, rows // groups, share, measures), axis=4)
    mine = jnp.transpose(mine, (1, 3, 0, 2))
    gradient = lax.all_to_all(mine, "src", split_axis=0, concat_axis=0, tiled=True)
    return (potential, gradient.reshape(frames, panels, rows // groups))


def solution(mesh):
    return jax.shard_map(
        shards,
        mesh=mesh,
        in_specs=(P(None, "row", "src"), P(None, "row", None), P(None, "row", None), P(), P()),
        out_specs=(P(None, "row", "src"), P(None, None, ("row", "src"))),
        check_vma=False,
    )
```

time: 901 us -> 257 us (0.29)
  waiting for transfers between devices: 380 us -> 108 us
  local copies, waits for them, and re-layouts: 235 us -> 21.6 us
  blocking collectives: 215 us -> 27 us
  starting transfers between devices: 7.42 us -> 66 us
  matrix products: 31.1 us -> 16.4 us
  between operations: 14.2 us -> 1.21 us
    reduce_scatter x4 -> x0, waiting for transfers between devices: 372 us -> none  [shards(): lax.psum_scatter(coupling_term(jnp.int32(0), total.shape[0] * lax.axis_si...]
    gather x4 -> x0, local copies, waits for them, and re-layouts: 230 us -> none  [picked(): return jnp.take(flat, columns[:, which], axis=1).astype(jnp.float32)]
    all_gather x5 -> x0, blocking collectives: 215 us -> none  [shards(): lax.all_gather(total.astype(jnp.bfloat16), 'row', axis=0, tiled=True)]
    all_to_all x1 -> x9, waiting for transfers between devices: 7.35 us -> 107 us  [the longest x8 75.8 us: exchange(): lax.all_to_all(blocks, 'row', split_axis=0, concat_axis=0, tiled=True, ax...]
    all_to_all x1 -> x9, starting transfers between devices: 7.26 us -> 40.4 us  [the longest x8 30.8 us: exchange(): lax.all_to_all(blocks, 'row', split_axis=0, concat_axis=0, tiled=True, ax...]
    all_to_all x0 -> x2, blocking collectives: none -> 27 us  [the longest x1 13.8 us: shards(): lax.all_to_all(mine, 'src', split_axis=0, concat_axis=0, tiled=True)]
    ppermute x0 -> x4, starting transfers between devices: none -> 25.5 us  [swap(): return lax.ppermute(value, 'row', pairs)]
    mul x1 -> x0, other arithmetic: 15.6 us -> none  [shards(): source_diff * measure_diff]
  transfers between devices with their start and end apart: 5 -> 13, of which waited for: 5 -> 10; matrix products, arithmetic and copies ran while one was open for 0% -> 9% of each run, Pallas kernels for 0% -> 0%
where the time goes in v1:
time: 257 us; the launch traced here: 255 us
  waiting for transfers between devices  108 us (42%)
  starting transfers between devices  66 us (26%)
  blocking collectives  27 us (11%)
  local copies, waits for them, and re-layouts  21.6 us (8%)
  matrix products  16.4 us (6%)
  other arithmetic  14.7 us (6%)
    all_to_all x8, waiting for transfers between devices, exchange(): lax.all_to_all(blocks, 'row', split_axis=0, concat_axis=0, tiled=True, ax...  75.8 us
    all_to_all x1, waiting for transfers between devices, shards(): lax.all_to_all(jnp.broadcast_to(nodes[None], (groups,) + nodes.shape), 's...  31.4 us
    all_to_all x8, starting transfers between devices, exchange(): lax.all_to_all(blocks, 'row', split_axis=0, concat_axis=0, tiled=True, ax...  30.8 us
    ppermute x4, starting transfers between devices, swap(): return lax.ppermute(value, 'row', pairs)  25.5 us
    dot_general x11, matrix products, dot(): lax.dot_general(left, right, (((left_dim,), (right_dim,)), ((), ())), pre...  16.4 us
    all_to_all x1, blocking collectives, shards(): lax.all_to_all(mine, 'src', split_axis=0, concat_axis=0, tiled=True)  13.8 us
    all_to_all x1, blocking collectives, exchange(): lax.all_to_all(blocks, 'row', split_axis=0, concat_axis=0, tiled=True, ax...  13.2 us
    all_to_all x1, starting transfers between devices, shards(): lax.all_to_all(jnp.broadcast_to(nodes[None], (groups,) + nodes.shape), 's...  9.69 us
  transfers between devices with their start and end apart: 13, of which 10 were waited for; matrix products, arithmetic and copies ran while one was open for 9% of the time, Pallas kernels for 0%

profile of v1, /device:TPU:1, one launch (start us, length us, event | category | flops | bytes accessed | tf_op | source)
XLA Modules:
  0.0 255.1 jit_solution(12372277310975333590)
XLA Ops:
  0.6 8.9 %collective-permute-start.1 = (bf16[10,64,2048]{2,1,0:T(8,128)(2,1)}, bf16[10,64,2048]{2,1,0:T(8,128)(2,1)S(1)}, u32[]{:S(2)}, u32[]{:S(2)}) collective-permute-start(bf16[10,64,2048]{2,1,0:T(8,128)(2,1)} %param.6), channel_id=1, source_target_pairs={{0,1},{1,0},{2,3},{3,2},{4,5},{5,4},{6,7},{7,6},{8,9},{9,8},{10,11... | collective-permute-start | bytes 7864328 | tf_op jit(solution)/shard_map/ppermute | solution.py:30
  9.6 1.9 collective-permute-start.2
  13.4 2.5 collective-permute-start
  15.9 3.1 %slice_bitcast_fusion.24 = (bf16[64,2048]{1,0:T(8,128)(2,1)}, bf16[64,2048]{1,0:T(8,128)(2,1)}, bf16[64,2048]{1,0:T(8,128)(2,1)}, bf16[64,2048]{1,0:T(8,128)(2,1...) fusion(bf16[10,64,2048]{2,1,0:T(8,128)(2,1)} %param.6), kind=kLoop, calls=%fused_computation.130 | loop fusion | bytes 5242880 | tf_op jit(solution)/shard_map/squeeze | solution.py:58
  22.6 4.2 %all-to-all-start = ((bf16[16,64,128]{2,1,0:T(8,128)(2,1)}), bf16[16,64,128]{2,1,0:T(8,128)(2,1)}, u32[]{:S(2)}, u32[]{:S(2)}) async-start(bf16[16,64,128]{2,1,0:T(8,128)(2,1)} %broadcast_in_dim.17), calls=%async_computation | async-start | bytes 524288 | tf_op jit(solution)/shard_map/all_to_all | solution.py:40
  26.8 2.3 slice_bitcast_fusion.6
  34.2 5.2 %all-to-all-done = bf16[16,64,128]{2,1,0:T(8,128)(2,1)} async-done(((bf16[16,64,128]{2,1,0:T(8,128)(2,1)}), bf16[16,64,128]{2,1,0:T(8,128)(2,1)}, u32[]{:S(2)}, u32[]{:S(2)}) %all-to-all-start) | async-done | bytes 262176 | tf_op jit(solution)/shard_map/all_to_all | solution.py:40
  39.4 1.9 fusion.88
  42.7 4.0 %all-to-all-start.1 = ((bf16[16,64,128]{2,1,0:T(8,128)(2,1)}), bf16[16,64,128]{2,1,0:T(8,128)(2,1)S(1)}, u32[]{:S(2)}, u32[]{:S(2)}) async-start(bf16[16,64,128]{2,1,0:T(8,128)(2,1)} %broadcast_in_dim.18), calls=%async_computation.1 | async-start | bytes 524288 | tf_op jit(solution)/shard_map/all_to_all | solution.py:40
  46.7 2.7 %maximum_select_fusion.5 = (bf16[128,2048]{1,0:T(8,128)(2,1)S(1)}, bf16[128,2048]{1,0:T(8,128)(2,1)}) fusion(bf16[64,2048]{1,0:T(8,128)(2,1)} %get-tuple-element.32, bf16[64,2048]{1,0:T(8,128)(2,1)} %get-tuple-element.22, pred[]{:T(512)S(6)} %eq.28, bf16[64,2048]{1,0:T(8,128)(2,1)} %get-tuple-element.25, bf16[64,2048]{1,0:T(8,128)(2,1)} %get-tuple-element.37), kind=kLoop, calls=%fused_computation.70 | loop fusion | flops 4718592 | bytes 2097153 | tf_op jit(solution)/shard_map/jit(_where)/select_n | solution.py:33
  50.7 8.1 %all-to-all-done.1 = bf16[16,64,128]{2,1,0:T(8,128)(2,1)S(1)} async-done(((bf16[16,64,128]{2,1,0:T(8,128)(2,1)}), bf16[16,64,128]{2,1,0:T(8,128)(2,1)S(1)}, u32[]{:S(2)}, u32[]{:S(2)}) %all-to-all-start.1) | async-done | bytes 262176 | tf_op jit(solution)/shard_map/all_to_all | solution.py:40
  58.9 2.2 fusion.16
  62.5 4.3 %all-to-all-start.2 = ((bf16[16,64,128]{2,1,0:T(8,128)(2,1)}), bf16[16,64,128]{2,1,0:T(8,128)(2,1)S(1)}, u32[]{:S(2)}, u32[]{:S(2)}) async-start(bf16[16,64,128]{2,1,0:T(8,128)(2,1)} %broadcast_in_dim.19), calls=%async_computation.2 | async-start | bytes 524288 | tf_op jit(solution)/shard_map/all_to_all | solution.py:40
  68.8 10.6 %all-to-all-done.2 = bf16[16,64,128]{2,1,0:T(8,128)(2,1)S(1)} async-done(((bf16[16,64,128]{2,1,0:T(8,128)(2,1)}), bf16[16,64,128]{2,1,0:T(8,128)(2,1)S(1)}, u32[]{:S(2)}, u32[]{:S(2)}) %all-to-all-start.2) | async-done | bytes 262176 | tf_op jit(solution)/shard_map/all_to_all | solution.py:40
  82.8 4.2 %all-to-all-start.3 = ((bf16[16,64,128]{2,1,0:T(8,128)(2,1)}), bf16[16,64,128]{2,1,0:T(8,128)(2,1)}, u32[]{:S(2)}, u32[]{:S(2)}) async-start(bf16[16,64,128]{2,1,0:T(8,128)(2,1)} %broadcast_in_dim.20), calls=%async_computation.3 | async-start | bytes 524288 | tf_op jit(solution)/shard_map/all_to_all | solution.py:40
  88.1 10.3 %all-to-all-done.3 = bf16[16,64,128]{2,1,0:T(8,128)(2,1)} async-done(((bf16[16,64,128]{2,1,0:T(8,128)(2,1)}), bf16[16,64,128]{2,1,0:T(8,128)(2,1)}, u32[]{:S(2)}, u32[]{:S(2)}) %all-to-all-start.3) | async-done | bytes 262176 | tf_op jit(solution)/shard_map/all_to_all | solution.py:40
  100.9 13.2 %all_to_all.55 = bf16[16,64,128]{2,1,0:T(8,128)(2,1)S(1)} all-to-all(bf16[16,64,128]{2,1,0:T(8,128)(2,1)S(1)} %broadcast_in_dim.21), channel_id=1, replica_groups={{0,2,4,6,8,10,12,14,16,18,20,22,24,26,28,30},{1,3,5,7,9,11,13,15,17,19,..., dimensions={0} | all-to-all | bytes 524288 | tf_op jit(solution)/shard_map/all_to_all | solution.py:40
  115.5 3.5 %all-to-all-start.5 = ((bf16[16,64,128]{2,1,0:T(8,128)(2,1)}), bf16[16,64,128]{2,1,0:T(8,128)(2,1)S(1)}, u32[]{:S(2)}, u32[]{:S(2)}) async-start(bf16[16,64,128]{2,1,0:T(8,128)(2,1)} %bitcast.198), calls=%async_computation.5 | async-start | bytes 524288 | tf_op jit(solution)/shard_map/all_to_all | solution.py:40
  119.1 10.5 %all-to-all-done.5 = bf16[16,64,128]{2,1,0:T(8,128)(2,1)S(1)} async-done(((bf16[16,64,128]{2,1,0:T(8,128)(2,1)}), bf16[16,64,128]{2,1,0:T(8,128)(2,1)S(1)}, u32[]{:S(2)}, u32[]{:S(2)}) %all-to-all-start.5) | async-done | bytes 262176 | tf_op jit(solution)/shard_map/all_to_all | solution.py:40
  131.9 3.5 %all-to-all-start.6 = ((bf16[16,64,128]{2,1,0:T(8,128)(2,1)}), bf16[16,64,128]{2,1,0:T(8,128)(2,1)S(1)}, u32[]{:S(2)}, u32[]{:S(2)}) async-start(bf16[16,64,128]{2,1,0:T(8,128)(2,1)} %bitcast.196), calls=%async_computation.6 | async-start | bytes 524288 | tf_op jit(solution)/shard_map/all_to_all | solution.py:40
  135.6 10.3 %all-to-all-done.6 = bf16[16,64,128]{2,1,0:T(8,128)(2,1)S(1)} async-done(((bf16[16,64,128]{2,1,0:T(8,128)(2,1)}), bf16[16,64,128]{2,1,0:T(8,128)(2,1)S(1)}, u32[]{:S(2)}, u32[]{:S(2)}) %all-to-all-start.6) | async-done | bytes 262176 | tf_op jit(solution)/shard_map/all_to_all | solution.py:40
  147.3 3.5 %all-to-all-start.7 = ((bf16[16,64,128]{2,1,0:T(8,128)(2,1)}), bf16[16,64,128]{2,1,0:T(8,128)(2,1)S(1)}, u32[]{:S(2)}, u32[]{:S(2)}) async-start(bf16[16,64,128]{2,1,0:T(8,128)(2,1)} %bitcast.194), calls=%async_computation.7 | async-start | bytes 524288 | tf_op jit(solution)/shard_map/all_to_all | solution.py:40
  150.9 10.3 %all-to-all-done.7 = bf16[16,64,128]{2,1,0:T(8,128)(2,1)S(1)} async-done(((bf16[16,64,128]{2,1,0:T(8,128)(2,1)}), bf16[16,64,128]{2,1,0:T(8,128)(2,1)S(1)}, u32[]{:S(2)}, u32[]{:S(2)}) %all-to-all-start.7) | async-done | bytes 262176 | tf_op jit(solution)/shard_map/all_to_all | solution.py:40
  161.4 1.9 fusion.60
  164.1 3.5 %all-to-all-start.8 = ((bf16[16,64,128]{2,1,0:T(8,128)(2,1)}), bf16[16,64,128]{2,1,0:T(8,128)(2,1)S(1)}, u32[]{:S(2)}, u32[]{:S(2)}) async-start(bf16[16,64,128]{2,1,0:T(8,128)(2,1)} %bitcast.192), calls=%async_computation.8 | async-start | bytes 524288 | tf_op jit(solution)/shard_map/all_to_all | solution.py:40
  167.7 10.3 %all-to-all-done.8 = bf16[16,64,128]{2,1,0:T(8,128)(2,1)S(1)} async-done(((bf16[16,64,128]{2,1,0:T(8,128)(2,1)}), bf16[16,64,128]{2,1,0:T(8,128)(2,1)S(1)}, u32[]{:S(2)}, u32[]{:S(2)}) %all-to-all-start.8) | async-done | bytes 262176 | tf_op jit(solution)/shard_map/all_to_all | solution.py:40
  178.3 12.2 %collective-permute-start.3 = (f32[5,64,64]{1,2,0:T(8,128)S(1)}, f32[5,64,64]{1,2,0:T(8,128)S(1)}, u32[]{:S(2)}, u32[]{:S(2)}) collective-permute-start(f32[5,64,64]{1,2,0:T(8,128)S(1)} %get-tuple-element.52), channel_id=1, source_target_pairs={{0,1},{1,0},{2,3},{3,2},{4,5},{5,4},{6,7},{7,6},{8,9},{9,8},{10,11... | collective-permute-start | bytes 245768 | tf_op jit(solution)/shard_map/ppermute | solution.py:30
  193.7 9.7 %all-to-all-start.9 = ((bf16[16,320,128]{2,1,0:T(8,128)(2,1)}), bf16[16,320,128]{2,1,0:T(8,128)(2,1)S(1)}, u32[]{:S(2)}, u32[]{:S(2)}) async-start(bf16[16,320,128]{2,1,0:T(8,128)(2,1)} %broadcast_in_dim.46), calls=%async_computation.9 | async-start | bytes 2621440 | tf_op jit(solution)/shard_map/all_to_all | solution.py:92
  204.2 31.4 %all-to-all-done.9 = bf16[16,320,128]{2,1,0:T(8,128)(2,1)S(1)} async-done(((bf16[16,320,128]{2,1,0:T(8,128)(2,1)}), bf16[16,320,128]{2,1,0:T(8,128)(2,1)S(1)}, u32[]{:S(2)}, u32[]{:S(2)}) %all-to-all-start.9) | async-done | bytes 1310752 | tf_op jit(solution)/shard_map/all_to_all | solution.py:92
  235.6 2.2 fusion.5
  237.8 2.4 fusion.50
  240.6 13.8 %all_to_all.56 = f32[16,1,5,4]{2,3,1,0:T(4,128)S(1)} all-to-all(f32[16,1,5,4]{2,3,1,0:T(4,128)S(1)} %copy.73), channel_id=1, replica_groups=mesh['src'=16,'row'=32] {'src'}, dimensions={0} | all-to-all | bytes 2560 | tf_op jit(solution)/shard_map/all_to_all | solution.py:115
  (124 shorter events, 35.0 us)
Async XLA Ops:
  0.6 203.5 %copy-start = (s32[16,1024,4]{1,2,0:T(4,128)S(1)}, s32[16,1024,4]{1,2,0:T(4,128)}, u32[]{:S(2)}) copy-start(s32[16,1024,4]{1,2,0:T(4,128)} %param.8) | copy-start | bytes 786436
  0.6 28.5 %collective-permute-start.1 = (bf16[10,64,2048]{2,1,0:T(8,128)(2,1)}, bf16[10,64,2048]{2,1,0:T(8,128)(2,1)S(1)}, u32[]{:S(2)}, u32[]{:S(2)}) collective-permute-start(bf16[10,64,2048]{2,1,0:T(8,128)(2,1)} %param.6), channel_id=1, source_target_pairs={{0,1},{1,0},{2,3},{3,2},{4,5},{5,4},{6,7},{7,6},{8,9},{9,8},{10,11... | collective-permute-start | bytes 7864328 | tf_op jit(solution)/shard_map/ppermute | solution.py:30
  9.6 17.3 %collective-permute-start.2 = (bf16[5,64,2048]{2,1,0:T(8,128)(2,1)}, bf16[5,64,2048]{2,1,0:T(8,128)(2,1)}, u32[]{:S(2)}, u32[]{:S(2)}) collective-permute-start(bf16[5,64,2048]{2,1,0:T(8,128)(2,1)} %param.7), channel_id=1, source_target_pairs={{0,1},{1,0},{2,3},{3,2},{4,5},{5,4},{6,7},{7,6},{8,9},{9,8},{10,11... | collective-permute-start | bytes 3932168 | tf_op jit(solution)/shard_map/ppermute | solution.py:30
  13.4 7.4 %collective-permute-start = (bf16[5,64,64]{2,1,0:T(8,128)(2,1)}, bf16[5,64,64]{2,1,0:T(8,128)(2,1)}, u32[]{:S(2)}, u32[]{:S(2)}) collective-permute-start(bf16[5,64,64]{2,1,0:T(8,128)(2,1)} %bitcast.1), channel_id=1, source_target_pairs={{0,1},{1,0},{2,3},{3,2},{4,5},{5,4},{6,7},{7,6},{8,9},{9,8},{10,11... | collective-permute-start | bytes 122888 | tf_op jit(solution)/shard_map/ppermute | solution.py:30
  22.6 16.7 %all-to-all-start = ((bf16[16,64,128]{2,1,0:T(8,128)(2,1)}), bf16[16,64,128]{2,1,0:T(8,128)(2,1)}, u32[]{:S(2)}, u32[]{:S(2)}) async-start(bf16[16,64,128]{2,1,0:T(8,128)(2,1)} %broadcast_in_dim.17), calls=%async_computation | async-start | bytes 524288 | tf_op jit(solution)/shard_map/all_to_all | solution.py:40
  41.9 7.5 %copy-start.6 = (bf16[64,2048]{1,0:T(8,128)(2,1)S(1)}, bf16[64,2048]{1,0:T(8,128)(2,1)}, u32[]{:S(2)}) copy-start(bf16[64,2048]{1,0:T(8,128)(2,1)} %get-tuple-element.24) | copy-start | bytes 786436
  41.9 7.5 %copy-start.7 = (bf16[64,2048]{1,0:T(8,128)(2,1)S(1)}, bf16[64,2048]{1,0:T(8,128)(2,1)}, u32[]{:S(2)}) copy-start(bf16[64,2048]{1,0:T(8,128)(2,1)} %get-tuple-element.42) | copy-start | bytes 786436
  41.9 7.5 %copy-start.10 = (bf16[64,2048]{1,0:T(8,128)(2,1)S(1)}, bf16[64,2048]{1,0:T(8,128)(2,1)}, u32[]{:S(2)}) copy-start(bf16[64,2048]{1,0:T(8,128)(2,1)} %get-tuple-element.47) | copy-start | bytes 786436
  41.9 7.5 %copy-start.11 = (bf16[64,2048]{1,0:T(8,128)(2,1)S(1)}, bf16[64,2048]{1,0:T(8,128)(2,1)}, u32[]{:S(2)}) copy-start(bf16[64,2048]{1,0:T(8,128)(2,1)} %get-tuple-element.36) | copy-start | bytes 786436
  42.7 16.1 %all-to-all-start.1 = ((bf16[16,64,128]{2,1,0:T(8,128)(2,1)}), bf16[16,64,128]{2,1,0:T(8,128)(2,1)S(1)}, u32[]{:S(2)}, u32[]{:S(2)}) async-start(bf16[16,64,128]{2,1,0:T(8,128)(2,1)} %broadcast_in_dim.18), calls=%async_computation.1 | async-start | bytes 524288 | tf_op jit(solution)/shard_map/all_to_all | solution.py:40
  58.8 8.0 %copy-start.12 = (bf16[64,2048]{1,0:T(8,128)(2,1)S(1)}, bf16[64,2048]{1,0:T(8,128)(2,1)}, u32[]{:S(2)}) copy-start(bf16[64,2048]{1,0:T(8,128)(2,1)} %get-tuple-element.43) | copy-start | bytes 786436
  58.8 8.0 %copy-start.13 = (bf16[64,2048]{1,0:T(8,128)(2,1)S(1)}, bf16[64,2048]{1,0:T(8,128)(2,1)}, u32[]{:S(2)}) copy-start(bf16[64,2048]{1,0:T(8,128)(2,1)} %get-tuple-element.50) | copy-start | bytes 786436
  58.8 8.9 %copy-start.2 = (bf16[64,2048]{1,0:T(8,128)(2,1)S(1)}, bf16[64,2048]{1,0:T(8,128)(2,1)}, u32[]{:S(2)}) copy-start(bf16[64,2048]{1,0:T(8,128)(2,1)} %get-tuple-element.23) | copy-start | bytes 786436
  58.8 8.9 %copy-start.3 = (bf16[64,2048]{1,0:T(8,128)(2,1)S(1)}, bf16[64,2048]{1,0:T(8,128)(2,1)}, u32[]{:S(2)}) copy-start(bf16[64,2048]{1,0:T(8,128)(2,1)} %get-tuple-element.31) | copy-start | bytes 786436
  58.9 8.9 %copy-start.8 = (bf16[64,2048]{1,0:T(8,128)(2,1)S(1)}, bf16[64,2048]{1,0:T(8,128)(2,1)}, u32[]{:S(2)}) copy-start(bf16[64,2048]{1,0:T(8,128)(2,1)} %get-tuple-element.34) | copy-start | bytes 786436
  58.9 8.9 %copy-start.9 = (bf16[64,2048]{1,0:T(8,128)(2,1)S(1)}, bf16[64,2048]{1,0:T(8,128)(2,1)}, u32[]{:S(2)}) copy-start(bf16[64,2048]{1,0:T(8,128)(2,1)} %get-tuple-element.35) | copy-start | bytes 786436
  62.5 16.8 %all-to-all-start.2 = ((bf16[16,64,128]{2,1,0:T(8,128)(2,1)}), bf16[16,64,128]{2,1,0:T(8,128)(2,1)S(1)}, u32[]{:S(2)}, u32[]{:S(2)}) async-start(bf16[16,64,128]{2,1,0:T(8,128)(2,1)} %broadcast_in_dim.19), calls=%async_computation.2 | async-start | bytes 524288 | tf_op jit(solution)/shard_map/all_to_all | solution.py:40
  79.4 7.6 %copy-start.4 = (bf16[64,2048]{1,0:T(8,128)(2,1)S(1)}, bf16[64,2048]{1,0:T(8,128)(2,1)}, u32[]{:S(2)}) copy-start(bf16[64,2048]{1,0:T(8,128)(2,1)} %get-tuple-element.49) | copy-start | bytes 786436
  79.4 7.6 %copy-start.5 = (bf16[64,2048]{1,0:T(8,128)(2,1)S(1)}, bf16[64,2048]{1,0:T(8,128)(2,1)}, u32[]{:S(2)}) copy-start(bf16[64,2048]{1,0:T(8,128)(2,1)} %get-tuple-element.33) | copy-start | bytes 786436
  81.2 17.2 %copy-start.27 = (f32[64,384]{1,0:T(8,128)}, f32[64,384]{1,0:T(8,128)S(1)}, u32[]{:S(2)}) copy-start(f32[64,384]{1,0:T(8,128)S(1)} %fusion.31) | copy-start | bytes 294916
  82.8 15.6 %all-to-all-start.3 = ((bf16[16,64,128]{2,1,0:T(8,128)(2,1)}), bf16[16,64,128]{2,1,0:T(8,128)(2,1)}, u32[]{:S(2)}, u32[]{:S(2)}) async-start(bf16[16,64,128]{2,1,0:T(8,128)(2,1)} %broadcast_in_dim.20), calls=%async_computation.3 | async-start | bytes 524288 | tf_op jit(solution)/shard_map/all_to_all | solution.py:40
  87.0 27.1 %copy-start.24 = (bf16[64,2048]{1,0:T(8,128)(2,1)S(1)}, bf16[64,2048]{1,0:T(8,128)(2,1)}, u32[]{:S(2)}) copy-start(bf16[64,2048]{1,0:T(8,128)(2,1)} %get-tuple-element.45) | copy-start | bytes 786436
  88.1 26.0 %copy-start.25 = (bf16[64,2048]{1,0:T(8,128)(2,1)S(1)}, bf16[64,2048]{1,0:T(8,128)(2,1)}, u32[]{:S(2)}) copy-start(bf16[64,2048]{1,0:T(8,128)(2,1)} %get-tuple-element.48) | copy-start | bytes 786436
  114.7 31.4 %copy-start.21 = (bf16[128,2048]{1,0:T(8,128)(2,1)S(1)}, bf16[128,2048]{1,0:T(8,128)(2,1)}, u32[]{:S(2)}) copy-start(bf16[128,2048]{1,0:T(8,128)(2,1)} %get-tuple-element.68) | copy-start | bytes 1572868
  114.7 31.4 %copy-start.22 = (bf16[128,2048]{1,0:T(8,128)(2,1)S(1)}, bf16[128,2048]{1,0:T(8,128)(2,1)}, u32[]{:S(2)}) copy-start(bf16[128,2048]{1,0:T(8,128)(2,1)} %get-tuple-element.69) | copy-start | bytes 1572868
  115.5 14.1 %all-to-all-start.5 = ((bf16[16,64,128]{2,1,0:T(8,128)(2,1)}), bf16[16,64,128]{2,1,0:T(8,128)(2,1)S(1)}, u32[]{:S(2)}, u32[]{:S(2)}) async-start(bf16[16,64,128]{2,1,0:T(8,128)(2,1)} %bitcast.198), calls=%async_computation.5 | async-start | bytes 524288 | tf_op jit(solution)/shard_map/all_to_all | solution.py:40
  131.9 14.0 %all-to-all-start.6 = ((bf16[16,64,128]{2,1,0:T(8,128)(2,1)}), bf16[16,64,128]{2,1,0:T(8,128)(2,1)S(1)}, u32[]{:S(2)}, u32[]{:S(2)}) async-start(bf16[16,64,128]{2,1,0:T(8,128)(2,1)} %bitcast.196), calls=%async_computation.6 | async-start | bytes 524288 | tf_op jit(solution)/shard_map/all_to_all | solution.py:40
  146.1 15.4 %copy-start.23 = (bf16[128,2048]{1,0:T(8,128)(2,1)S(1)}, bf16[128,2048]{1,0:T(8,128)(2,1)}, u32[]{:S(2)}) copy-start(bf16[128,2048]{1,0:T(8,128)(2,1)} %get-tuple-element.21) | copy-start | bytes 1572868
  147.3 14.0 %all-to-all-start.7 = ((bf16[16,64,128]{2,1,0:T(8,128)(2,1)}), bf16[16,64,128]{2,1,0:T(8,128)(2,1)S(1)}, u32[]{:S(2)}, u32[]{:S(2)}) async-start(bf16[16,64,128]{2,1,0:T(8,128)(2,1)} %bitcast.194), calls=%async_computation.7 | async-start | bytes 524288 | tf_op jit(solution)/shard_map/all_to_all | solution.py:40
  164.1 14.0 %all-to-all-start.8 = ((bf16[16,64,128]{2,1,0:T(8,128)(2,1)}), bf16[16,64,128]{2,1,0:T(8,128)(2,1)S(1)}, u32[]{:S(2)}, u32[]{:S(2)}) async-start(bf16[16,64,128]{2,1,0:T(8,128)(2,1)} %bitcast.192), calls=%async_computation.8 | async-start | bytes 524288 | tf_op jit(solution)/shard_map/all_to_all | solution.py:40
  178.3 13.2 %collective-permute-start.3 = (f32[5,64,64]{1,2,0:T(8,128)S(1)}, f32[5,64,64]{1,2,0:T(8,128)S(1)}, u32[]{:S(2)}, u32[]{:S(2)}) collective-permute-start(f32[5,64,64]{1,2,0:T(8,128)S(1)} %get-tuple-element.52), channel_id=1, source_target_pairs={{0,1},{1,0},{2,3},{3,2},{4,5},{5,4},{6,7},{7,6},{8,9},{9,8},{10,11... | collective-permute-start | bytes 245768 | tf_op jit(solution)/shard_map/ppermute | solution.py:30
  193.7 41.9 %all-to-all-start.9 = ((bf16[16,320,128]{2,1,0:T(8,128)(2,1)}), bf16[16,320,128]{2,1,0:T(8,128)(2,1)S(1)}, u32[]{:S(2)}, u32[]{:S(2)}) async-start(bf16[16,320,128]{2,1,0:T(8,128)(2,1)} %broadcast_in_dim.46), calls=%async_computation.9 | async-start | bytes 2621440 | tf_op jit(solution)/shard_map/all_to_all | solution.py:92
  (9 other events, 20.8 us)

commit v2 on v1

--- a/solution.py
+++ b/solution.py
@@ -1,6 +1,7 @@
 import jax
 import jax.numpy as jnp
 from jax import lax
+from jax.experimental import pallas as pl
 from jax.sharding import PartitionSpec as P
 
 BF = jnp.bfloat16
@@ -15,6 +16,44 @@
     return lax.dot_general(
         left, right, (((left_dim,), (right_dim,)), ((), ())), preferred_element_type=F32
     )
+
+
+def weigh_kernel(table_ref, picks_ref, weights_ref, out_ref):
+    parts, lines, depth = table_ref.shape
+    frames, _, measures = picks_ref.shape
+    table = table_ref[...].reshape(parts * lines, depth)
+    span = min(256, measures)
+    places = lax.broadcasted_iota(jnp.int32, (depth, span), 0)
+
+    def frame(at, carry):
+        total = jnp.zeros(out_ref.shape[1:], F32)
+        for start in range(0, measures, span):
+            values = []
+            for which in range(4):
+                index = picks_ref[at, which : which + 1, start : start + span]
+                hot = jnp.where(places == index % depth, 1.0, 0.0).astype(BF)
+                found = dot(table, hot, 1, 0)
+                part = index // depth
+                value = found[:lines]
+                for other in range(1, parts):
+                    piece = found[other * lines : (other + 1) * lines]
+                    value = jnp.where(part == other, piece, value)
+                values.append(value)
+            product = (values[0] - values[1]) * (values[2] - values[3])
+            product = product * weights_ref[pl.ds(at, 1), start : start + span]
+            for lane in range(0, span, 128):
+                total = total + product[:, lane : lane + 128]
+        out_ref[at] = total
+        return carry
+
+    lax.fori_loop(0, frames, frame, 0)
+
+
+def weigh(table, picks, weights):
+    return pl.pallas_call(
+        weigh_kernel,
+        out_shape=jax.ShapeDtypeStruct((weights.shape[0], table.shape[1], 128), F32),
+    )(table, picks, weights)
 
 
 def shards(rhs_panels, coupling, block_inverse, quadrupoles, misfit):
@@ -49,6 +88,7 @@
     keep = lax.dynamic_slice_in_dim(flipped, core * half, half, axis=1)
     send = lax.dynamic_slice_in_dim(flipped, (1 - core) * half, half, axis=1)
     rhs = in_order(keep, swap(send), 2)
+    rhs, coupling, block_inverse = lax.optimization_barrier((rhs, coupling, block_inverse))
 
     other_coupling = swap(coupling)
     other_inverse = swap(block_inverse)
@@ -70,8 +110,16 @@
             totals[later] = totals[later] - out[:, at * tall : (at + 1) * tall]
         totals[panel] = out[:, (panels - 1 - panel) * tall :]
 
-    solved = [None] * panels
+    groups = lax.axis_size("src")
+    nodes = rows // groups
+
+    def natural(value):
+        keep = lax.dynamic_slice_in_dim(value, core * rows, rows, axis=1)
+        send = lax.dynamic_slice_in_dim(value, (1 - core) * rows, rows, axis=1)
+        return jnp.transpose(in_order(keep, swap(send), 0))
+
     rounded = [None] * panels
+    potential = [None] * panels
     for panel in reversed(range(panels)):
         total = totals[panel]
         if panel < panels - 1:
@@ -79,41 +127,19 @@
             part = dot(later, stacked[panel][: later.shape[1]], 1, 0).astype(BF)
             part = jnp.transpose(part.reshape(half, chips, tall), (1, 0, 2))
             total = total - jnp.sum(exchange(part).astype(F32), axis=0)
-        solved[panel] = total
         rounded[panel] = total.astype(BF)
+        potential[panel] = natural(total)
 
-    solved = jnp.stack(solved)
-    keep = lax.dynamic_slice_in_dim(solved, core * rows, rows, axis=2)
-    send = lax.dynamic_slice_in_dim(solved, (1 - core) * rows, rows, axis=2)
-    potential = jnp.transpose(in_order(keep, swap(send), 1), (0, 2, 1))
-
-    groups = lax.axis_size("src")
-    nodes = potential.astype(BF).reshape(panels * rows, width)
-    nodes = lax.all_to_all(
-        jnp.broadcast_to(nodes[None], (groups,) + nodes.shape),
-        "src",
-        split_axis=0,
-        concat_axis=0,
-        tiled=True,
-    )
-    nodes = jnp.transpose(nodes, (1, 0, 2)).reshape(panels * rows, groups * width)
-    frames, measures = misfit.shape
-    share = frames // groups
-    first = lax.axis_index("src") * share
-    quads = lax.dynamic_slice_in_dim(quadrupoles, first, share, axis=0).reshape(share * measures, 4)
-    weights = lax.dynamic_slice_in_dim(misfit, first, share, axis=0).reshape(1, share * measures)
-    sources = lax.broadcasted_iota(jnp.int32, (groups * width, share * measures), 0)
-
-    def difference(plus, minus):
-        hot = (sources == quads[None, :, plus]).astype(BF)
-        hot = hot - (sources == quads[None, :, minus]).astype(BF)
-        return dot(nodes, hot, 1, 0)
-
-    product = difference(0, 1) * difference(2, 3) * weights
-    mine = jnp.sum(product.reshape(panels, groups, rows // groups, share, measures), axis=4)
-    mine = jnp.transpose(mine, (1, 3, 0, 2))
-    gradient = lax.all_to_all(mine, "src", split_axis=0, concat_axis=0, tiled=True)
-    return (potential, gradient.reshape(frames, panels, rows // groups))
+    lines = panels * nodes
+    table = jnp.stack([value.astype(BF).reshape(groups, nodes, width) for value in potential], 1)
+    table = table.reshape(groups, lines, width)
+    table = lax.all_to_all(table, "src", split_axis=0, concat_axis=0, tiled=True)
+    table = jnp.transpose(table.reshape(groups // 2, 2, lines, width), (0, 2, 1, 3))
+    table = table.reshape(groups // 2, lines, 2 * width)
+    table = jnp.pad(table, ((0, 0), (0, -lines % 8), (0, 0)))
+    sums = weigh(table, jnp.transpose(quadrupoles, (0, 2, 1)), misfit)
+    gradient = jnp.sum(sums, axis=2)[:, :lines]
+    return (jnp.stack(potential), gradient.reshape(misfit.shape[0], panels, nodes))
 
 
 def solution(mesh):

time: 257 us -> 228 us (0.89)
  waiting for transfers between devices: 108 us -> 59.9 us
  starting transfers between devices: 66 us -> 89.1 us
  Pallas kernels: 0 us -> 17.2 us
  blocking collectives: 27 us -> 13.2 us
  matrix products: 16.4 us -> 10.4 us
    all_to_all x8, waiting for transfers between devices: 75.8 us -> 49.7 us  [exchange(): lax.all_to_all(blocks, 'row', split_axis=0, concat_axis=0, tiled=True, ax...]
    all_to_all x1, waiting for transfers between devices: 31.4 us -> 6.93 us  [shards(): lax.all_to_all(table, 'src', split_axis=0, concat_axis=0, tiled=True)]
    pallas_call x0 -> x1, Pallas kernels: none -> 17.2 us  [weigh(): pl.pallas_call(weigh_kernel, out_shape=jax.ShapeDtypeStruct((weights.shap...]
    all_to_all x1 -> x0, blocking collectives: 13.8 us -> none  [shards(): lax.all_to_all(mine, 'src', split_axis=0, concat_axis=0, tiled=True)]
    ppermute x4 -> x8, starting transfers between devices: 25.5 us -> 38 us  [swap(): return lax.ppermute(value, 'row', pairs)]
    all_to_all x8, starting transfers between devices: 30.8 us -> 40.6 us  [exchange(): lax.all_to_all(blocks, 'row', split_axis=0, concat_axis=0, tiled=True, ax...]
    dot_general x11 -> x9, matrix products: 16.4 us -> 10.4 us  [dot(): lax.dot_general(left, right, (((left_dim,), (right_dim,)), ((), ())), pre...]
  transfers between devices with their start and end apart: 13 -> 17, of which waited for: 10 -> 13; matrix products, arithmetic and copies ran while one was open for 9% -> 10% of each run, Pallas kernels for 0% -> 0%
where the time goes in v2:
time: 228 us; the launch traced here: 226 us
  starting transfers between devices  89.1 us (39%)
  waiting for transfers between devices  59.9 us (26%)
  local copies, waits for them, and re-layouts  20.5 us (9%)
  Pallas kernels  17.2 us (8%)
  other arithmetic  14.7 us (6%)
  blocking collectives  13.2 us (6%)
  matrix products  10.4 us (5%)
    all_to_all x8, waiting for transfers between devices, exchange(): lax.all_to_all(blocks, 'row', split_axis=0, concat_axis=0, tiled=True, ax...  49.7 us
    all_to_all x8, starting transfers between devices, exchange(): lax.all_to_all(blocks, 'row', split_axis=0, concat_axis=0, tiled=True, ax...  40.6 us
    ppermute x8, starting transfers between devices, swap(): return lax.ppermute(value, 'row', pairs)  38 us
    pallas_call x1, Pallas kernels, weigh(): pl.pallas_call(weigh_kernel, out_shape=jax.ShapeDtypeStruct((weights.shap...  17.2 us
    all_to_all x1, blocking collectives, exchange(): lax.all_to_all(blocks, 'row', split_axis=0, concat_axis=0, tiled=True, ax...  13.2 us
    all_to_all x1, starting transfers between devices, shards(): lax.all_to_all(table, 'src', split_axis=0, concat_axis=0, tiled=True)  10.4 us
    dot_general x9, matrix products, dot(): lax.dot_general(left, right, (((left_dim,), (right_dim,)), ((), ())), pre...  10.4 us
    select_n x6, other arithmetic, in_order(): jnp.where(core == 0, jnp.concatenate([mine, other], axis=axis), jnp.conca...  7.08 us
  transfers between devices with their start and end apart: 17, of which 13 were waited for; matrix products, arithmetic and copies ran while one was open for 10% of the time, Pallas kernels for 0%

profile of v2, /device:TPU:1, one launch (start us, length us, event | category | flops | bytes accessed | tf_op | source)
XLA Modules:
  0.0 226.2 jit_solution(7891173198214431974)
XLA Ops:
  2.0 8.8 %collective-permute-start = (bf16[5,64,64]{2,1,0:T(8,128)(2,1)S(1)}, bf16[5,64,64]{2,1,0:T(8,128)(2,1)S(1)}, u32[]{:S(2)}, u32[]{:S(2)}) collective-permute-start(bf16[5,64,64]{2,1,0:T(8,128)(2,1)S(1)} %bitcast.197), channel_id=1, source_target_pairs={{0,1},{1,0},{2,3},{3,2},{4,5},{5,4},{6,7},{7,6},{8,9},{9,8},{10,11... | collective-permute-start | bytes 122888 | tf_op jit(solution)/shard_map/ppermute | solution.py:69
  11.8 2.3 %collective-permute-start.1 = (bf16[10,64,2048]{2,1,0:T(8,128)(2,1)}, bf16[10,64,2048]{2,1,0:T(8,128)(2,1)}, u32[]{:S(2)}, u32[]{:S(2)}) collective-permute-start(bf16[10,64,2048]{2,1,0:T(8,128)(2,1)} %param.6), channel_id=1, source_target_pairs={{0,1},{1,0},{2,3},{3,2},{4,5},{5,4},{6,7},{7,6},{8,9},{9,8},{10,11... | collective-permute-start | bytes 7864328 | tf_op jit(solution)/shard_map/ppermute | solution.py:69
  14.1 2.1 collective-permute-start.2
  17.0 4.2 %all-to-all-start = ((bf16[16,64,128]{2,1,0:T(8,128)(2,1)}), bf16[16,64,128]{2,1,0:T(8,128)(2,1)}, u32[]{:S(2)}, u32[]{:S(2)}) async-start(bf16[16,64,128]{2,1,0:T(8,128)(2,1)} %broadcast_in_dim.13), calls=%async_computation | async-start | bytes 524288 | tf_op jit(solution)/shard_map/all_to_all | solution.py:79
  21.2 2.2 slice_bitcast_fusion.21
  24.5 2.2 slice_bitcast_fusion.6
  26.7 2.9 %slice_bitcast_fusion.9 = (bf16[64,2048]{1,0:T(8,128)(2,1)}, bf16[64,2048]{1,0:T(8,128)(2,1)}, bf16[64,2048]{1,0:T(8,128)(2,1)}, bf16[64,2048]{1,0:T(8,128)(2,1)...) fusion(bf16[10,64,2048]{2,1,0:T(8,128)(2,1)} %collective-permut, ...), kind=kLoop, calls=%fused_computation.92 | loop fusion | bytes 5242880 | tf_op jit(solution)/shard_map/squeeze | solution.py:98
  33.7 1.9 fusion.57
  37.0 8.8 %all-to-all-start.1 = ((bf16[16,64,128]{2,1,0:T(8,128)(2,1)}), bf16[16,64,128]{2,1,0:T(8,128)(2,1)S(1)}, u32[]{:S(2)}, u32[]{:S(2)}) async-start(bf16[16,64,128]{2,1,0:T(8,128)(2,1)} %broadcast_in_dim.14), calls=%async_computation.1 | async-start | bytes 524288 | tf_op jit(solution)/shard_map/all_to_all | solution.py:79
  45.7 2.7 %maximum_select_fusion.5 = (bf16[128,2048]{1,0:T(8,128)(2,1)S(1)}, bf16[128,2048]{1,0:T(8,128)(2,1)}) fusion(bf16[64,2048]{1,0:T(8,128)(2,1)} %get-tuple-element.38, bf16[64,2048]{1,0:T(8,128)(2,1)} %get-tuple-element.28, pred[]{:T(512)S(6)} %eq.4, bf16[64,2048]{1,0:T(8,128)(2,1)} %get-tuple-element.33, bf16[64,2048]{1,0:T(8,128)(2,1)} %get-tuple-element.43), kind=kLoop, calls=%fused_computation.47 | loop fusion | flops 4718592 | bytes 2097153 | tf_op jit(solution)/shard_map/jit(_where)/select_n | solution.py:72
  49.7 8.1 %all-to-all-done.1 = bf16[16,64,128]{2,1,0:T(8,128)(2,1)S(1)} async-done(((bf16[16,64,128]{2,1,0:T(8,128)(2,1)}), bf16[16,64,128]{2,1,0:T(8,128)(2,1)S(1)}, u32[]{:S(2)}, u32[]{:S(2)}) %all-to-all-start.1) | async-done | bytes 262176 | tf_op jit(solution)/shard_map/all_to_all | solution.py:79
  57.8 2.2 fusion
  61.5 4.5 %all-to-all-start.2 = ((bf16[16,64,128]{2,1,0:T(8,128)(2,1)}), bf16[16,64,128]{2,1,0:T(8,128)(2,1)S(1)}, u32[]{:S(2)}, u32[]{:S(2)}) async-start(bf16[16,64,128]{2,1,0:T(8,128)(2,1)} %broadcast_in_dim.15), calls=%async_computation.2 | async-start | bytes 524288 | tf_op jit(solution)/shard_map/all_to_all | solution.py:79
  68.0 10.4 %all-to-all-done.2 = bf16[16,64,128]{2,1,0:T(8,128)(2,1)S(1)} async-done(((bf16[16,64,128]{2,1,0:T(8,128)(2,1)}), bf16[16,64,128]{2,1,0:T(8,128)(2,1)S(1)}, u32[]{:S(2)}, u32[]{:S(2)}) %all-to-all-start.2) | async-done | bytes 262176 | tf_op jit(solution)/shard_map/all_to_all | solution.py:79
  78.4 1.8 fusion.15
  81.8 3.5 %all-to-all-start.3 = ((bf16[16,64,128]{2,1,0:T(8,128)(2,1)}), bf16[16,64,128]{2,1,0:T(8,128)(2,1)S(1)}, u32[]{:S(2)}, u32[]{:S(2)}) async-start(bf16[16,64,128]{2,1,0:T(8,128)(2,1)} %broadcast_in_dim.16), calls=%async_computation.3 | async-start | bytes 524288 | tf_op jit(solution)/shard_map/all_to_all | solution.py:79
  86.5 9.7 %all-to-all-done.3 = bf16[16,64,128]{2,1,0:T(8,128)(2,1)S(1)} async-done(((bf16[16,64,128]{2,1,0:T(8,128)(2,1)}), bf16[16,64,128]{2,1,0:T(8,128)(2,1)S(1)}, u32[]{:S(2)}, u32[]{:S(2)}) %all-to-all-start.3) | async-done | bytes 262176 | tf_op jit(solution)/shard_map/all_to_all | solution.py:79
  98.5 13.2 %all_to_all.50 = bf16[16,64,128]{2,1,0:T(8,128)(2,1)S(1)} all-to-all(bf16[16,64,128]{2,1,0:T(8,128)(2,1)S(1)} %broadcast_in_dim.17), channel_id=1, replica_groups={{0,2,4,6,8,10,12,14,16,18,20,22,24,26,28,30},{1,3,5,7,9,11,13,15,17,19,..., dimensions={0} | all-to-all | bytes 524288 | tf_op jit(solution)/shard_map/all_to_all | solution.py:79
  113.0 3.5 %all-to-all-start.5 = ((bf16[16,64,128]{2,1,0:T(8,128)(2,1)}), bf16[16,64,128]{2,1,0:T(8,128)(2,1)S(1)}, u32[]{:S(2)}, u32[]{:S(2)}) async-start(bf16[16,64,128]{2,1,0:T(8,128)(2,1)} %bitcast.191), calls=%async_computation.5 | async-start | bytes 524288 | tf_op jit(solution)/shard_map/all_to_all | solution.py:79
  116.7 10.4 %all-to-all-done.5 = bf16[16,64,128]{2,1,0:T(8,128)(2,1)S(1)} async-done(((bf16[16,64,128]{2,1,0:T(8,128)(2,1)}), bf16[16,64,128]{2,1,0:T(8,128)(2,1)S(1)}, u32[]{:S(2)}, u32[]{:S(2)}) %all-to-all-start.5) | async-done | bytes 262176 | tf_op jit(solution)/shard_map/all_to_all | solution.py:79
  128.4 3.5 %all-to-all-start.6 = ((bf16[16,64,128]{2,1,0:T(8,128)(2,1)}), bf16[16,64,128]{2,1,0:T(8,128)(2,1)S(1)}, u32[]{:S(2)}, u32[]{:S(2)}) async-start(bf16[16,64,128]{2,1,0:T(8,128)(2,1)} %bitcast.189), calls=%async_computation.6 | async-start | bytes 524288 | tf_op jit(solution)/shard_map/all_to_all | solution.py:79
  132.0 10.5 %all-to-all-done.6 = bf16[16,64,128]{2,1,0:T(8,128)(2,1)S(1)} async-done(((bf16[16,64,128]{2,1,0:T(8,128)(2,1)}), bf16[16,64,128]{2,1,0:T(8,128)(2,1)S(1)}, u32[]{:S(2)}, u32[]{:S(2)}) %all-to-all-start.6) | async-done | bytes 262176 | tf_op jit(solution)/shard_map/all_to_all | solution.py:79
  143.9 3.5 %all-to-all-start.7 = ((bf16[16,64,128]{2,1,0:T(8,128)(2,1)}), bf16[16,64,128]{2,1,0:T(8,128)(2,1)S(1)}, u32[]{:S(2)}, u32[]{:S(2)}) async-start(bf16[16,64,128]{2,1,0:T(8,128)(2,1)} %bitcast.187), calls=%async_computation.7 | async-start | bytes 524288 | tf_op jit(solution)/shard_map/all_to_all | solution.py:79
  147.5 9.3 %collective-permute-start.7 = (f32[64,64]{0,1:T(8,128)S(1)}, f32[64,64]{0,1:T(8,128)S(1)}, u32[]{:S(2)}, u32[]{:S(2)}) collective-permute-start(f32[64,64]{0,1:T(8,128)S(1)} %get-tuple-element.65), channel_id=1, source_target_pairs={{0,1},{1,0},{2,3},{3,2},{4,5},{5,4},{6,7},{7,6},{8,9},{9,8},{10,11... | collective-permute-start | bytes 49160 | tf_op jit(solution)/shard_map/ppermute | solution.py:69
  160.5 9.1 %all-to-all-start.8 = ((bf16[16,64,128]{2,1,0:T(8,128)(2,1)}), bf16[16,64,128]{2,1,0:T(8,128)(2,1)S(1)}, u32[]{:S(2)}, u32[]{:S(2)}) async-start(bf16[16,64,128]{2,1,0:T(8,128)(2,1)} %bitcast.185), calls=%async_computation.8 | async-start | bytes 524288 | tf_op jit(solution)/shard_map/all_to_all | solution.py:79
  169.6 5.3 %collective-permute-start.6 = (f32[64,64]{0,1:T(8,128)S(1)}, f32[64,64]{0,1:T(8,128)S(1)}, u32[]{:S(2)}, u32[]{:S(2)}) collective-permute-start(f32[64,64]{0,1:T(8,128)S(1)} %get-tuple-element.67), channel_id=1, source_target_pairs={{0,1},{1,0},{2,3},{3,2},{4,5},{5,4},{6,7},{7,6},{8,9},{9,8},{10,11... | collective-permute-start | bytes 49160 | tf_op jit(solution)/shard_map/ppermute | solution.py:69
  175.0 1.9 collective-permute-start.5
  178.2 2.1 collective-permute-start.4
  180.7 6.3 %collective-permute-start.3 = (f32[64,64]{0,1:T(8,128)S(1)}, f32[64,64]{0,1:T(8,128)S(1)}, u32[]{:S(2)}, u32[]{:S(2)}) collective-permute-start(f32[64,64]{0,1:T(8,128)S(1)} %get-tuple-element.73), channel_id=1, source_target_pairs={{0,1},{1,0},{2,3},{3,2},{4,5},{5,4},{6,7},{7,6},{8,9},{9,8},{10,11... | collective-permute-start | bytes 49160 | tf_op jit(solution)/shard_map/ppermute | solution.py:69
  188.7 10.4 %all-to-all-start.9 = ((bf16[16,20,128]{2,1,0:T(8,128)(2,1)}), bf16[16,20,128]{2,1,0:T(8,128)(2,1)S(1)}, u32[]{:S(2)}, u32[]{:S(2)}) async-start(bf16[16,20,128]{2,1,0:T(8,128)(2,1)} %copy.88), calls=%async_computation.9 | async-start | bytes 196608 | tf_op jit(solution)/shard_map/all_to_all | solution.py:136
  199.6 6.9 %all-to-all-done.9 = bf16[16,20,128]{2,1,0:T(8,128)(2,1)S(1)} async-done(((bf16[16,20,128]{2,1,0:T(8,128)(2,1)}), bf16[16,20,128]{2,1,0:T(8,128)(2,1)S(1)}, u32[]{:S(2)}, u32[]{:S(2)}) %all-to-all-start.9) | async-done | bytes 81952 | tf_op jit(solution)/shard_map/all_to_all | solution.py:136
  207.3 17.2 %shard_map.68 = f32[16,24,128]{2,1,0:T(8,128)} custom-call(bf16[8,24,256]{2,1,0:T(8,128)(2,1)} %pad.4.table_ref, s32[16,4,1024]{2,1,0:T(4,128)} %bitcast.196, f32[16,1024]{1,0:T(8,128)} %weights_ref.1), custom_call_target="tpu_custom_call" | custom-call | tf_op jit(solution)/shard_map/pallas_call | solution.py:53
  (138 shorter events, 33.5 us)
Async XLA Ops:
  0.6 22.7 %copy-start = (bf16[10,64,2048]{2,1,0:T(8,128)(2,1)S(1)}, bf16[10,64,2048]{2,1,0:T(8,128)(2,1)}, u32[]{:S(2)}) copy-start(bf16[10,64,2048]{2,1,0:T(8,128)(2,1)} %param.6) | copy-start | bytes 7864324
  2.0 9.7 %collective-permute-start = (bf16[5,64,64]{2,1,0:T(8,128)(2,1)S(1)}, bf16[5,64,64]{2,1,0:T(8,128)(2,1)S(1)}, u32[]{:S(2)}, u32[]{:S(2)}) collective-permute-start(bf16[5,64,64]{2,1,0:T(8,128)(2,1)S(1)} %bitcast.197), channel_id=1, source_target_pairs={{0,1},{1,0},{2,3},{3,2},{4,5},{5,4},{6,7},{7,6},{8,9},{9,8},{10,11... | collective-permute-start | bytes 122888 | tf_op jit(solution)/shard_map/ppermute | solution.py:69
  11.8 14.9 %collective-permute-start.1 = (bf16[10,64,2048]{2,1,0:T(8,128)(2,1)}, bf16[10,64,2048]{2,1,0:T(8,128)(2,1)}, u32[]{:S(2)}, u32[]{:S(2)}) collective-permute-start(bf16[10,64,2048]{2,1,0:T(8,128)(2,1)} %param.6), channel_id=1, source_target_pairs={{0,1},{1,0},{2,3},{3,2},{4,5},{5,4},{6,7},{7,6},{8,9},{9,8},{10,11... | collective-permute-start | bytes 7864328 | tf_op jit(solution)/shard_map/ppermute | solution.py:69
  14.1 10.4 %collective-permute-start.2 = (bf16[5,64,2048]{2,1,0:T(8,128)(2,1)}, bf16[5,64,2048]{2,1,0:T(8,128)(2,1)}, u32[]{:S(2)}, u32[]{:S(2)}) collective-permute-start(bf16[5,64,2048]{2,1,0:T(8,128)(2,1)} %param.7), channel_id=1, source_target_pairs={{0,1},{1,0},{2,3},{3,2},{4,5},{5,4},{6,7},{7,6},{8,9},{9,8},{10,11... | collective-permute-start | bytes 3932168 | tf_op jit(solution)/shard_map/ppermute | solution.py:69
  17.0 16.7 %all-to-all-start = ((bf16[16,64,128]{2,1,0:T(8,128)(2,1)}), bf16[16,64,128]{2,1,0:T(8,128)(2,1)}, u32[]{:S(2)}, u32[]{:S(2)}) async-start(bf16[16,64,128]{2,1,0:T(8,128)(2,1)} %broadcast_in_dim.13), calls=%async_computation | async-start | bytes 524288 | tf_op jit(solution)/shard_map/all_to_all | solution.py:79
  36.2 12.3 %copy-start.4 = (bf16[64,2048]{1,0:T(8,128)(2,1)S(1)}, bf16[64,2048]{1,0:T(8,128)(2,1)}, u32[]{:S(2)}) copy-start(bf16[64,2048]{1,0:T(8,128)(2,1)} %get-tuple-element.48) | copy-start | bytes 786436
  36.2 12.3 %copy-start.7 = (bf16[64,2048]{1,0:T(8,128)(2,1)S(1)}, bf16[64,2048]{1,0:T(8,128)(2,1)}, u32[]{:S(2)}) copy-start(bf16[64,2048]{1,0:T(8,128)(2,1)} %get-tuple-element.32) | copy-start | bytes 786436
  36.2 12.3 %copy-start.8 = (bf16[64,2048]{1,0:T(8,128)(2,1)S(1)}, bf16[64,2048]{1,0:T(8,128)(2,1)}, u32[]{:S(2)}) copy-start(bf16[64,2048]{1,0:T(8,128)(2,1)} %get-tuple-element.53) | copy-start | bytes 786436
  36.2 12.3 %copy-start.9 = (bf16[64,2048]{1,0:T(8,128)(2,1)S(1)}, bf16[64,2048]{1,0:T(8,128)(2,1)}, u32[]{:S(2)}) copy-start(bf16[64,2048]{1,0:T(8,128)(2,1)} %get-tuple-element.42) | copy-start | bytes 786436
  37.0 20.8 %all-to-all-start.1 = ((bf16[16,64,128]{2,1,0:T(8,128)(2,1)}), bf16[16,64,128]{2,1,0:T(8,128)(2,1)S(1)}, u32[]{:S(2)}, u32[]{:S(2)}) async-start(bf16[16,64,128]{2,1,0:T(8,128)(2,1)} %broadcast_in_dim.14), calls=%async_computation.1 | async-start | bytes 524288 | tf_op jit(solution)/shard_map/all_to_all | solution.py:79
  57.8 9.1 %copy-start.2 = (bf16[64,2048]{1,0:T(8,128)(2,1)S(1)}, bf16[64,2048]{1,0:T(8,128)(2,1)}, u32[]{:S(2)}) copy-start(bf16[64,2048]{1,0:T(8,128)(2,1)} %get-tuple-element.30) | copy-start | bytes 786436
  61.5 16.9 %all-to-all-start.2 = ((bf16[16,64,128]{2,1,0:T(8,128)(2,1)}), bf16[16,64,128]{2,1,0:T(8,128)(2,1)S(1)}, u32[]{:S(2)}, u32[]{:S(2)}) async-start(bf16[16,64,128]{2,1,0:T(8,128)(2,1)} %broadcast_in_dim.15), calls=%async_computation.2 | async-start | bytes 524288 | tf_op jit(solution)/shard_map/all_to_all | solution.py:79
  80.2 15.9 %copy-start.22 = (f32[64,384]{1,0:T(8,128)}, f32[64,384]{1,0:T(8,128)S(1)}, u32[]{:S(2)}) copy-start(f32[64,384]{1,0:T(8,128)S(1)} %fusion.15) | copy-start | bytes 294916
  81.8 14.3 %all-to-all-start.3 = ((bf16[16,64,128]{2,1,0:T(8,128)(2,1)}), bf16[16,64,128]{2,1,0:T(8,128)(2,1)S(1)}, u32[]{:S(2)}, u32[]{:S(2)}) async-start(bf16[16,64,128]{2,1,0:T(8,128)(2,1)} %broadcast_in_dim.16), calls=%async_computation.3 | async-start | bytes 524288 | tf_op jit(solution)/shard_map/all_to_all | solution.py:79
  85.4 26.3 %copy-start.19 = (bf16[64,2048]{1,0:T(8,128)(2,1)S(1)}, bf16[64,2048]{1,0:T(8,128)(2,1)}, u32[]{:S(2)}) copy-start(bf16[64,2048]{1,0:T(8,128)(2,1)} %get-tuple-element.49) | copy-start | bytes 786436
  86.5 25.2 %copy-start.20 = (bf16[64,2048]{1,0:T(8,128)(2,1)S(1)}, bf16[64,2048]{1,0:T(8,128)(2,1)}, u32[]{:S(2)}) copy-start(bf16[64,2048]{1,0:T(8,128)(2,1)} %get-tuple-element.54) | copy-start | bytes 786436
  111.7 15.6 %copy-start.16 = (bf16[128,2048]{1,0:T(8,128)(2,1)S(1)}, bf16[128,2048]{1,0:T(8,128)(2,1)}, u32[]{:S(2)}) copy-start(bf16[128,2048]{1,0:T(8,128)(2,1)} %get-tuple-element.82) | copy-start | bytes 1572868
  112.2 30.4 %copy-start.14 = (bf16[128,2048]{1,0:T(8,128)(2,1)S(1)}, bf16[128,2048]{1,0:T(8,128)(2,1)}, u32[]{:S(2)}) copy-start(bf16[128,2048]{1,0:T(8,128)(2,1)} %get-tuple-element.78) | copy-start | bytes 1572868
  112.2 30.4 %copy-start.15 = (bf16[128,2048]{1,0:T(8,128)(2,1)S(1)}, bf16[128,2048]{1,0:T(8,128)(2,1)}, u32[]{:S(2)}) copy-start(bf16[128,2048]{1,0:T(8,128)(2,1)} %get-tuple-element.79) | copy-start | bytes 1572868
  113.0 14.1 %all-to-all-start.5 = ((bf16[16,64,128]{2,1,0:T(8,128)(2,1)}), bf16[16,64,128]{2,1,0:T(8,128)(2,1)S(1)}, u32[]{:S(2)}, u32[]{:S(2)}) async-start(bf16[16,64,128]{2,1,0:T(8,128)(2,1)} %bitcast.191), calls=%async_computation.5 | async-start | bytes 524288 | tf_op jit(solution)/shard_map/all_to_all | solution.py:79
  128.4 14.1 %all-to-all-start.6 = ((bf16[16,64,128]{2,1,0:T(8,128)(2,1)}), bf16[16,64,128]{2,1,0:T(8,128)(2,1)S(1)}, u32[]{:S(2)}, u32[]{:S(2)}) async-start(bf16[16,64,128]{2,1,0:T(8,128)(2,1)} %bitcast.189), calls=%async_computation.6 | async-start | bytes 524288 | tf_op jit(solution)/shard_map/all_to_all | solution.py:79
  142.7 15.4 %copy-start.17 = (bf16[128,2048]{1,0:T(8,128)(2,1)S(1)}, bf16[128,2048]{1,0:T(8,128)(2,1)}, u32[]{:S(2)}) copy-start(bf16[128,2048]{1,0:T(8,128)(2,1)} %get-tuple-element.27) | copy-start | bytes 1572868
  142.7 15.4 %copy-start.18 = (bf16[128,2048]{1,0:T(8,128)(2,1)S(1)}, bf16[128,2048]{1,0:T(8,128)(2,1)}, u32[]{:S(2)}) copy-start(bf16[128,2048]{1,0:T(8,128)(2,1)} %get-tuple-element.25) | copy-start | bytes 1572868
  143.9 14.0 %all-to-all-start.7 = ((bf16[16,64,128]{2,1,0:T(8,128)(2,1)}), bf16[16,64,128]{2,1,0:T(8,128)(2,1)S(1)}, u32[]{:S(2)}, u32[]{:S(2)}) async-start(bf16[16,64,128]{2,1,0:T(8,128)(2,1)} %bitcast.187), calls=%async_computation.7 | async-start | bytes 524288 | tf_op jit(solution)/shard_map/all_to_all | solution.py:79
  147.5 10.1 %collective-permute-start.7 = (f32[64,64]{0,1:T(8,128)S(1)}, f32[64,64]{0,1:T(8,128)S(1)}, u32[]{:S(2)}, u32[]{:S(2)}) collective-permute-start(f32[64,64]{0,1:T(8,128)S(1)} %get-tuple-element.65), channel_id=1, source_target_pairs={{0,1},{1,0},{2,3},{3,2},{4,5},{5,4},{6,7},{7,6},{8,9},{9,8},{10,11... | collective-permute-start | bytes 49160 | tf_op jit(solution)/shard_map/ppermute | solution.py:69
  160.5 20.0 %all-to-all-start.8 = ((bf16[16,64,128]{2,1,0:T(8,128)(2,1)}), bf16[16,64,128]{2,1,0:T(8,128)(2,1)S(1)}, u32[]{:S(2)}, u32[]{:S(2)}) async-start(bf16[16,64,128]{2,1,0:T(8,128)(2,1)} %bitcast.185), calls=%async_computation.8 | async-start | bytes 524288 | tf_op jit(solution)/shard_map/all_to_all | solution.py:79
  169.6 7.3 %collective-permute-start.6 = (f32[64,64]{0,1:T(8,128)S(1)}, f32[64,64]{0,1:T(8,128)S(1)}, u32[]{:S(2)}, u32[]{:S(2)}) collective-permute-start(f32[64,64]{0,1:T(8,128)S(1)} %get-tuple-element.67), channel_id=1, source_target_pairs={{0,1},{1,0},{2,3},{3,2},{4,5},{5,4},{6,7},{7,6},{8,9},{9,8},{10,11... | collective-permute-start | bytes 49160 | tf_op jit(solution)/shard_map/ppermute | solution.py:69
  175.0 3.1 %collective-permute-start.5 = (f32[64,64]{0,1:T(8,128)S(1)}, f32[64,64]{0,1:T(8,128)S(1)}, u32[]{:S(2)}, u32[]{:S(2)}) collective-permute-start(f32[64,64]{0,1:T(8,128)S(1)} %get-tuple-element.69), channel_id=1, source_target_pairs={{0,1},{1,0},{2,3},{3,2},{4,5},{5,4},{6,7},{7,6},{8,9},{9,8},{10,11... | collective-permute-start | bytes 49160 | tf_op jit(solution)/shard_map/ppermute | solution.py:69
  178.2 8.8 %collective-permute-start.4 = (f32[64,64]{0,1:T(8,128)S(1)}, f32[64,64]{0,1:T(8,128)S(1)}, u32[]{:S(2)}, u32[]{:S(2)}) collective-permute-start(f32[64,64]{0,1:T(8,128)S(1)} %get-tuple-element.71), channel_id=1, source_target_pairs={{0,1},{1,0},{2,3},{3,2},{4,5},{5,4},{6,7},{7,6},{8,9},{9,8},{10,11... | collective-permute-start | bytes 49160 | tf_op jit(solution)/shard_map/ppermute | solution.py:69
  180.7 7.1 %collective-permute-start.3 = (f32[64,64]{0,1:T(8,128)S(1)}, f32[64,64]{0,1:T(8,128)S(1)}, u32[]{:S(2)}, u32[]{:S(2)}) collective-permute-start(f32[64,64]{0,1:T(8,128)S(1)} %get-tuple-element.73), channel_id=1, source_target_pairs={{0,1},{1,0},{2,3},{3,2},{4,5},{5,4},{6,7},{7,6},{8,9},{9,8},{10,11... | collective-permute-start | bytes 49160 | tf_op jit(solution)/shard_map/ppermute | solution.py:69
  188.7 17.8 %all-to-all-start.9 = ((bf16[16,20,128]{2,1,0:T(8,128)(2,1)}), bf16[16,20,128]{2,1,0:T(8,128)(2,1)S(1)}, u32[]{:S(2)}, u32[]{:S(2)}) async-start(bf16[16,20,128]{2,1,0:T(8,128)(2,1)} %copy.88), calls=%async_computation.9 | async-start | bytes 196608 | tf_op jit(solution)/shard_map/all_to_all | solution.py:136
  199.6 26.6 %copy-start.23 = (f32[5,64,128]{2,1,0:T(8,128)}, f32[5,64,128]{2,1,0:T(8,128)S(1)}, u32[]{:S(2)}) copy-start(f32[5,64,128]{2,1,0:T(8,128)S(1)} %constant_dynamic-update-slice_fusion.4) | copy-start | bytes 491524
  (9 other events, 55.0 us)

commit v3 on v2

v3 whole, which is shorter than its diff:
```python
import jax
import jax.numpy as jnp
from jax import lax
from jax.experimental import pallas as pl
from jax.sharding import PartitionSpec as P

BF = jnp.bfloat16
F32 = jnp.float32


def pair_index(later, earlier):
    return later * (later - 1) // 2 + earlier


def dot(left, right, left_dim, right_dim):
    return lax.dot_general(
        left, right, (((left_dim,), (right_dim,)), ((), ())), preferred_element_type=F32
    )


def weigh_kernel(table_ref, picks_ref, weights_ref, out_ref):
    groups, count, width = table_ref.shape
    panels, nodes, frames = out_ref.shape
    measures = picks_ref.shape[2]
    depth, parts = 2 * width, groups // 2
    lines = count + -count % 8
    table = []
    for part in range(parts):
        pair = [table_ref[2 * part].astype(F32), table_ref[2 * part + 1].astype(F32)]
        table.append(jnp.concatenate(pair, axis=1))
        table.append(jnp.zeros((lines - count, depth), F32))
    table = jnp.concatenate(table, axis=0).astype(BF)
    span = min(256, measures)
    places = lax.broadcasted_iota(jnp.int32, (depth, span), 0).astype(jnp.int16)
    lane = lax.broadcasted_iota(jnp.int32, (lines, 128), 1)

    def frame(at, result):
        total = jnp.zeros((lines, span), F32)
        for start in range(0, measures, span):
            values = []
            for which in range(4):
                index = picks_ref[at, which : which + 1, start : start + span]
                low = (index & (depth - 1)).astype(jnp.int16)
                hot = jnp.where(places == low, jnp.ones((), BF), jnp.zeros((), BF))
                found = dot(table, hot, 1, 0)
                part = index // depth
                value = found[:lines]
                for other in range(1, parts):
                    piece = found[other * lines : (other + 1) * lines]
                    value = jnp.where(part == other, piece, value)
                values.append(value)
            product = (values[0] - values[1]) * (values[2] - values[3])
            total = total + product * weights_ref[pl.ds(at, 1), start : start + span]
        return jnp.where(lane == at, jnp.sum(total, axis=1, keepdims=True), result)

    result = lax.fori_loop(0, frames, frame, jnp.zeros((lines, 128), F32), unroll=2)
    for panel in range(panels):
        out_ref[panel] = result[panel * nodes : (panel + 1) * nodes, :frames]


def weigh(table, picks, weights, panels):
    return pl.pallas_call(
        weigh_kernel,
        out_shape=jax.ShapeDtypeStruct(
            (panels, table.shape[1] // panels, weights.shape[0]), F32
        ),
    )(table, picks, weights)


def shards(rhs_panels, coupling, block_inverse, quadrupoles, misfit):
    panels, rows, width = rhs_panels.shape
    size = coupling.shape[2]
    chips = lax.axis_size("row") // 2
    half = width // 2
    core = lax.axis_index("row") % 2
    pairs = [(2 * p + c, 2 * p + 1 - c) for p in range(chips) for c in range(2)]
    same_core = [[2 * p + c for p in range(chips)] for c in range(2)]

    def swap(value):
        return lax.ppermute(value, "row", pairs)

    def in_order(mine, other, axis):
        return jnp.where(
            core == 0,
            jnp.concatenate([mine, other], axis=axis),
            jnp.concatenate([other, mine], axis=axis),
        )

    def exchange(blocks):
        return lax.all_to_all(
            blocks, "row", split_axis=0, concat_axis=0, tiled=True, axis_index_groups=same_core
        )

    def gather(value):
        got = exchange(jnp.broadcast_to(value[None], (chips,) + value.shape))
        return jnp.transpose(got, (1, 0, 2)).reshape(value.shape[0], size)

    def pieces_of(part):
        return jnp.transpose(part.astype(BF).reshape(half, chips, tall), (1, 0, 2))

    tall = 2 * rows
    groups = lax.axis_size("src")
    nodes = rows // groups

    flipped = jnp.transpose(rhs_panels, (0, 2, 1))
    keep = lax.dynamic_slice_in_dim(flipped, core * half, half, axis=1)
    send = lax.dynamic_slice_in_dim(flipped, (1 - core) * half, half, axis=1)
    rhs = in_order(keep, swap(send), 2)
    other_coupling = swap(coupling)
    other_inverse = swap(block_inverse)

    def factor(later, earlier):
        at = pair_index(later, earlier)
        return in_order(coupling[at], other_coupling[at], 0)

    factors = {
        (later, earlier): factor(later, earlier)
        for later in range(1, panels)
        for earlier in range(later)
    }
    inverses = [in_order(block_inverse[k], other_inverse[k], 0) for k in range(panels)]

    full = []
    for panel in range(panels):
        total = rhs[panel].astype(F32)
        for earlier in range(panel):
            total = total - dot(full[earlier], factors[panel, earlier], 1, 1)
        full.append(gather(total.astype(BF)))
    totals = [lax.optimization_barrier(dot(full[k], inverses[k], 1, 1)) for k in range(panels)]

    rounded = [None] * panels
    solved = [None] * panels
    for panel in reversed(range(panels)):
        total = totals[panel]
        if panel < panels - 1:
            part = dot(rounded[panels - 1], factors[panels - 1, panel], 1, 0)
            for later in reversed(range(panel + 1, panels - 1)):
                part = part + dot(rounded[later], factors[later, panel], 1, 0)
            total = total - jnp.sum(exchange(pieces_of(part)).astype(F32), axis=0)
        rounded[panel] = total.astype(BF)
        solved[panel] = total

    solved = jnp.stack(solved)
    keep = lax.dynamic_slice_in_dim(solved, core * rows, rows, axis=2)
    send = lax.dynamic_slice_in_dim(solved, (1 - core) * rows, rows, axis=2)
    potential = jnp.transpose(in_order(keep, swap(send), 1), (0, 2, 1))

    table = jnp.transpose(potential.astype(BF).reshape(panels, groups, nodes, width), (1, 0, 2, 3))
    table = table.reshape(groups, panels * nodes, width)
    table = lax.all_to_all(table, "src", split_axis=0, concat_axis=0, tiled=True)
    sums = weigh(table, jnp.transpose(quadrupoles, (0, 2, 1)), misfit, panels)
    gradient = jnp.transpose(sums, (2, 0, 1))
    return (potential, gradient)


def solution(mesh):
    return jax.shard_map(
        shards,
        mesh=mesh,
        in_specs=(P(None, "row", "src"), P(None, "row", None), P(None, "row", None), P(), P()),
        out_specs=(P(None, "row", "src"), P(None, None, ("row", "src"))),
        check_vma=False,
    )
```

time: 228 us -> 215 us (0.943)
  starting transfers between devices: 89.1 us -> 61.7 us
  matrix products: 10.4 us -> 29.1 us
  waiting for transfers between devices: 59.9 us -> 74.6 us
  other arithmetic: 14.7 us -> 2.14 us
  Pallas kernels: 17.2 us -> 10.3 us
  blocking collectives: 13.2 us -> 17.9 us
  local copies, waits for them, and re-layouts: 20.5 us -> 16.4 us
    all_to_all x8 -> x9, waiting for transfers between devices: 49.7 us -> 73.6 us  [exchange(): lax.all_to_all(blocks, 'row', split_axis=0, concat_axis=0, tiled=True, ax...]
    dot_general x9 -> x25, matrix products: 10.4 us -> 29.1 us  [dot(): lax.dot_general(left, right, (((left_dim,), (right_dim,)), ((), ())), pre...]
    ppermute x8 -> x4, starting transfers between devices: 38 us -> 26.7 us  [swap(): return lax.ppermute(value, 'row', pairs)]
    all_to_all x1 -> x0, starting transfers between devices: 10.4 us -> none  [shards(): lax.all_to_all(table, 'src', split_axis=0, concat_axis=0, tiled=True)]
    all_to_all x1 -> x0, waiting for transfers between devices: 6.93 us -> none  [shards(): lax.all_to_all(table, 'src', split_axis=0, concat_axis=0, tiled=True)]
    pallas_call x1, Pallas kernels: 17.2 us -> 10.3 us  [weigh(): pl.pallas_call(weigh_kernel, out_shape=jax.ShapeDtypeStruct((panels, tabl...]
    select_n x6 -> x1, other arithmetic: 7.08 us -> 1.08 us  [in_order(): jnp.where(core == 0, jnp.concatenate([mine, other], axis=axis), jnp.conca...]
    all_to_all x8 -> x9, starting transfers between devices: 40.6 us -> 35.1 us  [exchange(): lax.all_to_all(blocks, 'row', split_axis=0, concat_axis=0, tiled=True, ax...]
  transfers between devices with their start and end apart: 17 -> 13, of which waited for: 13 -> 10; matrix products, arithmetic and copies ran while one was open for 10% -> 17% of each run, Pallas kernels for 0% -> 0%
where the time goes in v3:
time: 215 us; the launch traced here: 214 us
  waiting for transfers between devices  74.6 us (35%)
  starting transfers between devices  61.7 us (29%)
  matrix products  29.1 us (14%)
  blocking collectives  17.9 us (8%)
  local copies, waits for them, and re-layouts  16.4 us (8%)
  Pallas kernels  10.3 us (5%)
    all_to_all x9, waiting for transfers between devices, exchange(): lax.all_to_all(blocks, 'row', split_axis=0, concat_axis=0, tiled=True, ax...  73.6 us
    all_to_all x9, starting transfers between devices, exchange(): lax.all_to_all(blocks, 'row', split_axis=0, concat_axis=0, tiled=True, ax...  35.1 us
    dot_general x25, matrix products, dot(): lax.dot_general(left, right, (((left_dim,), (right_dim,)), ((), ())), pre...  29.1 us
    ppermute x4, starting transfers between devices, swap(): return lax.ppermute(value, 'row', pairs)  26.7 us
    all_to_all x1, blocking collectives, shards(): lax.all_to_all(table, 'src', split_axis=0, concat_axis=0, tiled=True)  17.9 us
    pallas_call x1, Pallas kernels, weigh(): pl.pallas_call(weigh_kernel, out_shape=jax.ShapeDtypeStruct((panels, tabl...  10.3 us
    squeeze x2, local copies, waits for them, and re-layouts, factor(): return in_order(coupling[at], other_coupling[at], 0)  4.39 us
  transfers between devices with their start and end apart: 13, of which 10 were waited for; matrix products, arithmetic and copies ran while one was open for 17% of the time, Pallas kernels for 0%

profile of v3, /device:TPU:1, one launch (start us, length us, event | category | flops | bytes accessed | tf_op | source)
XLA Modules:
  0.0 213.7 jit_solution(5641205311748827173)
XLA Ops:
  0.6 8.8 %collective-permute-start.2 = (bf16[10,64,2048]{2,1,0:T(8,128)(2,1)}, bf16[10,64,2048]{2,1,0:T(8,128)(2,1)S(1)}, u32[]{:S(2)}, u32[]{:S(2)}) collective-permute-start(bf16[10,64,2048]{2,1,0:T(8,128)(2,1)} %param.6), channel_id=1, source_target_pairs={{0,1},{1,0},{2,3},{3,2},{4,5},{5,4},{6,7},{7,6},{8,9},{9,8},{10,11... | collective-permute-start | bytes 7864328 | tf_op jit(solution)/shard_map/ppermute | solution.py:80
  10.7 1.9 collective-permute-start
  12.6 3.0 %slice_bitcast_fusion.19 = (bf16[64,2048]{1,0:T(8,128)(2,1)}, bf16[64,2048]{1,0:T(8,128)(2,1)}, bf16[64,2048]{1,0:T(8,128)(2,1)}, bf16[64,2048]{1,0:T(8,128)(2,1...) fusion(bf16[10,64,2048]{2,1,0:T(8,128)(2,1)} %param.6), kind=kLoop, calls=%fused_computation.121 | loop fusion | bytes 5242880 | tf_op jit(solution)/shard_map/squeeze | solution.py:114
  18.2 4.2 %all-to-all-start = ((bf16[16,64,128]{2,1,0:T(8,128)(2,1)}), bf16[16,64,128]{2,1,0:T(8,128)(2,1)}, u32[]{:S(2)}, u32[]{:S(2)}) async-start(bf16[16,64,128]{2,1,0:T(8,128)(2,1)} %broadcast_in_dim.13), calls=%async_computation | async-start | bytes 524288 | tf_op jit(solution)/shard_map/all_to_all | solution.py:90
  22.4 1.4 slice_bitcast_fusion.4
  23.8 11.2 %all-to-all-done = bf16[16,64,128]{2,1,0:T(8,128)(2,1)} async-done(((bf16[16,64,128]{2,1,0:T(8,128)(2,1)}), bf16[16,64,128]{2,1,0:T(8,128)(2,1)}, u32[]{:S(2)}, u32[]{:S(2)}) %all-to-all-start) | async-done | bytes 262176 | tf_op jit(solution)/shard_map/all_to_all | solution.py:90
  37.1 4.2 %all-to-all-start.1 = ((bf16[16,64,128]{2,1,0:T(8,128)(2,1)}), bf16[16,64,128]{2,1,0:T(8,128)(2,1)}, u32[]{:S(2)}, u32[]{:S(2)}) async-start(bf16[16,64,128]{2,1,0:T(8,128)(2,1)} %broadcast_in_dim.14), calls=%async_computation.1 | async-start | bytes 524288 | tf_op jit(solution)/shard_map/all_to_all | solution.py:90
  41.3 3.5 %collective-permute-start.1 = (bf16[5,64,2048]{2,1,0:T(8,128)(2,1)S(1)}, bf16[5,64,2048]{2,1,0:T(8,128)(2,1)S(1)}, u32[]{:S(2)}, u32[]{:S(2)}) collective-permute-start(bf16[5,64,2048]{2,1,0:T(8,128)(2,1)S(1)} %copy-done), channel_id=1, source_target_pairs={{0,1},{1,0},{2,3},{3,2},{4,5},{5,4},{6,7},{7,6},{8,9},{9,8},{10,11... | collective-permute-start | bytes 3932168 | tf_op jit(solution)/shard_map/ppermute | solution.py:80
  46.0 7.3 %all-to-all-done.1 = bf16[16,64,128]{2,1,0:T(8,128)(2,1)} async-done(((bf16[16,64,128]{2,1,0:T(8,128)(2,1)}), bf16[16,64,128]{2,1,0:T(8,128)(2,1)}, u32[]{:S(2)}, u32[]{:S(2)}) %all-to-all-start.1) | async-done | bytes 262176 | tf_op jit(solution)/shard_map/all_to_all | solution.py:90
  53.3 1.6 fusion.8
  55.7 4.2 %all-to-all-start.2 = ((bf16[16,64,128]{2,1,0:T(8,128)(2,1)}), bf16[16,64,128]{2,1,0:T(8,128)(2,1)}, u32[]{:S(2)}, u32[]{:S(2)}) async-start(bf16[16,64,128]{2,1,0:T(8,128)(2,1)} %broadcast_in_dim.15), calls=%async_computation.2 | async-start | bytes 524288 | tf_op jit(solution)/shard_map/all_to_all | solution.py:90
  63.6 7.1 %all-to-all-done.2 = bf16[16,64,128]{2,1,0:T(8,128)(2,1)} async-done(((bf16[16,64,128]{2,1,0:T(8,128)(2,1)}), bf16[16,64,128]{2,1,0:T(8,128)(2,1)}, u32[]{:S(2)}, u32[]{:S(2)}) %all-to-all-start.2) | async-done | bytes 262176 | tf_op jit(solution)/shard_map/all_to_all | solution.py:90
  70.7 1.6 fusion.9
  73.0 4.2 %all-to-all-start.3 = ((bf16[16,64,128]{2,1,0:T(8,128)(2,1)}), bf16[16,64,128]{2,1,0:T(8,128)(2,1)}, u32[]{:S(2)}, u32[]{:S(2)}) async-start(bf16[16,64,128]{2,1,0:T(8,128)(2,1)} %broadcast_in_dim.16), calls=%async_computation.3 | async-start | bytes 524288 | tf_op jit(solution)/shard_map/all_to_all | solution.py:90
  77.3 1.6 convolution_subtract_fusion.9
  78.9 1.6 convolution_subtract_fusion.7
  81.8 6.2 %all-to-all-done.3 = bf16[16,64,128]{2,1,0:T(8,128)(2,1)} async-done(((bf16[16,64,128]{2,1,0:T(8,128)(2,1)}), bf16[16,64,128]{2,1,0:T(8,128)(2,1)}, u32[]{:S(2)}, u32[]{:S(2)}) %all-to-all-start.3) | async-done | bytes 262176 | tf_op jit(solution)/shard_map/all_to_all | solution.py:90
  87.9 1.6 fusion.10
  90.3 4.2 %all-to-all-start.4 = ((bf16[16,64,128]{2,1,0:T(8,128)(2,1)}), bf16[16,64,128]{2,1,0:T(8,128)(2,1)}, u32[]{:S(2)}, u32[]{:S(2)}) async-start(bf16[16,64,128]{2,1,0:T(8,128)(2,1)} %broadcast_in_dim.17), calls=%async_computation.4 | async-start | bytes 524288 | tf_op jit(solution)/shard_map/all_to_all | solution.py:90
  96.9 8.1 %all-to-all-done.4 = bf16[16,64,128]{2,1,0:T(8,128)(2,1)} async-done(((bf16[16,64,128]{2,1,0:T(8,128)(2,1)}), bf16[16,64,128]{2,1,0:T(8,128)(2,1)}, u32[]{:S(2)}, u32[]{:S(2)}) %all-to-all-start.4) | async-done | bytes 262176 | tf_op jit(solution)/shard_map/all_to_all | solution.py:90
  107.4 3.5 %all-to-all-start.5 = ((bf16[16,64,128]{2,1,0:T(8,128)(2,1)}), bf16[16,64,128]{2,1,0:T(8,128)(2,1)S(1)}, u32[]{:S(2)}, u32[]{:S(2)}) async-start(bf16[16,64,128]{2,1,0:T(8,128)(2,1)} %bitcast.233), calls=%async_computation.5 | async-start | bytes 524288 | tf_op jit(solution)/shard_map/all_to_all | solution.py:90
  114.9 6.5 %all-to-all-done.5 = bf16[16,64,128]{2,1,0:T(8,128)(2,1)S(1)} async-done(((bf16[16,64,128]{2,1,0:T(8,128)(2,1)}), bf16[16,64,128]{2,1,0:T(8,128)(2,1)S(1)}, u32[]{:S(2)}, u32[]{:S(2)}) %all-to-all-start.5) | async-done | bytes 262176 | tf_op jit(solution)/shard_map/all_to_all | solution.py:90
  121.6 1.4 fusion.6
  123.8 3.5 %all-to-all-start.6 = ((bf16[16,64,128]{2,1,0:T(8,128)(2,1)}), bf16[16,64,128]{2,1,0:T(8,128)(2,1)S(1)}, u32[]{:S(2)}, u32[]{:S(2)}) async-start(bf16[16,64,128]{2,1,0:T(8,128)(2,1)} %bitcast.231), calls=%async_computation.6 | async-start | bytes 524288 | tf_op jit(solution)/shard_map/all_to_all | solution.py:90
  129.8 8.6 %all-to-all-done.6 = bf16[16,64,128]{2,1,0:T(8,128)(2,1)S(1)} async-done(((bf16[16,64,128]{2,1,0:T(8,128)(2,1)}), bf16[16,64,128]{2,1,0:T(8,128)(2,1)S(1)}, u32[]{:S(2)}, u32[]{:S(2)}) %all-to-all-start.6) | async-done | bytes 262176 | tf_op jit(solution)/shard_map/all_to_all | solution.py:90
  140.7 3.5 %all-to-all-start.7 = ((bf16[16,64,128]{2,1,0:T(8,128)(2,1)}), bf16[16,64,128]{2,1,0:T(8,128)(2,1)S(1)}, u32[]{:S(2)}, u32[]{:S(2)}) async-start(bf16[16,64,128]{2,1,0:T(8,128)(2,1)} %bitcast.229), calls=%async_computation.7 | async-start | bytes 524288 | tf_op jit(solution)/shard_map/all_to_all | solution.py:90
  145.9 8.9 %all-to-all-done.7 = bf16[16,64,128]{2,1,0:T(8,128)(2,1)S(1)} async-done(((bf16[16,64,128]{2,1,0:T(8,128)(2,1)}), bf16[16,64,128]{2,1,0:T(8,128)(2,1)S(1)}, u32[]{:S(2)}, u32[]{:S(2)}) %all-to-all-start.7) | async-done | bytes 262176 | tf_op jit(solution)/shard_map/all_to_all | solution.py:90
  156.0 3.5 %all-to-all-start.8 = ((bf16[16,64,128]{2,1,0:T(8,128)(2,1)}), bf16[16,64,128]{2,1,0:T(8,128)(2,1)S(1)}, u32[]{:S(2)}, u32[]{:S(2)}) async-start(bf16[16,64,128]{2,1,0:T(8,128)(2,1)} %bitcast.227), calls=%async_computation.8 | async-start | bytes 524288 | tf_op jit(solution)/shard_map/all_to_all | solution.py:90
  161.0 9.8 %all-to-all-done.8 = bf16[16,64,128]{2,1,0:T(8,128)(2,1)S(1)} async-done(((bf16[16,64,128]{2,1,0:T(8,128)(2,1)}), bf16[16,64,128]{2,1,0:T(8,128)(2,1)S(1)}, u32[]{:S(2)}, u32[]{:S(2)}) %all-to-all-start.8) | async-done | bytes 262176 | tf_op jit(solution)/shard_map/all_to_all | solution.py:90
  171.1 12.5 %collective-permute-start.3 = (f32[5,64,64]{1,2,0:T(8,128)S(1)}, f32[5,64,64]{1,2,0:T(8,128)S(1)}, u32[]{:S(2)}, u32[]{:S(2)}) collective-permute-start(f32[5,64,64]{1,2,0:T(8,128)S(1)} %get-tuple-element.40), channel_id=1, source_target_pairs={{0,1},{1,0},{2,3},{3,2},{4,5},{5,4},{6,7},{7,6},{8,9},{9,8},{10,11... | collective-permute-start | bytes 245768 | tf_op jit(solution)/shard_map/ppermute | solution.py:80
  185.5 17.9 %all_to_all.50.table_ref = bf16[16,20,128]{2,1,0:T(8,128)(2,1)} all-to-all(bf16[16,20,128]{2,1,0:T(8,128)(2,1)S(1)} %copy.71), channel_id=1, replica_groups=mesh['src'=16,'row'=32] {'src'}, dimensions={0} | all-to-all | bytes 163840 | tf_op jit(solution)/shard_map/all_to_all | solution.py:150
  203.4 10.3 %shard_map.68 = f32[5,4,16]{2,1,0:T(4,128)} custom-call(bf16[16,20,128]{2,1,0:T(8,128)(2,1)} %all_to_all.50.table_ref, s32[16,4,1024]{2,1,0:T(4,128)} %bitcast.237, f32[16,1024]{1,0:T(8,128)} %weights_ref.1), custom_call_target="tpu_custom_call" | custom-call | tf_op jit(solution)/shard_map/pallas_call | solution.py:62
  (134 shorter events, 34.9 us)
Async XLA Ops:
  0.6 21.8 %collective-permute-start.2 = (bf16[10,64,2048]{2,1,0:T(8,128)(2,1)}, bf16[10,64,2048]{2,1,0:T(8,128)(2,1)S(1)}, u32[]{:S(2)}, u32[]{:S(2)}) collective-permute-start(bf16[10,64,2048]{2,1,0:T(8,128)(2,1)} %param.6), channel_id=1, source_target_pairs={{0,1},{1,0},{2,3},{3,2},{4,5},{5,4},{6,7},{7,6},{8,9},{9,8},{10,11... | collective-permute-start | bytes 7864328 | tf_op jit(solution)/shard_map/ppermute | solution.py:80
  10.7 5.0 %collective-permute-start = (bf16[5,64,64]{2,1,0:T(8,128)(2,1)S(1)}, bf16[5,64,64]{2,1,0:T(8,128)(2,1)S(1)}, u32[]{:S(2)}, u32[]{:S(2)}) collective-permute-start(bf16[5,64,64]{2,1,0:T(8,128)(2,1)S(1)} %bitcast.238), channel_id=1, source_target_pairs={{0,1},{1,0},{2,3},{3,2},{4,5},{5,4},{6,7},{7,6},{8,9},{9,8},{10,11... | collective-permute-start | bytes 122888 | tf_op jit(solution)/shard_map/ppermute | solution.py:80
  18.2 16.8 %all-to-all-start = ((bf16[16,64,128]{2,1,0:T(8,128)(2,1)}), bf16[16,64,128]{2,1,0:T(8,128)(2,1)}, u32[]{:S(2)}, u32[]{:S(2)}) async-start(bf16[16,64,128]{2,1,0:T(8,128)(2,1)} %broadcast_in_dim.13), calls=%async_computation | async-start | bytes 524288 | tf_op jit(solution)/shard_map/all_to_all | solution.py:90
  23.8 13.2 %copy-start.3 = (bf16[64,2048]{1,0:T(8,128)(2,1)}, bf16[64,2048]{1,0:T(8,128)(2,1)S(1)}, u32[]{:S(2)}) copy-start(bf16[64,2048]{1,0:T(8,128)(2,1)S(1)} %get-tuple-element.28) | copy-start | bytes 786436
  23.8 17.4 %copy-start = (bf16[5,64,2048]{2,1,0:T(8,128)(2,1)S(1)}, bf16[5,64,2048]{2,1,0:T(8,128)(2,1)}, u32[]{:S(2)}) copy-start(bf16[5,64,2048]{2,1,0:T(8,128)(2,1)} %param.7) | copy-start | bytes 3932164
  23.8 20.9 %copy-start.9 = (bf16[64,2048]{1,0:T(8,128)(2,1)S(1)}, bf16[64,2048]{1,0:T(8,128)(2,1)}, u32[]{:S(2)}) copy-start(bf16[64,2048]{1,0:T(8,128)(2,1)} %get-tuple-element.26) | copy-start | bytes 786436
  37.1 16.3 %all-to-all-start.1 = ((bf16[16,64,128]{2,1,0:T(8,128)(2,1)}), bf16[16,64,128]{2,1,0:T(8,128)(2,1)}, u32[]{:S(2)}, u32[]{:S(2)}) async-start(bf16[16,64,128]{2,1,0:T(8,128)(2,1)} %broadcast_in_dim.14), calls=%async_computation.1 | async-start | bytes 524288 | tf_op jit(solution)/shard_map/all_to_all | solution.py:90
  41.3 53.2 %collective-permute-start.1 = (bf16[5,64,2048]{2,1,0:T(8,128)(2,1)S(1)}, bf16[5,64,2048]{2,1,0:T(8,128)(2,1)S(1)}, u32[]{:S(2)}, u32[]{:S(2)}) collective-permute-start(bf16[5,64,2048]{2,1,0:T(8,128)(2,1)S(1)} %copy-done), channel_id=1, source_target_pairs={{0,1},{1,0},{2,3},{3,2},{4,5},{5,4},{6,7},{7,6},{8,9},{9,8},{10,11... | collective-permute-start | bytes 3932168 | tf_op jit(solution)/shard_map/ppermute | solution.py:80
  53.3 7.7 %copy-start.1 = (bf16[64,2048]{1,0:T(8,128)(2,1)S(1)}, bf16[64,2048]{1,0:T(8,128)(2,1)}, u32[]{:S(2)}) copy-start(bf16[64,2048]{1,0:T(8,128)(2,1)} %get-tuple-element.12) | copy-start | bytes 786436
  55.7 15.0 %all-to-all-start.2 = ((bf16[16,64,128]{2,1,0:T(8,128)(2,1)}), bf16[16,64,128]{2,1,0:T(8,128)(2,1)}, u32[]{:S(2)}, u32[]{:S(2)}) async-start(bf16[16,64,128]{2,1,0:T(8,128)(2,1)} %broadcast_in_dim.15), calls=%async_computation.2 | async-start | bytes 524288 | tf_op jit(solution)/shard_map/all_to_all | solution.py:90
  73.0 14.9 %all-to-all-start.3 = ((bf16[16,64,128]{2,1,0:T(8,128)(2,1)}), bf16[16,64,128]{2,1,0:T(8,128)(2,1)}, u32[]{:S(2)}, u32[]{:S(2)}) async-start(bf16[16,64,128]{2,1,0:T(8,128)(2,1)} %broadcast_in_dim.16), calls=%async_computation.3 | async-start | bytes 524288 | tf_op jit(solution)/shard_map/all_to_all | solution.py:90
  90.3 14.7 %all-to-all-start.4 = ((bf16[16,64,128]{2,1,0:T(8,128)(2,1)}), bf16[16,64,128]{2,1,0:T(8,128)(2,1)}, u32[]{:S(2)}, u32[]{:S(2)}) async-start(bf16[16,64,128]{2,1,0:T(8,128)(2,1)} %broadcast_in_dim.17), calls=%async_computation.4 | async-start | bytes 524288 | tf_op jit(solution)/shard_map/all_to_all | solution.py:90
  94.5 10.5 %copy-start.30 = (bf16[64,2048]{1,0:T(8,128)(2,1)S(1)}, bf16[64,2048]{1,0:T(8,128)(2,1)}, u32[]{:S(2)}) copy-start(bf16[64,2048]{1,0:T(8,128)(2,1)} %get-tuple-element.32) | copy-start | bytes 786436
  95.5 10.8 %copy-start.22 = (bf16[64,2048]{1,0:T(8,128)(2,1)S(1)}, bf16[64,2048]{1,0:T(8,128)(2,1)}, u32[]{:S(2)}) copy-start(bf16[64,2048]{1,0:T(8,128)(2,1)} %get-tuple-element.10) | copy-start | bytes 786436
  95.5 10.8 %copy-start.27 = (bf16[64,2048]{1,0:T(8,128)(2,1)S(1)}, bf16[64,2048]{1,0:T(8,128)(2,1)}, u32[]{:S(2)}) copy-start(bf16[64,2048]{1,0:T(8,128)(2,1)} %get-tuple-element.20) | copy-start | bytes 786436
  107.4 14.1 %all-to-all-start.5 = ((bf16[16,64,128]{2,1,0:T(8,128)(2,1)}), bf16[16,64,128]{2,1,0:T(8,128)(2,1)S(1)}, u32[]{:S(2)}, u32[]{:S(2)}) async-start(bf16[16,64,128]{2,1,0:T(8,128)(2,1)} %bitcast.233), calls=%async_computation.5 | async-start | bytes 524288 | tf_op jit(solution)/shard_map/all_to_all | solution.py:90
  112.2 9.3 %copy-start.13 = (bf16[64,2048]{1,0:T(8,128)(2,1)S(1)}, bf16[64,2048]{1,0:T(8,128)(2,1)}, u32[]{:S(2)}) copy-start(bf16[64,2048]{1,0:T(8,128)(2,1)} %get-tuple-element.19) | copy-start | bytes 786436
  112.3 9.3 %copy-start.23 = (bf16[64,2048]{1,0:T(8,128)(2,1)S(1)}, bf16[64,2048]{1,0:T(8,128)(2,1)}, u32[]{:S(2)}) copy-start(bf16[64,2048]{1,0:T(8,128)(2,1)} %get-tuple-element.21) | copy-start | bytes 786436
  113.8 13.5 %copy-start.8 = (bf16[64,2048]{1,0:T(8,128)(2,1)S(1)}, bf16[64,2048]{1,0:T(8,128)(2,1)}, u32[]{:S(2)}) copy-start(bf16[64,2048]{1,0:T(8,128)(2,1)} %get-tuple-element.18) | copy-start | bytes 786436
  113.8 13.5 %copy-start.21 = (bf16[64,2048]{1,0:T(8,128)(2,1)S(1)}, bf16[64,2048]{1,0:T(8,128)(2,1)}, u32[]{:S(2)}) copy-start(bf16[64,2048]{1,0:T(8,128)(2,1)} %get-tuple-element.29) | copy-start | bytes 786436
  121.6 6.8 %copy-start.7 = (bf16[64,2048]{1,0:T(8,128)(2,1)S(1)}, bf16[64,2048]{1,0:T(8,128)(2,1)}, u32[]{:S(2)}) copy-start(bf16[64,2048]{1,0:T(8,128)(2,1)} %get-tuple-element.16) | copy-start | bytes 786436
  123.8 14.6 %all-to-all-start.6 = ((bf16[16,64,128]{2,1,0:T(8,128)(2,1)}), bf16[16,64,128]{2,1,0:T(8,128)(2,1)S(1)}, u32[]{:S(2)}, u32[]{:S(2)}) async-start(bf16[16,64,128]{2,1,0:T(8,128)(2,1)} %bitcast.231), calls=%async_computation.6 | async-start | bytes 524288 | tf_op jit(solution)/shard_map/all_to_all | solution.py:90
  128.4 10.2 %copy-start.2 = (bf16[64,2048]{1,0:T(8,128)(2,1)S(1)}, bf16[64,2048]{1,0:T(8,128)(2,1)}, u32[]{:S(2)}) copy-start(bf16[64,2048]{1,0:T(8,128)(2,1)} %get-tuple-element.14) | copy-start | bytes 786436
  128.4 10.2 %copy-start.15 = (bf16[64,2048]{1,0:T(8,128)(2,1)S(1)}, bf16[64,2048]{1,0:T(8,128)(2,1)}, u32[]{:S(2)}) copy-start(bf16[64,2048]{1,0:T(8,128)(2,1)} %get-tuple-element.25) | copy-start | bytes 786436
  128.7 15.6 %copy-start.12 = (bf16[64,2048]{1,0:T(8,128)(2,1)S(1)}, bf16[64,2048]{1,0:T(8,128)(2,1)}, u32[]{:S(2)}) copy-start(bf16[64,2048]{1,0:T(8,128)(2,1)} %get-tuple-element.23) | copy-start | bytes 786436
  138.5 7.1 %copy-start.10 = (bf16[64,2048]{1,0:T(8,128)(2,1)S(1)}, bf16[64,2048]{1,0:T(8,128)(2,1)}, u32[]{:S(2)}) copy-start(bf16[64,2048]{1,0:T(8,128)(2,1)} %get-tuple-element.26) | copy-start | bytes 786436
  139.9 15.0 %copy-start.4 = (bf16[64,2048]{1,0:T(8,128)(2,1)S(1)}, bf16[64,2048]{1,0:T(8,128)(2,1)}, u32[]{:S(2)}) copy-start(bf16[64,2048]{1,0:T(8,128)(2,1)} %copy-done.3) | copy-start | bytes 786436
  140.7 14.1 %all-to-all-start.7 = ((bf16[16,64,128]{2,1,0:T(8,128)(2,1)}), bf16[16,64,128]{2,1,0:T(8,128)(2,1)S(1)}, u32[]{:S(2)}, u32[]{:S(2)}) async-start(bf16[16,64,128]{2,1,0:T(8,128)(2,1)} %bitcast.229), calls=%async_computation.7 | async-start | bytes 524288 | tf_op jit(solution)/shard_map/all_to_all | solution.py:90
  145.6 13.9 %copy-start.14 = (bf16[64,2048]{1,0:T(8,128)(2,1)S(1)}, bf16[64,2048]{1,0:T(8,128)(2,1)}, u32[]{:S(2)}) copy-start(bf16[64,2048]{1,0:T(8,128)(2,1)} %get-tuple-element.33) | copy-start | bytes 786436
  145.6 13.9 %copy-start.26 = (bf16[64,2048]{1,0:T(8,128)(2,1)S(1)}, bf16[64,2048]{1,0:T(8,128)(2,1)}, u32[]{:S(2)}) copy-start(bf16[64,2048]{1,0:T(8,128)(2,1)} %get-tuple-element.39) | copy-start | bytes 786436
  156.0 14.8 %all-to-all-start.8 = ((bf16[16,64,128]{2,1,0:T(8,128)(2,1)}), bf16[16,64,128]{2,1,0:T(8,128)(2,1)S(1)}, u32[]{:S(2)}, u32[]{:S(2)}) async-start(bf16[16,64,128]{2,1,0:T(8,128)(2,1)} %bitcast.227), calls=%async_computation.8 | async-start | bytes 524288 | tf_op jit(solution)/shard_map/all_to_all | solution.py:90
  171.1 13.5 %collective-permute-start.3 = (f32[5,64,64]{1,2,0:T(8,128)S(1)}, f32[5,64,64]{1,2,0:T(8,128)S(1)}, u32[]{:S(2)}, u32[]{:S(2)}) collective-permute-start(f32[5,64,64]{1,2,0:T(8,128)S(1)} %get-tuple-element.40), channel_id=1, source_target_pairs={{0,1},{1,0},{2,3},{3,2},{4,5},{5,4},{6,7},{7,6},{8,9},{9,8},{10,11... | collective-permute-start | bytes 245768 | tf_op jit(solution)/shard_map/ppermute | solution.py:80
  (16 other events, 62.1 us)

commit v4 on v3

--- a/solution.py
+++ b/solution.py
@@ -2,6 +2,7 @@
 import jax.numpy as jnp
 from jax import lax
 from jax.experimental import pallas as pl
+from jax.experimental.pallas import tpu as pltpu
 from jax.sharding import PartitionSpec as P
 
 BF = jnp.bfloat16
@@ -16,6 +17,78 @@
     return lax.dot_general(
         left, right, (((left_dim,), (right_dim,)), ((), ())), preferred_element_type=F32
     )
+
+
+SCALAR = pl.BlockSpec(memory_space=pltpu.SMEM)
+WHOLE = pl.BlockSpec(memory_space=pltpu.VMEM)
+PARAMS = pltpu.CompilerParams(vmem_limit_bytes=24 * 1024 * 1024)
+
+
+def lay_rows(core, mine_ref, other_ref, wide_ref):
+    rows = mine_ref.shape[0]
+    wide_ref[pl.ds(pl.multiple_of(core * rows, rows), rows)] = mine_ref[...]
+    wide_ref[pl.ds(pl.multiple_of((1 - core) * rows, rows), rows)] = other_ref[...]
+
+
+def lay_columns(got_ref, full_ref):
+    for chip in range(got_ref.shape[0]):
+        lanes = got_ref.shape[2]
+        full_ref[:, chip * lanes : (chip + 1) * lanes] = got_ref[chip]
+
+
+def ahead_kernel(core_ref, base_ref, got_ref, mine_ref, other_ref, out_ref, wide_ref, full_ref):
+    lay_rows(core_ref[0], mine_ref, other_ref, wide_ref)
+    lay_columns(got_ref, full_ref)
+    value = base_ref[...] - dot(full_ref[...], wide_ref[...], 1, 1)
+    value = value.astype(BF)
+    for chip in range(out_ref.shape[0]):
+        out_ref[chip] = value
+
+
+def send_pieces(part, out_ref):
+    lanes = out_ref.shape[2]
+    for chip in range(out_ref.shape[0]):
+        out_ref[chip] = part[:, chip * lanes : (chip + 1) * lanes].astype(BF)
+
+
+def turn_kernel(
+    core_ref, got_ref, mine_d_ref, other_d_ref, mine_ref, other_ref, out_ref, x_ref, wide_ref, full_ref
+):
+    lay_rows(core_ref[0], mine_d_ref, other_d_ref, wide_ref)
+    lay_columns(got_ref, full_ref)
+    value = dot(full_ref[...], wide_ref[...], 1, 1)
+    x_ref[...] = value
+    lay_rows(core_ref[0], mine_ref, other_ref, wide_ref)
+    send_pieces(dot(value.astype(BF), wide_ref[...], 1, 0), out_ref)
+
+
+def back_kernel(
+    core_ref, base_ref, got_ref, part_ref, mine_ref, other_ref, out_ref, x_ref, wide_ref
+):
+    lay_rows(core_ref[0], mine_ref, other_ref, wide_ref)
+    value = base_ref[...]
+    for chip in range(got_ref.shape[0]):
+        value = value - got_ref[chip].astype(F32)
+    x_ref[...] = value
+    part = part_ref[...] + dot(value.astype(BF), wide_ref[...], 1, 0)
+    send_pieces(part, out_ref)
+
+
+def call(kernel, core, operands, got, solved, full):
+    size = got.shape[0] * got.shape[2]
+    out = jax.ShapeDtypeStruct(got.shape, BF)
+    x = jax.ShapeDtypeStruct(got.shape[1:], F32)
+    scratch = [pltpu.VMEM((got.shape[2], size), BF)]
+    if full:
+        scratch.append(pltpu.VMEM((got.shape[1], size), BF))
+    return pl.pallas_call(
+        kernel,
+        out_shape=(out, x) if solved else out,
+        in_specs=[SCALAR] + [WHOLE] * len(operands),
+        out_specs=(WHOLE, WHOLE) if solved else WHOLE,
+        scratch_shapes=scratch,
+        compiler_params=PARAMS,
+    )(core, *operands)
 
 
 def weigh_kernel(table_ref, picks_ref, weights_ref, out_ref):
@@ -64,6 +137,9 @@
         out_shape=jax.ShapeDtypeStruct(
             (panels, table.shape[1] // panels, weights.shape[0]), F32
         ),
+        in_specs=[WHOLE] * 3,
+        out_specs=WHOLE,
+        compiler_params=PARAMS,
     )(table, picks, weights)
 
 
@@ -91,12 +167,8 @@
             blocks, "row", split_axis=0, concat_axis=0, tiled=True, axis_index_groups=same_core
         )
 
-    def gather(value):
-        got = exchange(jnp.broadcast_to(value[None], (chips,) + value.shape))
-        return jnp.transpose(got, (1, 0, 2)).reshape(value.shape[0], size)
-
-    def pieces_of(part):
-        return jnp.transpose(part.astype(BF).reshape(half, chips, tall), (1, 0, 2))
+    def collect(got):
+        return jnp.transpose(got, (1, 0, 2)).reshape(half, size)
 
     tall = 2 * rows
     groups = lax.axis_size("src")
@@ -120,25 +192,42 @@
     }
     inverses = [in_order(block_inverse[k], other_inverse[k], 0) for k in range(panels)]
 
+    def halves(later, earlier):
+        at = pair_index(later, earlier)
+        return [coupling[at], other_coupling[at]]
+
+    place = core.reshape(1)
+    message = jnp.broadcast_to(rhs[0][None], (chips,) + rhs[0].shape)
     full = []
     for panel in range(panels):
-        total = rhs[panel].astype(F32)
-        for earlier in range(panel):
-            total = total - dot(full[earlier], factors[panel, earlier], 1, 1)
-        full.append(gather(total.astype(BF)))
-    totals = [lax.optimization_barrier(dot(full[k], inverses[k], 1, 1)) for k in range(panels)]
-
+        got = exchange(message)
+        full.append(collect(got))
+        if panel + 1 < panels:
+            base = rhs[panel + 1].astype(F32)
+            for earlier in range(panel):
+                base = base - dot(full[earlier], factors[panel + 1, earlier], 1, 1)
+            operands = [base, got] + halves(panel + 1, panel)
+            message = call(ahead_kernel, place, operands, got, False, True)
+    totals = [
+        lax.optimization_barrier(dot(full[k], inverses[k], 1, 1)) for k in range(panels - 1)
+    ]
+
+    last = panels - 1
+    solved = [None] * panels
     rounded = [None] * panels
-    solved = [None] * panels
-    for panel in reversed(range(panels)):
-        total = totals[panel]
-        if panel < panels - 1:
-            part = dot(rounded[panels - 1], factors[panels - 1, panel], 1, 0)
-            for later in reversed(range(panel + 1, panels - 1)):
-                part = part + dot(rounded[later], factors[later, panel], 1, 0)
-            total = total - jnp.sum(exchange(pieces_of(part)).astype(F32), axis=0)
-        rounded[panel] = total.astype(BF)
-        solved[panel] = total
+    operands = [got, block_inverse[last], other_inverse[last]] + halves(last, last - 1)
+    message, solved[last] = call(turn_kernel, place, operands, got, True, True)
+    for panel in reversed(range(last)):
+        rounded[panel + 1] = solved[panel + 1].astype(BF)
+        got = exchange(message)
+        if panel:
+            part = dot(rounded[last], factors[last, panel - 1], 1, 0)
+            for later in reversed(range(panel + 1, last)):
+                part = part + dot(rounded[later], factors[later, panel - 1], 1, 0)
+            operands = [totals[panel], got, part] + halves(panel, panel - 1)
+            message, solved[panel] = call(back_kernel, place, operands, got, True, False)
+        else:
+            solved[panel] = totals[panel] - jnp.sum(got.astype(F32), axis=0)
 
     solved = jnp.stack(solved)
     keep = lax.dynamic_slice_in_dim(solved, core * rows, rows, axis=2)

time: 215 us -> 201 us (0.935)
  blocking collectives: 17.9 us -> 0 us
  matrix products: 29.1 us -> 17.7 us
  starting transfers between devices: 61.7 us -> 69.6 us
  Pallas kernels: 10.3 us -> 15.7 us
  waiting for transfers between devices: 74.6 us -> 78.6 us
    all_to_all x1 -> x0, blocking collectives: 17.9 us -> none  [shards(): lax.all_to_all(table, 'src', split_axis=0, concat_axis=0, tiled=True)]
    dot_general x25 -> x16, matrix products: 29.1 us -> 17.7 us  [dot(): lax.dot_general(left, right, (((left_dim,), (right_dim,)), ((), ())), pre...]
    all_to_all x0 -> x1, starting transfers between devices: none -> 10.6 us  [shards(): lax.all_to_all(table, 'src', split_axis=0, concat_axis=0, tiled=True)]
    all_to_all x0 -> x1, waiting for transfers between devices: none -> 6.58 us  [shards(): lax.all_to_all(table, 'src', split_axis=0, concat_axis=0, tiled=True)]
    pallas_call x0 -> x8, Pallas kernels: none -> 6.4 us  [call(): pl.pallas_call(kernel, out_shape=(out, x) if solved else out, in_specs=[S...]
    squeeze x4, local copies, waits for them, and re-layouts: 6.46 us -> 10.3 us  [the longest x2 5.67 us: halves(): return [coupling[at], other_coupling[at]]]
    reshape x4 -> x0, local copies, waits for them, and re-layouts: 3.09 us -> none  [pieces_of(): return jnp.transpose(part.astype(BF).reshape(half, chips, tall), (1, 0, 2))]
    broadcast_in_dim x6 -> x1, local copies, waits for them, and re-layouts: 3.85 us -> 0.76 us  [shards(): message = jnp.broadcast_to(rhs[0][None], (chips,) + rhs[0].shape)]
  transfers between devices with their start and end apart: 13 -> 14, of which waited for: 10 -> 11; matrix products, arithmetic and copies ran while one was open for 17% -> 16% of each run, Pallas kernels for 0% -> 1%
where the time goes in v4:
time: 201 us; the launch traced here: 199 us
  waiting for transfers between devices  78.6 us (39%)
  starting transfers between devices  69.6 us (35%)
  matrix products  17.7 us (9%)
  local copies, waits for them, and re-layouts  16.3 us (8%)
  Pallas kernels  15.7 us (8%)
    all_to_all x9, waiting for transfers between devices, exchange(): lax.all_to_all(blocks, 'row', split_axis=0, concat_axis=0, tiled=True, ax...  71 us
    all_to_all x9, starting transfers between devices, exchange(): lax.all_to_all(blocks, 'row', split_axis=0, concat_axis=0, tiled=True, ax...  32.5 us
    ppermute x4, starting transfers between devices, swap(): return lax.ppermute(value, 'row', pairs)  26.5 us
    dot_general x16, matrix products, dot(): lax.dot_general(left, right, (((left_dim,), (right_dim,)), ((), ())), pre...  17.7 us
    all_to_all x1, starting transfers between devices, shards(): lax.all_to_all(table, 'src', split_axis=0, concat_axis=0, tiled=True)  10.6 us
    pallas_call x1, Pallas kernels, weigh(): pl.pallas_call(weigh_kernel, out_shape=jax.ShapeDtypeStruct((panels, tabl...  9.31 us
    all_to_all x1, waiting for transfers between devices, shards(): lax.all_to_all(table, 'src', split_axis=0, concat_axis=0, tiled=True)  6.58 us
    pallas_call x8, Pallas kernels, call(): pl.pallas_call(kernel, out_shape=(out, x) if solved else out, in_specs=[S...  6.4 us
  transfers between devices with their start and end apart: 14, of which 11 were waited for; matrix products, arithmetic and copies ran while one was open for 16% of the time, Pallas kernels for 1%

profile of v4, /device:TPU:1, one launch (start us, length us, event | category | flops | bytes accessed | tf_op | source)
XLA Modules:
  0.0 199.5 jit_solution(9009414196544619533)
XLA Ops:
  0.6 8.8 %collective-permute-start.2 = (bf16[10,64,2048]{2,1,0:T(8,128)(2,1)}, bf16[10,64,2048]{2,1,0:T(8,128)(2,1)}, u32[]{:S(2)}, u32[]{:S(2)}) collective-permute-start(bf16[10,64,2048]{2,1,0:T(8,128)(2,1)} %param.6), channel_id=1, source_target_pairs={{0,1},{1,0},{2,3},{3,2},{4,5},{5,4},{6,7},{7,6},{8,9},{9,8},{10,11... | collective-permute-start | bytes 7864328 | tf_op jit(solution)/shard_map/ppermute | solution.py:156
  10.7 1.9 collective-permute-start
  12.6 2.8 %slice_bitcast_fusion.16 = (bf16[64,2048]{1,0:T(8,128)(2,1)S(1)}, bf16[64,2048]{1,0:T(8,128)(2,1)}, bf16[64,2048]{1,0:T(8,128)(2,1)}, bf16[64,2048]{1,0:T(8,128)...) fusion(bf16[10,64,2048]{2,1,0:T(8,128)(2,1)} %param.6), kind=kLoop, calls=%fused_computation.77 | loop fusion | bytes 5242880 | tf_op jit(solution)/shard_map/squeeze | solution.py:197
  16.4 4.0 %all-to-all-start = ((bf16[16,64,128]{2,1,0:T(8,128)(2,1)}), bf16[16,64,128]{2,1,0:T(8,128)(2,1)S(1)}, u32[]{:S(2)}, u32[]{:S(2)}) async-start(bf16[16,64,128]{2,1,0:T(8,128)(2,1)} %broadcast_in_dim.8), calls=%async_computation | async-start | bytes 524288 | tf_op jit(solution)/shard_map/all_to_all | solution.py:166
  20.5 2.9 %slice_bitcast_fusion.1 = (bf16[64,2048]{1,0:T(8,128)(2,1)S(1)}, bf16[64,2048]{1,0:T(8,128)(2,1)}, bf16[64,2048]{1,0:T(8,128)(2,1)}, bf16[64,2048]{1,0:T(8,128)(...) fusion(bf16[10,64,2048]{2,1,0:T(8,128)(2,1)} %collective-permut, ...), kind=kLoop, calls=%fused_computation.62 | loop fusion | bytes 5242880 | tf_op jit(solution)/shard_map/squeeze | solution.py:197
  23.3 9.7 %all-to-all-done.got_ref = bf16[16,64,128]{2,1,0:T(8,128)(2,1)S(1)} async-done(((bf16[16,64,128]{2,1,0:T(8,128)(2,1)}), bf16[16,64,128]{2,1,0:T(8,128)(2,1)S(1)}, u32[]{:S(2)}, u32[]{:S(2)}) %all-to-all-start) | async-done | bytes 262176 | tf_op jit(solution)/shard_map/all_to_all | solution.py:166
  34.1 3.6 %all-to-all-start.1 = ((bf16[16,64,128]{2,1,0:T(8,128)(2,1)}), bf16[16,64,128]{2,1,0:T(8,128)(2,1)S(1)}, u32[]{:S(2)}, u32[]{:S(2)}) async-start(bf16[16,64,128]{2,1,0:T(8,128)(2,1)} %shard_map.68), calls=%async_computation.1 | async-start | bytes 524288 | tf_op jit(solution)/shard_map/all_to_all | solution.py:166
  37.7 3.2 %collective-permute-start.1 = (bf16[5,64,2048]{2,1,0:T(8,128)(2,1)}, bf16[5,64,2048]{2,1,0:T(8,128)(2,1)}, u32[]{:S(2)}, u32[]{:S(2)}) collective-permute-start(bf16[5,64,2048]{2,1,0:T(8,128)(2,1)} %param.7), channel_id=1, source_target_pairs={{0,1},{1,0},{2,3},{3,2},{4,5},{5,4},{6,7},{7,6},{8,9},{9,8},{10,11... | collective-permute-start | bytes 3932168 | tf_op jit(solution)/shard_map/ppermute | solution.py:156
  42.3 7.4 %all-to-all-done.1.got_ref = bf16[16,64,128]{2,1,0:T(8,128)(2,1)S(1)} async-done(((bf16[16,64,128]{2,1,0:T(8,128)(2,1)}), bf16[16,64,128]{2,1,0:T(8,128)(2,1)S(1)}, u32[]{:S(2)}, u32[]{:S(2)}) %all-to-all-start.1) | async-done | bytes 262176 | tf_op jit(solution)/shard_map/all_to_all | solution.py:166
  50.8 3.5 %all-to-all-start.2 = ((bf16[16,64,128]{2,1,0:T(8,128)(2,1)}), bf16[16,64,128]{2,1,0:T(8,128)(2,1)S(1)}, u32[]{:S(2)}, u32[]{:S(2)}) async-start(bf16[16,64,128]{2,1,0:T(8,128)(2,1)} %shard_map.69), calls=%async_computation.2 | async-start | bytes 524288 | tf_op jit(solution)/shard_map/all_to_all | solution.py:166
  54.4 2.3 %slice_bitcast_fusion.15 = (bf16[64,2048]{1,0:T(8,128)(2,1)S(1)}, bf16[64,2048]{1,0:T(8,128)(2,1)}, bf16[64,2048]{1,0:T(8,128)(2,1)}, bf16[64,2048]{1,0:T(8,128)(2,1)}, bf16[64,2048]{1,0:T(8,128)(2,1)}) fusion(bf16[5,64,2048]{2,1,0:T(8,128)(2,1)} %param.7), kind=kLoop, calls=%fused_computation.76 | loop fusion | bytes 2621440 | tf_op jit(solution)/shard_map/squeeze | solution.py:218
  58.4 6.7 %all-to-all-done.2.got_ref = bf16[16,64,128]{2,1,0:T(8,128)(2,1)S(1)} async-done(((bf16[16,64,128]{2,1,0:T(8,128)(2,1)}), bf16[16,64,128]{2,1,0:T(8,128)(2,1)S(1)}, u32[]{:S(2)}, u32[]{:S(2)}) %all-to-all-start.2) | async-done | bytes 262176 | tf_op jit(solution)/shard_map/all_to_all | solution.py:166
  66.2 3.5 %all-to-all-start.3 = ((bf16[16,64,128]{2,1,0:T(8,128)(2,1)}), bf16[16,64,128]{2,1,0:T(8,128)(2,1)S(1)}, u32[]{:S(2)}, u32[]{:S(2)}) async-start(bf16[16,64,128]{2,1,0:T(8,128)(2,1)} %copy-done.4), calls=%async_computation.3 | async-start | bytes 524288 | tf_op jit(solution)/shard_map/all_to_all | solution.py:166
  69.7 1.5 convolution_subtract_fusion.2
  73.1 7.1 %all-to-all-done.3.got_ref = bf16[16,64,128]{2,1,0:T(8,128)(2,1)S(1)} async-done(((bf16[16,64,128]{2,1,0:T(8,128)(2,1)}), bf16[16,64,128]{2,1,0:T(8,128)(2,1)S(1)}, u32[]{:S(2)}, u32[]{:S(2)}) %all-to-all-start.3) | async-done | bytes 262176 | tf_op jit(solution)/shard_map/all_to_all | solution.py:166
  81.3 3.5 %all-to-all-start.4 = ((bf16[16,64,128]{2,1,0:T(8,128)(2,1)}), bf16[16,64,128]{2,1,0:T(8,128)(2,1)S(1)}, u32[]{:S(2)}, u32[]{:S(2)}) async-start(bf16[16,64,128]{2,1,0:T(8,128)(2,1)} %copy-done.3), calls=%async_computation.4 | async-start | bytes 524288 | tf_op jit(solution)/shard_map/all_to_all | solution.py:166
  84.9 2.3 %slice_bitcast_fusion = (bf16[64,2048]{1,0:T(8,128)(2,1)S(1)}, bf16[64,2048]{1,0:T(8,128)(2,1)}, bf16[64,2048]{1,0:T(8,128)(2,1)}, bf16[64,2048]{1,0:T(8,128)(2,1)S(1)}, bf16[64,2048]{1,0:T(8,128)(2,1)}) fusion(bf16[5,64,2048]{2,1,0:T(8,128)(2,1)} %collective-permute-done.1), kind=kLoop, calls=%fused_computation.61 | loop fusion | bytes 2621440 | tf_op jit(solution)/shard_map/squeeze | solution.py:218
  88.4 6.9 %all-to-all-done.4.got_ref = bf16[16,64,128]{2,1,0:T(8,128)(2,1)S(1)} async-done(((bf16[16,64,128]{2,1,0:T(8,128)(2,1)}), bf16[16,64,128]{2,1,0:T(8,128)(2,1)S(1)}, u32[]{:S(2)}, u32[]{:S(2)}) %all-to-all-start.4) | async-done | bytes 262176 | tf_op jit(solution)/shard_map/all_to_all | solution.py:166
  96.6 3.7 %all-to-all-start.5 = ((bf16[16,64,128]{2,1,0:T(8,128)(2,1)}), bf16[16,64,128]{2,1,0:T(8,128)(2,1)S(1)}, u32[]{:S(2)}, u32[]{:S(2)}) async-start(bf16[16,64,128]{2,1,0:T(8,128)(2,1)} %copy-done.6), calls=%async_computation.5 | async-start | bytes 524288 | tf_op jit(solution)/shard_map/all_to_all | solution.py:166
  100.3 1.5 fusion.12.base_ref
  103.5 7.8 %all-to-all-done.5.got_ref = bf16[16,64,128]{2,1,0:T(8,128)(2,1)S(1)} async-done(((bf16[16,64,128]{2,1,0:T(8,128)(2,1)}), bf16[16,64,128]{2,1,0:T(8,128)(2,1)S(1)}, u32[]{:S(2)}, u32[]{:S(2)}) %all-to-all-start.5) | async-done | bytes 262176 | tf_op jit(solution)/shard_map/all_to_all | solution.py:166
  112.3 3.5 %all-to-all-start.6 = ((bf16[16,64,128]{2,1,0:T(8,128)(2,1)}), bf16[16,64,128]{2,1,0:T(8,128)(2,1)S(1)}, u32[]{:S(2)}, u32[]{:S(2)}) async-start(bf16[16,64,128]{2,1,0:T(8,128)(2,1)} %get-tuple-element.12), calls=%async_computation.6 | async-start | bytes 524288 | tf_op jit(solution)/shard_map/all_to_all | solution.py:166
  115.9 2.3 %fusion.51 = f32[64,2048]{1,0:T(8,128)} fusion(bf16[64,2048]{1,0:T(8,128)(2,1)} %get-tuple-element.29, bf16[64,2048]{1,0:T(8,128)(2,1)} %get-tuple-element.38, pred[]{:T(512)S(6)} %eq.4, f32[64,128]{1,0:T(8,128)S(1)} %get-tuple-element.11), kind=kOutput, calls=%fused_computation.102 | convolution fusion | flops 35921920 | bytes 1081345 | tf_op jit(solution)/shard_map/dot_general | solution.py:17
  120.9 5.8 %all-to-all-done.6.got_ref = bf16[16,64,128]{2,1,0:T(8,128)(2,1)S(1)} async-done(((bf16[16,64,128]{2,1,0:T(8,128)(2,1)}), bf16[16,64,128]{2,1,0:T(8,128)(2,1)S(1)}, u32[]{:S(2)}, u32[]{:S(2)}) %all-to-all-start.6) | async-done | bytes 262176 | tf_op jit(solution)/shard_map/all_to_all | solution.py:166
  127.6 3.5 %all-to-all-start.7 = ((bf16[16,64,128]{2,1,0:T(8,128)(2,1)}), bf16[16,64,128]{2,1,0:T(8,128)(2,1)S(1)}, u32[]{:S(2)}, u32[]{:S(2)}) async-start(bf16[16,64,128]{2,1,0:T(8,128)(2,1)} %get-tuple-element.14), calls=%async_computation.7 | async-start | bytes 524288 | tf_op jit(solution)/shard_map/all_to_all | solution.py:166
  133.0 9.2 %all-to-all-done.7.got_ref = bf16[16,64,128]{2,1,0:T(8,128)(2,1)S(1)} async-done(((bf16[16,64,128]{2,1,0:T(8,128)(2,1)}), bf16[16,64,128]{2,1,0:T(8,128)(2,1)S(1)}, u32[]{:S(2)}, u32[]{:S(2)}) %all-to-all-start.7) | async-done | bytes 262176 | tf_op jit(solution)/shard_map/all_to_all | solution.py:166
  143.1 3.5 %all-to-all-start.8 = ((bf16[16,64,128]{2,1,0:T(8,128)(2,1)}), bf16[16,64,128]{2,1,0:T(8,128)(2,1)S(1)}, u32[]{:S(2)}, u32[]{:S(2)}) async-start(bf16[16,64,128]{2,1,0:T(8,128)(2,1)} %get-tuple-element.16), calls=%async_computation.8 | async-start | bytes 524288 | tf_op jit(solution)/shard_map/all_to_all | solution.py:166
  147.0 10.4 %all-to-all-done.8 = bf16[16,64,128]{2,1,0:T(8,128)(2,1)S(1)} async-done(((bf16[16,64,128]{2,1,0:T(8,128)(2,1)}), bf16[16,64,128]{2,1,0:T(8,128)(2,1)S(1)}, u32[]{:S(2)}, u32[]{:S(2)}) %all-to-all-start.8) | async-done | bytes 262176 | tf_op jit(solution)/shard_map/all_to_all | solution.py:166
  157.7 12.6 %collective-permute-start.3 = (f32[5,64,64]{2,1,0:T(8,128)S(1)}, f32[5,64,64]{2,1,0:T(8,128)S(1)}, u32[]{:S(2)}, u32[]{:S(2)}) collective-permute-start(f32[5,64,64]{2,1,0:T(8,128)S(1)} %get-tuple-element.56), channel_id=1, source_target_pairs={{0,1},{1,0},{2,3},{3,2},{4,5},{5,4},{6,7},{7,6},{8,9},{9,8},{10,11... | collective-permute-start | bytes 245768 | tf_op jit(solution)/shard_map/ppermute | solution.py:156
  172.2 10.6 %all-to-all-start.9 = ((bf16[16,20,128]{2,1,0:T(8,128)(2,1)}), bf16[16,20,128]{2,1,0:T(8,128)(2,1)S(1)}, u32[]{:S(2)}, u32[]{:S(2)}) async-start(bf16[16,20,128]{2,1,0:T(8,128)(2,1)} %copy.29), calls=%async_computation.9 | async-start | bytes 196608 | tf_op jit(solution)/shard_map/all_to_all | solution.py:239
  183.6 6.6 %all-to-all-done.9.table_ref = bf16[16,20,128]{2,1,0:T(8,128)(2,1)S(1)} async-done(((bf16[16,20,128]{2,1,0:T(8,128)(2,1)}), bf16[16,20,128]{2,1,0:T(8,128)(2,1)S(1)}, u32[]{:S(2)}, u32[]{:S(2)}) %all-to-all-start.9) | async-done | bytes 81952 | tf_op jit(solution)/shard_map/all_to_all | solution.py:239
  190.2 9.3 %shard_map.76 = f32[5,4,16]{2,1,0:T(4,128)} custom-call(bf16[16,20,128]{2,1,0:T(8,128)(2,1)S(1)} %all-to-all-done.9.table_ref, s32[16,4,1024]{2,1,0:T(4,128)S(1)} %bitcast.166, f32[16,1024]{1,0:T(8,128)S(1)} %copy-done.7), custom_call_target="tpu_custom_call" | custom-call | tf_op jit(solution)/shard_map/pallas_call | solution.py:135
  (93 shorter events, 26.1 us)
Async XLA Ops:
  0.6 19.8 %collective-permute-start.2 = (bf16[10,64,2048]{2,1,0:T(8,128)(2,1)}, bf16[10,64,2048]{2,1,0:T(8,128)(2,1)}, u32[]{:S(2)}, u32[]{:S(2)}) collective-permute-start(bf16[10,64,2048]{2,1,0:T(8,128)(2,1)} %param.6), channel_id=1, source_target_pairs={{0,1},{1,0},{2,3},{3,2},{4,5},{5,4},{6,7},{7,6},{8,9},{9,8},{10,11... | collective-permute-start | bytes 7864328 | tf_op jit(solution)/shard_map/ppermute | solution.py:156
  10.7 4.9 %collective-permute-start = (bf16[5,64,64]{2,1,0:T(8,128)(2,1)S(1)}, bf16[5,64,64]{2,1,0:T(8,128)(2,1)S(1)}, u32[]{:S(2)}, u32[]{:S(2)}) collective-permute-start(bf16[5,64,64]{2,1,0:T(8,128)(2,1)S(1)} %bitcast.170), channel_id=1, source_target_pairs={{0,1},{1,0},{2,3},{3,2},{4,5},{5,4},{6,7},{7,6},{8,9},{9,8},{10,11... | collective-permute-start | bytes 122888 | tf_op jit(solution)/shard_map/ppermute | solution.py:156
  15.4 25.6 %copy-start.8 = (bf16[64,2048]{1,0:T(8,128)(2,1)}, bf16[64,2048]{1,0:T(8,128)(2,1)S(1)}, u32[]{:S(2)}) copy-start(bf16[64,2048]{1,0:T(8,128)(2,1)S(1)} %get-tuple-element.43) | copy-start | bytes 786436
  16.4 16.6 %all-to-all-start = ((bf16[16,64,128]{2,1,0:T(8,128)(2,1)}), bf16[16,64,128]{2,1,0:T(8,128)(2,1)S(1)}, u32[]{:S(2)}, u32[]{:S(2)}) async-start(bf16[16,64,128]{2,1,0:T(8,128)(2,1)} %broadcast_in_dim.8), calls=%async_computation | async-start | bytes 524288 | tf_op jit(solution)/shard_map/all_to_all | solution.py:166
  34.1 15.7 %all-to-all-start.1 = ((bf16[16,64,128]{2,1,0:T(8,128)(2,1)}), bf16[16,64,128]{2,1,0:T(8,128)(2,1)S(1)}, u32[]{:S(2)}, u32[]{:S(2)}) async-start(bf16[16,64,128]{2,1,0:T(8,128)(2,1)} %shard_map.68), calls=%async_computation.1 | async-start | bytes 524288 | tf_op jit(solution)/shard_map/all_to_all | solution.py:166
  37.7 47.1 %collective-permute-start.1 = (bf16[5,64,2048]{2,1,0:T(8,128)(2,1)}, bf16[5,64,2048]{2,1,0:T(8,128)(2,1)}, u32[]{:S(2)}, u32[]{:S(2)}) collective-permute-start(bf16[5,64,2048]{2,1,0:T(8,128)(2,1)} %param.7), channel_id=1, source_target_pairs={{0,1},{1,0},{2,3},{3,2},{4,5},{5,4},{6,7},{7,6},{8,9},{9,8},{10,11... | collective-permute-start | bytes 3932168 | tf_op jit(solution)/shard_map/ppermute | solution.py:156
  42.3 14.4 %copy-start.10 = (bf16[64,2048]{1,0:T(8,128)(2,1)S(1)}, bf16[64,2048]{1,0:T(8,128)(2,1)}, u32[]{:S(2)}) copy-start(bf16[64,2048]{1,0:T(8,128)(2,1)} %get-tuple-element.41) | copy-start | bytes 786436
  49.8 21.5 %copy-start = (bf16[16,64,128]{2,1,0:T(8,128)(2,1)}, bf16[16,64,128]{2,1,0:T(8,128)(2,1)S(1)}, u32[]{:S(2)}) copy-start(bf16[16,64,128]{2,1,0:T(8,128)(2,1)S(1)} %all-to-all-done.1.got_ref) | copy-start | bytes 786436
  50.8 14.3 %all-to-all-start.2 = ((bf16[16,64,128]{2,1,0:T(8,128)(2,1)}), bf16[16,64,128]{2,1,0:T(8,128)(2,1)S(1)}, u32[]{:S(2)}, u32[]{:S(2)}) async-start(bf16[16,64,128]{2,1,0:T(8,128)(2,1)} %shard_map.69), calls=%async_computation.2 | async-start | bytes 524288 | tf_op jit(solution)/shard_map/all_to_all | solution.py:166
  54.4 3.7 %copy-start.12 = (bf16[64,2048]{1,0:T(8,128)(2,1)S(1)}, bf16[64,2048]{1,0:T(8,128)(2,1)}, u32[]{:S(2)}) copy-start(bf16[64,2048]{1,0:T(8,128)(2,1)} %get-tuple-element.40) | copy-start | bytes 786436
  54.4 3.7 %copy-start.19 = (bf16[64,2048]{1,0:T(8,128)(2,1)S(1)}, bf16[64,2048]{1,0:T(8,128)(2,1)}, u32[]{:S(2)}) copy-start(bf16[64,2048]{1,0:T(8,128)(2,1)} %get-tuple-element.31) | copy-start | bytes 786436
  66.2 14.1 %all-to-all-start.3 = ((bf16[16,64,128]{2,1,0:T(8,128)(2,1)}), bf16[16,64,128]{2,1,0:T(8,128)(2,1)S(1)}, u32[]{:S(2)}, u32[]{:S(2)}) async-start(bf16[16,64,128]{2,1,0:T(8,128)(2,1)} %copy-done.4), calls=%async_computation.3 | async-start | bytes 524288 | tf_op jit(solution)/shard_map/all_to_all | solution.py:166
  80.2 4.6 %copy-start.1 = (bf16[16,64,128]{2,1,0:T(8,128)(2,1)}, bf16[16,64,128]{2,1,0:T(8,128)(2,1)S(1)}, u32[]{:S(2)}) copy-start(bf16[16,64,128]{2,1,0:T(8,128)(2,1)S(1)} %all-to-all-done.3.got_ref) | copy-start | bytes 786436
  81.3 14.0 %all-to-all-start.4 = ((bf16[16,64,128]{2,1,0:T(8,128)(2,1)}), bf16[16,64,128]{2,1,0:T(8,128)(2,1)S(1)}, u32[]{:S(2)}, u32[]{:S(2)}) async-start(bf16[16,64,128]{2,1,0:T(8,128)(2,1)} %copy-done.3), calls=%async_computation.4 | async-start | bytes 524288 | tf_op jit(solution)/shard_map/all_to_all | solution.py:166
  96.6 5.2 %copy-start.2 = (bf16[16,64,128]{2,1,0:T(8,128)(2,1)S(1)}, bf16[16,64,128]{2,1,0:T(8,128)(2,1)}, u32[]{:S(2)}) copy-start(bf16[16,64,128]{2,1,0:T(8,128)(2,1)} %copy-done.1) | copy-start | bytes 786436
  96.6 5.2 %copy-start.23 = (bf16[64,2048]{1,0:T(8,128)(2,1)S(1)}, bf16[64,2048]{1,0:T(8,128)(2,1)}, u32[]{:S(2)}) copy-start(bf16[64,2048]{1,0:T(8,128)(2,1)} %get-tuple-element.55) | copy-start | bytes 786436
  96.6 6.6 %copy-start.17 = (bf16[64,2048]{1,0:T(8,128)(2,1)S(1)}, bf16[64,2048]{1,0:T(8,128)(2,1)}, u32[]{:S(2)}) copy-start(bf16[64,2048]{1,0:T(8,128)(2,1)} %get-tuple-element.45) | copy-start | bytes 786436
  96.6 14.7 %all-to-all-start.5 = ((bf16[16,64,128]{2,1,0:T(8,128)(2,1)}), bf16[16,64,128]{2,1,0:T(8,128)(2,1)S(1)}, u32[]{:S(2)}, u32[]{:S(2)}) async-start(bf16[16,64,128]{2,1,0:T(8,128)(2,1)} %copy-done.6), calls=%async_computation.5 | async-start | bytes 524288 | tf_op jit(solution)/shard_map/all_to_all | solution.py:166
  103.2 14.9 %copy-start.14 = (bf16[64,2048]{1,0:T(8,128)(2,1)S(1)}, bf16[64,2048]{1,0:T(8,128)(2,1)}, u32[]{:S(2)}) copy-start(bf16[64,2048]{1,0:T(8,128)(2,1)} %get-tuple-element.37) | copy-start | bytes 786436
  103.5 16.0 %copy-start.13 = (bf16[64,2048]{1,0:T(8,128)(2,1)S(1)}, bf16[64,2048]{1,0:T(8,128)(2,1)}, u32[]{:S(2)}) copy-start(bf16[64,2048]{1,0:T(8,128)(2,1)} %get-tuple-element.40) | copy-start | bytes 786436
  112.3 14.3 %all-to-all-start.6 = ((bf16[16,64,128]{2,1,0:T(8,128)(2,1)}), bf16[16,64,128]{2,1,0:T(8,128)(2,1)S(1)}, u32[]{:S(2)}, u32[]{:S(2)}) async-start(bf16[16,64,128]{2,1,0:T(8,128)(2,1)} %get-tuple-element.12), calls=%async_computation.6 | async-start | bytes 524288 | tf_op jit(solution)/shard_map/all_to_all | solution.py:166
  118.2 13.0 %copy-start.11 = (bf16[64,2048]{1,0:T(8,128)(2,1)S(1)}, bf16[64,2048]{1,0:T(8,128)(2,1)}, u32[]{:S(2)}) copy-start(bf16[64,2048]{1,0:T(8,128)(2,1)} %get-tuple-element.41) | copy-start | bytes 786436
  119.5 13.2 %copy-start.9 = (bf16[64,2048]{1,0:T(8,128)(2,1)S(1)}, bf16[64,2048]{1,0:T(8,128)(2,1)}, u32[]{:S(2)}) copy-start(bf16[64,2048]{1,0:T(8,128)(2,1)} %copy-done.8) | copy-start | bytes 786436
  119.5 13.2 %copy-start.15 = (bf16[64,2048]{1,0:T(8,128)(2,1)S(1)}, bf16[64,2048]{1,0:T(8,128)(2,1)}, u32[]{:S(2)}) copy-start(bf16[64,2048]{1,0:T(8,128)(2,1)} %get-tuple-element.34) | copy-start | bytes 786436
  127.6 14.5 %all-to-all-start.7 = ((bf16[16,64,128]{2,1,0:T(8,128)(2,1)}), bf16[16,64,128]{2,1,0:T(8,128)(2,1)S(1)}, u32[]{:S(2)}, u32[]{:S(2)}) async-start(bf16[16,64,128]{2,1,0:T(8,128)(2,1)} %get-tuple-element.14), calls=%async_computation.7 | async-start | bytes 524288 | tf_op jit(solution)/shard_map/all_to_all | solution.py:166
  131.2 15.5 %copy-start.18 = (bf16[64,2048]{1,0:T(8,128)(2,1)S(1)}, bf16[64,2048]{1,0:T(8,128)(2,1)}, u32[]{:S(2)}) copy-start(bf16[64,2048]{1,0:T(8,128)(2,1)} %get-tuple-element.54) | copy-start | bytes 786436
  131.2 15.5 %copy-start.22 = (bf16[64,2048]{1,0:T(8,128)(2,1)S(1)}, bf16[64,2048]{1,0:T(8,128)(2,1)}, u32[]{:S(2)}) copy-start(bf16[64,2048]{1,0:T(8,128)(2,1)} %get-tuple-element.50) | copy-start | bytes 786436
  143.1 14.3 %all-to-all-start.8 = ((bf16[16,64,128]{2,1,0:T(8,128)(2,1)}), bf16[16,64,128]{2,1,0:T(8,128)(2,1)S(1)}, u32[]{:S(2)}, u32[]{:S(2)}) async-start(bf16[16,64,128]{2,1,0:T(8,128)(2,1)} %get-tuple-element.16), calls=%async_computation.8 | async-start | bytes 524288 | tf_op jit(solution)/shard_map/all_to_all | solution.py:166
  146.7 43.5 %copy-start.5 = (s32[16,1024,4]{1,2,0:T(4,128)S(1)}, s32[16,1024,4]{1,2,0:T(4,128)}, u32[]{:S(2)}) copy-start(s32[16,1024,4]{1,2,0:T(4,128)} %param.8) | copy-start | bytes 786436
  146.7 43.5 %copy-start.7 = (f32[16,1024]{1,0:T(8,128)S(1)}, f32[16,1024]{1,0:T(8,128)}, u32[]{:S(2)}) copy-start(f32[16,1024]{1,0:T(8,128)} %weights_ref.1) | copy-start | bytes 196612
  157.7 13.6 %collective-permute-start.3 = (f32[5,64,64]{2,1,0:T(8,128)S(1)}, f32[5,64,64]{2,1,0:T(8,128)S(1)}, u32[]{:S(2)}, u32[]{:S(2)}) collective-permute-start(f32[5,64,64]{2,1,0:T(8,128)S(1)} %get-tuple-element.56), channel_id=1, source_target_pairs={{0,1},{1,0},{2,3},{3,2},{4,5},{5,4},{6,7},{7,6},{8,9},{9,8},{10,11... | collective-permute-start | bytes 245768 | tf_op jit(solution)/shard_map/ppermute | solution.py:156
  172.2 18.0 %all-to-all-start.9 = ((bf16[16,20,128]{2,1,0:T(8,128)(2,1)}), bf16[16,20,128]{2,1,0:T(8,128)(2,1)S(1)}, u32[]{:S(2)}, u32[]{:S(2)}) async-start(bf16[16,20,128]{2,1,0:T(8,128)(2,1)} %copy.29), calls=%async_computation.9 | async-start | bytes 196608 | tf_op jit(solution)/shard_map/all_to_all | solution.py:239
  (7 other events, 13.5 us)

commit v5 on v4

--- a/solution.py
+++ b/solution.py
@@ -126,7 +126,7 @@
             total = total + product * weights_ref[pl.ds(at, 1), start : start + span]
         return jnp.where(lane == at, jnp.sum(total, axis=1, keepdims=True), result)
 
-    result = lax.fori_loop(0, frames, frame, jnp.zeros((lines, 128), F32), unroll=2)
+    result = lax.fori_loop(0, frames, frame, jnp.zeros((lines, 128), F32), unroll=8)
     for panel in range(panels):
         out_ref[panel] = result[panel * nodes : (panel + 1) * nodes, :frames]
 
@@ -181,6 +181,9 @@
     other_coupling = swap(coupling)
     other_inverse = swap(block_inverse)
 
+    message = jnp.broadcast_to(rhs[0][None], (chips,) + rhs[0].shape)
+    message, coupling = lax.optimization_barrier((message, coupling))
+
     def factor(later, earlier):
         at = pair_index(later, earlier)
         return in_order(coupling[at], other_coupling[at], 0)
@@ -197,7 +200,6 @@
         return [coupling[at], other_coupling[at]]
 
     place = core.reshape(1)
-    message = jnp.broadcast_to(rhs[0][None], (chips,) + rhs[0].shape)
     full = []
     for panel in range(panels):
         got = exchange(message)

time: 201 us -> 198 us (0.985)
    all_to_all x9, waiting for transfers between devices: 71 us -> 68.2 us  [exchange(): lax.all_to_all(blocks, 'row', split_axis=0, concat_axis=0, tiled=True, ax...]
  transfers between devices with their start and end apart: 14 -> 14, of which waited for: 11 -> 12; matrix products, arithmetic and copies ran while one was open for 16% -> 16% of each run, Pallas kernels for 1% -> 1%
where the time goes in v5:
time: 198 us; the launch traced here: 196 us
  waiting for transfers between devices  77.1 us (39%)
  starting transfers between devices  69.5 us (35%)
  matrix products  17.7 us (9%)
  local copies, waits for them, and re-layouts  16.3 us (8%)
  Pallas kernels  14.2 us (7%)
    all_to_all x9, waiting for transfers between devices, exchange(): lax.all_to_all(blocks, 'row', split_axis=0, concat_axis=0, tiled=True, ax...  68.2 us
    all_to_all x9, starting transfers between devices, exchange(): lax.all_to_all(blocks, 'row', split_axis=0, concat_axis=0, tiled=True, ax...  32.5 us
    ppermute x4, starting transfers between devices, swap(): return lax.ppermute(value, 'row', pairs)  26.7 us
    dot_general x16, matrix products, dot(): lax.dot_general(left, right, (((left_dim,), (right_dim,)), ((), ())), pre...  17.7 us
    all_to_all x1, starting transfers between devices, shards(): lax.all_to_all(table, 'src', split_axis=0, concat_axis=0, tiled=True)  10.3 us
    pallas_call x1, Pallas kernels, weigh(): pl.pallas_call(weigh_kernel, out_shape=jax.ShapeDtypeStruct((panels, tabl...  7.81 us
    all_to_all x1, waiting for transfers between devices, shards(): lax.all_to_all(table, 'src', split_axis=0, concat_axis=0, tiled=True)  6.57 us
    pallas_call x8, Pallas kernels, call(): pl.pallas_call(kernel, out_shape=(out, x) if solved else out, in_specs=[S...  6.36 us
  transfers between devices with their start and end apart: 14, of which 12 were waited for; matrix products, arithmetic and copies ran while one was open for 16% of the time, Pallas kernels for 1%

profile of v5, /device:TPU:1, one launch (start us, length us, event | category | flops | bytes accessed | tf_op | source)
XLA Modules:
  0.0 196.3 jit_solution(5735522280694491037)
XLA Ops:
  0.6 8.8 %collective-permute-start.2 = (bf16[10,64,2048]{2,1,0:T(8,128)(2,1)}, bf16[10,64,2048]{2,1,0:T(8,128)(2,1)}, u32[]{:S(2)}, u32[]{:S(2)}) collective-permute-start(bf16[10,64,2048]{2,1,0:T(8,128)(2,1)} %param.6), channel_id=1, source_target_pairs={{0,1},{1,0},{2,3},{3,2},{4,5},{5,4},{6,7},{7,6},{8,9},{9,8},{10,11... | collective-permute-start | bytes 7864328 | tf_op jit(solution)/shard_map/ppermute | solution.py:156
  10.7 1.9 collective-permute-start
  14.9 4.0 %all-to-all-start = ((bf16[16,64,128]{2,1,0:T(8,128)(2,1)}), bf16[16,64,128]{2,1,0:T(8,128)(2,1)S(1)}, u32[]{:S(2)}, u32[]{:S(2)}) async-start(bf16[16,64,128]{2,1,0:T(8,128)(2,1)} %broadcast_in_dim.8), calls=%async_computation | async-start | bytes 524288 | tf_op jit(solution)/shard_map/all_to_all | solution.py:166
  19.0 2.8 %slice_bitcast_fusion.16 = (bf16[64,2048]{1,0:T(8,128)(2,1)S(1)}, bf16[64,2048]{1,0:T(8,128)(2,1)}, bf16[64,2048]{1,0:T(8,128)(2,1)}, bf16[64,2048]{1,0:T(8,128)...) fusion(bf16[10,64,2048]{2,1,0:T(8,128)(2,1)} %param.6), kind=kLoop, calls=%fused_computation.77 | loop fusion | bytes 5242880 | tf_op jit(solution)/shard_map/squeeze | solution.py:200
  21.8 2.9 %slice_bitcast_fusion.1 = (bf16[64,2048]{1,0:T(8,128)(2,1)S(1)}, bf16[64,2048]{1,0:T(8,128)(2,1)}, bf16[64,2048]{1,0:T(8,128)(2,1)}, bf16[64,2048]{1,0:T(8,128)(...) fusion(bf16[10,64,2048]{2,1,0:T(8,128)(2,1)} %collective-permut, ...), kind=kLoop, calls=%fused_computation.62 | loop fusion | bytes 5242880 | tf_op jit(solution)/shard_map/squeeze | solution.py:200
  24.7 6.9 %all-to-all-done.got_ref = bf16[16,64,128]{2,1,0:T(8,128)(2,1)S(1)} async-done(((bf16[16,64,128]{2,1,0:T(8,128)(2,1)}), bf16[16,64,128]{2,1,0:T(8,128)(2,1)S(1)}, u32[]{:S(2)}, u32[]{:S(2)}) %all-to-all-start) | async-done | bytes 262176 | tf_op jit(solution)/shard_map/all_to_all | solution.py:166
  32.7 3.6 %all-to-all-start.1 = ((bf16[16,64,128]{2,1,0:T(8,128)(2,1)}), bf16[16,64,128]{2,1,0:T(8,128)(2,1)S(1)}, u32[]{:S(2)}, u32[]{:S(2)}) async-start(bf16[16,64,128]{2,1,0:T(8,128)(2,1)} %shard_map.68), calls=%async_computation.1 | async-start | bytes 524288 | tf_op jit(solution)/shard_map/all_to_all | solution.py:166
  36.2 3.2 %collective-permute-start.1 = (bf16[5,64,2048]{2,1,0:T(8,128)(2,1)}, bf16[5,64,2048]{2,1,0:T(8,128)(2,1)}, u32[]{:S(2)}, u32[]{:S(2)}) collective-permute-start(bf16[5,64,2048]{2,1,0:T(8,128)(2,1)} %param.7), channel_id=1, source_target_pairs={{0,1},{1,0},{2,3},{3,2},{4,5},{5,4},{6,7},{7,6},{8,9},{9,8},{10,11... | collective-permute-start | bytes 3932168 | tf_op jit(solution)/shard_map/ppermute | solution.py:156
  40.8 7.4 %all-to-all-done.1.got_ref = bf16[16,64,128]{2,1,0:T(8,128)(2,1)S(1)} async-done(((bf16[16,64,128]{2,1,0:T(8,128)(2,1)}), bf16[16,64,128]{2,1,0:T(8,128)(2,1)S(1)}, u32[]{:S(2)}, u32[]{:S(2)}) %all-to-all-start.1) | async-done | bytes 262176 | tf_op jit(solution)/shard_map/all_to_all | solution.py:166
  49.3 3.5 %all-to-all-start.2 = ((bf16[16,64,128]{2,1,0:T(8,128)(2,1)}), bf16[16,64,128]{2,1,0:T(8,128)(2,1)S(1)}, u32[]{:S(2)}, u32[]{:S(2)}) async-start(bf16[16,64,128]{2,1,0:T(8,128)(2,1)} %shard_map.69), calls=%async_computation.2 | async-start | bytes 524288 | tf_op jit(solution)/shard_map/all_to_all | solution.py:166
  52.9 2.3 %slice_bitcast_fusion.15 = (bf16[64,2048]{1,0:T(8,128)(2,1)S(1)}, bf16[64,2048]{1,0:T(8,128)(2,1)}, bf16[64,2048]{1,0:T(8,128)(2,1)}, bf16[64,2048]{1,0:T(8,128)(2,1)}, bf16[64,2048]{1,0:T(8,128)(2,1)}) fusion(bf16[5,64,2048]{2,1,0:T(8,128)(2,1)} %param.7), kind=kLoop, calls=%fused_computation.76 | loop fusion | bytes 2621440 | tf_op jit(solution)/shard_map/squeeze | solution.py:220
  56.9 6.7 %all-to-all-done.2.got_ref = bf16[16,64,128]{2,1,0:T(8,128)(2,1)S(1)} async-done(((bf16[16,64,128]{2,1,0:T(8,128)(2,1)}), bf16[16,64,128]{2,1,0:T(8,128)(2,1)S(1)}, u32[]{:S(2)}, u32[]{:S(2)}) %all-to-all-start.2) | async-done | bytes 262176 | tf_op jit(solution)/shard_map/all_to_all | solution.py:166
  64.7 3.5 %all-to-all-start.3 = ((bf16[16,64,128]{2,1,0:T(8,128)(2,1)}), bf16[16,64,128]{2,1,0:T(8,128)(2,1)S(1)}, u32[]{:S(2)}, u32[]{:S(2)}) async-start(bf16[16,64,128]{2,1,0:T(8,128)(2,1)} %copy-done.4), calls=%async_computation.3 | async-start | bytes 524288 | tf_op jit(solution)/shard_map/all_to_all | solution.py:166
  68.2 1.5 convolution_subtract_fusion.2
  71.6 7.1 %all-to-all-done.3.got_ref = bf16[16,64,128]{2,1,0:T(8,128)(2,1)S(1)} async-done(((bf16[16,64,128]{2,1,0:T(8,128)(2,1)}), bf16[16,64,128]{2,1,0:T(8,128)(2,1)S(1)}, u32[]{:S(2)}, u32[]{:S(2)}) %all-to-all-start.3) | async-done | bytes 262176 | tf_op jit(solution)/shard_map/all_to_all | solution.py:166
  79.8 3.5 %all-to-all-start.4 = ((bf16[16,64,128]{2,1,0:T(8,128)(2,1)}), bf16[16,64,128]{2,1,0:T(8,128)(2,1)S(1)}, u32[]{:S(2)}, u32[]{:S(2)}) async-start(bf16[16,64,128]{2,1,0:T(8,128)(2,1)} %copy-done.3), calls=%async_computation.4 | async-start | bytes 524288 | tf_op jit(solution)/shard_map/all_to_all | solution.py:166
  83.4 2.2 %slice_bitcast_fusion = (bf16[64,2048]{1,0:T(8,128)(2,1)S(1)}, bf16[64,2048]{1,0:T(8,128)(2,1)}, bf16[64,2048]{1,0:T(8,128)(2,1)}, bf16[64,2048]{1,0:T(8,128)(2,1)S(1)}, bf16[64,2048]{1,0:T(8,128)(2,1)}) fusion(bf16[5,64,2048]{2,1,0:T(8,128)(2,1)} %collective-permute-done.1), kind=kLoop, calls=%fused_computation.61 | loop fusion | bytes 2621440 | tf_op jit(solution)/shard_map/squeeze | solution.py:220
  86.9 6.9 %all-to-all-done.4.got_ref = bf16[16,64,128]{2,1,0:T(8,128)(2,1)S(1)} async-done(((bf16[16,64,128]{2,1,0:T(8,128)(2,1)}), bf16[16,64,128]{2,1,0:T(8,128)(2,1)S(1)}, u32[]{:S(2)}, u32[]{:S(2)}) %all-to-all-start.4) | async-done | bytes 262176 | tf_op jit(solution)/shard_map/all_to_all | solution.py:166
  95.1 3.7 %all-to-all-start.5 = ((bf16[16,64,128]{2,1,0:T(8,128)(2,1)}), bf16[16,64,128]{2,1,0:T(8,128)(2,1)S(1)}, u32[]{:S(2)}, u32[]{:S(2)}) async-start(bf16[16,64,128]{2,1,0:T(8,128)(2,1)} %copy-done.6), calls=%async_computation.5 | async-start | bytes 524288 | tf_op jit(solution)/shard_map/all_to_all | solution.py:166
  102.1 7.9 %all-to-all-done.5.got_ref = bf16[16,64,128]{2,1,0:T(8,128)(2,1)S(1)} async-done(((bf16[16,64,128]{2,1,0:T(8,128)(2,1)}), bf16[16,64,128]{2,1,0:T(8,128)(2,1)S(1)}, u32[]{:S(2)}, u32[]{:S(2)}) %all-to-all-start.5) | async-done | bytes 262176 | tf_op jit(solution)/shard_map/all_to_all | solution.py:166
  111.0 3.5 %all-to-all-start.6 = ((bf16[16,64,128]{2,1,0:T(8,128)(2,1)}), bf16[16,64,128]{2,1,0:T(8,128)(2,1)S(1)}, u32[]{:S(2)}, u32[]{:S(2)}) async-start(bf16[16,64,128]{2,1,0:T(8,128)(2,1)} %get-tuple-element.16), calls=%async_computation.6 | async-start | bytes 524288 | tf_op jit(solution)/shard_map/all_to_all | solution.py:166
  114.5 2.1 %fusion.51 = f32[64,2048]{1,0:T(8,128)} fusion(bf16[64,2048]{1,0:T(8,128)(2,1)} %get-tuple-element.33, bf16[64,2048]{1,0:T(8,128)(2,1)S(1)} %copy-done.17, pred[]{:T(512)S(6)} %eq.4, f32[64,128]{1,0:T(8,128)S(1)} %get-tuple-element.15), kind=kOutput, calls=%fused_computation.102 | convolution fusion | flops 35921920 | bytes 1081345 | tf_op jit(solution)/shard_map/dot_general | solution.py:17
  118.0 1.6 convolution_add_fusion.2.part_ref
  119.6 5.4 %all-to-all-done.6.got_ref = bf16[16,64,128]{2,1,0:T(8,128)(2,1)S(1)} async-done(((bf16[16,64,128]{2,1,0:T(8,128)(2,1)}), bf16[16,64,128]{2,1,0:T(8,128)(2,1)S(1)}, u32[]{:S(2)}, u32[]{:S(2)}) %all-to-all-start.6) | async-done | bytes 262176 | tf_op jit(solution)/shard_map/all_to_all | solution.py:166
  126.0 3.6 %all-to-all-start.7 = ((bf16[16,64,128]{2,1,0:T(8,128)(2,1)}), bf16[16,64,128]{2,1,0:T(8,128)(2,1)S(1)}, u32[]{:S(2)}, u32[]{:S(2)}) async-start(bf16[16,64,128]{2,1,0:T(8,128)(2,1)} %get-tuple-element.18), calls=%async_computation.7 | async-start | bytes 524288 | tf_op jit(solution)/shard_map/all_to_all | solution.py:166
  131.2 9.1 %all-to-all-done.7.got_ref = bf16[16,64,128]{2,1,0:T(8,128)(2,1)S(1)} async-done(((bf16[16,64,128]{2,1,0:T(8,128)(2,1)}), bf16[16,64,128]{2,1,0:T(8,128)(2,1)S(1)}, u32[]{:S(2)}, u32[]{:S(2)}) %all-to-all-start.7) | async-done | bytes 262176 | tf_op jit(solution)/shard_map/all_to_all | solution.py:166
  141.4 3.5 %all-to-all-start.8 = ((bf16[16,64,128]{2,1,0:T(8,128)(2,1)}), bf16[16,64,128]{2,1,0:T(8,128)(2,1)S(1)}, u32[]{:S(2)}, u32[]{:S(2)}) async-start(bf16[16,64,128]{2,1,0:T(8,128)(2,1)} %get-tuple-element.20), calls=%async_computation.8 | async-start | bytes 524288 | tf_op jit(solution)/shard_map/all_to_all | solution.py:166
  145.2 10.6 %all-to-all-done.8 = bf16[16,64,128]{2,1,0:T(8,128)(2,1)S(1)} async-done(((bf16[16,64,128]{2,1,0:T(8,128)(2,1)}), bf16[16,64,128]{2,1,0:T(8,128)(2,1)S(1)}, u32[]{:S(2)}, u32[]{:S(2)}) %all-to-all-start.8) | async-done | bytes 262176 | tf_op jit(solution)/shard_map/all_to_all | solution.py:166
  156.1 12.7 %collective-permute-start.3 = (f32[5,64,64]{2,1,0:T(8,128)S(1)}, f32[5,64,64]{2,1,0:T(8,128)S(1)}, u32[]{:S(2)}, u32[]{:S(2)}) collective-permute-start(f32[5,64,64]{2,1,0:T(8,128)S(1)} %get-tuple-element.60), channel_id=1, source_target_pairs={{0,1},{1,0},{2,3},{3,2},{4,5},{5,4},{6,7},{7,6},{8,9},{9,8},{10,11... | collective-permute-start | bytes 245768 | tf_op jit(solution)/shard_map/ppermute | solution.py:156
  170.8 10.3 %all-to-all-start.9 = ((bf16[16,20,128]{2,1,0:T(8,128)(2,1)}), bf16[16,20,128]{2,1,0:T(8,128)(2,1)S(1)}, u32[]{:S(2)}, u32[]{:S(2)}) async-start(bf16[16,20,128]{2,1,0:T(8,128)(2,1)} %copy.29), calls=%async_computation.9 | async-start | bytes 196608 | tf_op jit(solution)/shard_map/all_to_all | solution.py:241
  181.9 6.6 %all-to-all-done.9.table_ref = bf16[16,20,128]{2,1,0:T(8,128)(2,1)S(1)} async-done(((bf16[16,20,128]{2,1,0:T(8,128)(2,1)}), bf16[16,20,128]{2,1,0:T(8,128)(2,1)S(1)}, u32[]{:S(2)}, u32[]{:S(2)}) %all-to-all-start.9) | async-done | bytes 81952 | tf_op jit(solution)/shard_map/all_to_all | solution.py:241
  188.5 7.8 %shard_map.76 = f32[5,4,16]{2,1,0:T(4,128)} custom-call(bf16[16,20,128]{2,1,0:T(8,128)(2,1)S(1)} %all-to-all-done.9.table_ref, s32[16,4,1024]{2,1,0:T(4,128)S(1)} %bitcast.166, f32[16,1024]{1,0:T(8,128)S(1)} %copy-done.7), custom_call_target="tpu_custom_call" | custom-call | tf_op jit(solution)/shard_map/pallas_call | solution.py:135
  (95 shorter events, 27.5 us)
Async XLA Ops:
  0.6 21.1 %collective-permute-start.2 = (bf16[10,64,2048]{2,1,0:T(8,128)(2,1)}, bf16[10,64,2048]{2,1,0:T(8,128)(2,1)}, u32[]{:S(2)}, u32[]{:S(2)}) collective-permute-start(bf16[10,64,2048]{2,1,0:T(8,128)(2,1)} %param.6), channel_id=1, source_target_pairs={{0,1},{1,0},{2,3},{3,2},{4,5},{5,4},{6,7},{7,6},{8,9},{9,8},{10,11... | collective-permute-start | bytes 7864328 | tf_op jit(solution)/shard_map/ppermute | solution.py:156
  10.7 3.4 %collective-permute-start = (bf16[5,64,64]{2,1,0:T(8,128)(2,1)S(1)}, bf16[5,64,64]{2,1,0:T(8,128)(2,1)S(1)}, u32[]{:S(2)}, u32[]{:S(2)}) collective-permute-start(bf16[5,64,64]{2,1,0:T(8,128)(2,1)S(1)} %bitcast.170), channel_id=1, source_target_pairs={{0,1},{1,0},{2,3},{3,2},{4,5},{5,4},{6,7},{7,6},{8,9},{9,8},{10,11... | collective-permute-start | bytes 122888 | tf_op jit(solution)/shard_map/ppermute | solution.py:156
  14.9 16.7 %all-to-all-start = ((bf16[16,64,128]{2,1,0:T(8,128)(2,1)}), bf16[16,64,128]{2,1,0:T(8,128)(2,1)S(1)}, u32[]{:S(2)}, u32[]{:S(2)}) async-start(bf16[16,64,128]{2,1,0:T(8,128)(2,1)} %broadcast_in_dim.8), calls=%async_computation | async-start | bytes 524288 | tf_op jit(solution)/shard_map/all_to_all | solution.py:166
  21.7 17.7 %copy-start.8 = (bf16[64,2048]{1,0:T(8,128)(2,1)}, bf16[64,2048]{1,0:T(8,128)(2,1)S(1)}, u32[]{:S(2)}) copy-start(bf16[64,2048]{1,0:T(8,128)(2,1)S(1)} %get-tuple-element.48) | copy-start | bytes 786436
  32.7 15.6 %all-to-all-start.1 = ((bf16[16,64,128]{2,1,0:T(8,128)(2,1)}), bf16[16,64,128]{2,1,0:T(8,128)(2,1)S(1)}, u32[]{:S(2)}, u32[]{:S(2)}) async-start(bf16[16,64,128]{2,1,0:T(8,128)(2,1)} %shard_map.68), calls=%async_computation.1 | async-start | bytes 524288 | tf_op jit(solution)/shard_map/all_to_all | solution.py:166
  36.2 47.1 %collective-permute-start.1 = (bf16[5,64,2048]{2,1,0:T(8,128)(2,1)}, bf16[5,64,2048]{2,1,0:T(8,128)(2,1)}, u32[]{:S(2)}, u32[]{:S(2)}) collective-permute-start(bf16[5,64,2048]{2,1,0:T(8,128)(2,1)} %param.7), channel_id=1, source_target_pairs={{0,1},{1,0},{2,3},{3,2},{4,5},{5,4},{6,7},{7,6},{8,9},{9,8},{10,11... | collective-permute-start | bytes 3932168 | tf_op jit(solution)/shard_map/ppermute | solution.py:156
  40.8 14.4 %copy-start.10 = (bf16[64,2048]{1,0:T(8,128)(2,1)S(1)}, bf16[64,2048]{1,0:T(8,128)(2,1)}, u32[]{:S(2)}) copy-start(bf16[64,2048]{1,0:T(8,128)(2,1)} %get-tuple-element.46) | copy-start | bytes 786436
  48.3 21.5 %copy-start = (bf16[16,64,128]{2,1,0:T(8,128)(2,1)}, bf16[16,64,128]{2,1,0:T(8,128)(2,1)S(1)}, u32[]{:S(2)}) copy-start(bf16[16,64,128]{2,1,0:T(8,128)(2,1)S(1)} %all-to-all-done.1.got_ref) | copy-start | bytes 786436
  49.3 14.3 %all-to-all-start.2 = ((bf16[16,64,128]{2,1,0:T(8,128)(2,1)}), bf16[16,64,128]{2,1,0:T(8,128)(2,1)S(1)}, u32[]{:S(2)}, u32[]{:S(2)}) async-start(bf16[16,64,128]{2,1,0:T(8,128)(2,1)} %shard_map.69), calls=%async_computation.2 | async-start | bytes 524288 | tf_op jit(solution)/shard_map/all_to_all | solution.py:166
  52.9 3.7 %copy-start.14 = (bf16[64,2048]{1,0:T(8,128)(2,1)S(1)}, bf16[64,2048]{1,0:T(8,128)(2,1)}, u32[]{:S(2)}) copy-start(bf16[64,2048]{1,0:T(8,128)(2,1)} %get-tuple-element.45) | copy-start | bytes 786436
  52.9 3.7 %copy-start.18 = (bf16[64,2048]{1,0:T(8,128)(2,1)S(1)}, bf16[64,2048]{1,0:T(8,128)(2,1)}, u32[]{:S(2)}) copy-start(bf16[64,2048]{1,0:T(8,128)(2,1)} %get-tuple-element.35) | copy-start | bytes 786436
  64.7 14.1 %all-to-all-start.3 = ((bf16[16,64,128]{2,1,0:T(8,128)(2,1)}), bf16[16,64,128]{2,1,0:T(8,128)(2,1)S(1)}, u32[]{:S(2)}, u32[]{:S(2)}) async-start(bf16[16,64,128]{2,1,0:T(8,128)(2,1)} %copy-done.4), calls=%async_computation.3 | async-start | bytes 524288 | tf_op jit(solution)/shard_map/all_to_all | solution.py:166
  78.7 4.6 %copy-start.1 = (bf16[16,64,128]{2,1,0:T(8,128)(2,1)}, bf16[16,64,128]{2,1,0:T(8,128)(2,1)S(1)}, u32[]{:S(2)}) copy-start(bf16[16,64,128]{2,1,0:T(8,128)(2,1)S(1)} %all-to-all-done.3.got_ref) | copy-start | bytes 786436
  79.8 14.0 %all-to-all-start.4 = ((bf16[16,64,128]{2,1,0:T(8,128)(2,1)}), bf16[16,64,128]{2,1,0:T(8,128)(2,1)S(1)}, u32[]{:S(2)}, u32[]{:S(2)}) async-start(bf16[16,64,128]{2,1,0:T(8,128)(2,1)} %copy-done.3), calls=%async_computation.4 | async-start | bytes 524288 | tf_op jit(solution)/shard_map/all_to_all | solution.py:166
  95.1 5.3 %copy-start.2 = (bf16[16,64,128]{2,1,0:T(8,128)(2,1)S(1)}, bf16[16,64,128]{2,1,0:T(8,128)(2,1)}, u32[]{:S(2)}) copy-start(bf16[16,64,128]{2,1,0:T(8,128)(2,1)} %copy-done.1) | copy-start | bytes 786436
  95.1 5.3 %copy-start.24 = (bf16[64,2048]{1,0:T(8,128)(2,1)S(1)}, bf16[64,2048]{1,0:T(8,128)(2,1)}, u32[]{:S(2)}) copy-start(bf16[64,2048]{1,0:T(8,128)(2,1)} %get-tuple-element.59) | copy-start | bytes 786436
  95.1 14.8 %all-to-all-start.5 = ((bf16[16,64,128]{2,1,0:T(8,128)(2,1)}), bf16[16,64,128]{2,1,0:T(8,128)(2,1)S(1)}, u32[]{:S(2)}, u32[]{:S(2)}) async-start(bf16[16,64,128]{2,1,0:T(8,128)(2,1)} %copy-done.6), calls=%async_computation.5 | async-start | bytes 524288 | tf_op jit(solution)/shard_map/all_to_all | solution.py:166
  100.4 14.1 %copy-start.17 = (bf16[64,2048]{1,0:T(8,128)(2,1)S(1)}, bf16[64,2048]{1,0:T(8,128)(2,1)}, u32[]{:S(2)}) copy-start(bf16[64,2048]{1,0:T(8,128)(2,1)} %get-tuple-element.43) | copy-start | bytes 786436
  101.8 14.8 %copy-start.16 = (bf16[64,2048]{1,0:T(8,128)(2,1)S(1)}, bf16[64,2048]{1,0:T(8,128)(2,1)}, u32[]{:S(2)}) copy-start(bf16[64,2048]{1,0:T(8,128)(2,1)} %get-tuple-element.42) | copy-start | bytes 786436
  111.0 14.0 %all-to-all-start.6 = ((bf16[16,64,128]{2,1,0:T(8,128)(2,1)}), bf16[16,64,128]{2,1,0:T(8,128)(2,1)S(1)}, u32[]{:S(2)}, u32[]{:S(2)}) async-start(bf16[16,64,128]{2,1,0:T(8,128)(2,1)} %get-tuple-element.16), calls=%async_computation.6 | async-start | bytes 524288 | tf_op jit(solution)/shard_map/all_to_all | solution.py:166
  116.6 13.0 %copy-start.11 = (bf16[64,2048]{1,0:T(8,128)(2,1)S(1)}, bf16[64,2048]{1,0:T(8,128)(2,1)}, u32[]{:S(2)}) copy-start(bf16[64,2048]{1,0:T(8,128)(2,1)} %get-tuple-element.46) | copy-start | bytes 786436
  116.6 13.0 %copy-start.13 = (bf16[64,2048]{1,0:T(8,128)(2,1)S(1)}, bf16[64,2048]{1,0:T(8,128)(2,1)}, u32[]{:S(2)}) copy-start(bf16[64,2048]{1,0:T(8,128)(2,1)} %get-tuple-element.36) | copy-start | bytes 786436
  118.0 13.0 %copy-start.9 = (bf16[64,2048]{1,0:T(8,128)(2,1)S(1)}, bf16[64,2048]{1,0:T(8,128)(2,1)}, u32[]{:S(2)}) copy-start(bf16[64,2048]{1,0:T(8,128)(2,1)} %copy-done.8) | copy-start | bytes 786436
  118.0 13.0 %copy-start.12 = (bf16[64,2048]{1,0:T(8,128)(2,1)S(1)}, bf16[64,2048]{1,0:T(8,128)(2,1)}, u32[]{:S(2)}) copy-start(bf16[64,2048]{1,0:T(8,128)(2,1)} %get-tuple-element.38) | copy-start | bytes 786436
  126.0 14.4 %all-to-all-start.7 = ((bf16[16,64,128]{2,1,0:T(8,128)(2,1)}), bf16[16,64,128]{2,1,0:T(8,128)(2,1)S(1)}, u32[]{:S(2)}, u32[]{:S(2)}) async-start(bf16[16,64,128]{2,1,0:T(8,128)(2,1)} %get-tuple-element.18), calls=%async_computation.7 | async-start | bytes 524288 | tf_op jit(solution)/shard_map/all_to_all | solution.py:166
  129.6 15.3 %copy-start.15 = (bf16[64,2048]{1,0:T(8,128)(2,1)S(1)}, bf16[64,2048]{1,0:T(8,128)(2,1)}, u32[]{:S(2)}) copy-start(bf16[64,2048]{1,0:T(8,128)(2,1)} %get-tuple-element.58) | copy-start | bytes 786436
  129.6 15.3 %copy-start.23 = (bf16[64,2048]{1,0:T(8,128)(2,1)S(1)}, bf16[64,2048]{1,0:T(8,128)(2,1)}, u32[]{:S(2)}) copy-start(bf16[64,2048]{1,0:T(8,128)(2,1)} %get-tuple-element.54) | copy-start | bytes 786436
  141.4 14.5 %all-to-all-start.8 = ((bf16[16,64,128]{2,1,0:T(8,128)(2,1)}), bf16[16,64,128]{2,1,0:T(8,128)(2,1)S(1)}, u32[]{:S(2)}, u32[]{:S(2)}) async-start(bf16[16,64,128]{2,1,0:T(8,128)(2,1)} %get-tuple-element.20), calls=%async_computation.8 | async-start | bytes 524288 | tf_op jit(solution)/shard_map/all_to_all | solution.py:166
  144.9 43.6 %copy-start.5 = (s32[16,1024,4]{1,2,0:T(4,128)S(1)}, s32[16,1024,4]{1,2,0:T(4,128)}, u32[]{:S(2)}) copy-start(s32[16,1024,4]{1,2,0:T(4,128)} %param.8) | copy-start | bytes 786436
  144.9 43.6 %copy-start.7 = (f32[16,1024]{1,0:T(8,128)S(1)}, f32[16,1024]{1,0:T(8,128)}, u32[]{:S(2)}) copy-start(f32[16,1024]{1,0:T(8,128)} %weights_ref.1) | copy-start | bytes 196612
  156.1 13.8 %collective-permute-start.3 = (f32[5,64,64]{2,1,0:T(8,128)S(1)}, f32[5,64,64]{2,1,0:T(8,128)S(1)}, u32[]{:S(2)}, u32[]{:S(2)}) collective-permute-start(f32[5,64,64]{2,1,0:T(8,128)S(1)} %get-tuple-element.60), channel_id=1, source_target_pairs={{0,1},{1,0},{2,3},{3,2},{4,5},{5,4},{6,7},{7,6},{8,9},{9,8},{10,11... | collective-permute-start | bytes 245768 | tf_op jit(solution)/shard_map/ppermute | solution.py:156
  170.8 17.7 %all-to-all-start.9 = ((bf16[16,20,128]{2,1,0:T(8,128)(2,1)}), bf16[16,20,128]{2,1,0:T(8,128)(2,1)S(1)}, u32[]{:S(2)}, u32[]{:S(2)}) async-start(bf16[16,20,128]{2,1,0:T(8,128)(2,1)} %copy.29), calls=%async_computation.9 | async-start | bytes 196608 | tf_op jit(solution)/shard_map/all_to_all | solution.py:241
  (8 other events, 16.5 us)

commit v6 on v5

--- a/solution.py
+++ b/solution.py
@@ -116,7 +116,7 @@
                 low = (index & (depth - 1)).astype(jnp.int16)
                 hot = jnp.where(places == low, jnp.ones((), BF), jnp.zeros((), BF))
                 found = dot(table, hot, 1, 0)
-                part = index // depth
+                part = index >> (depth.bit_length() - 1)
                 value = found[:lines]
                 for other in range(1, parts):
                     piece = found[other * lines : (other + 1) * lines]
@@ -221,6 +221,8 @@
     message, solved[last] = call(turn_kernel, place, operands, got, True, True)
     for panel in reversed(range(last)):
         rounded[panel + 1] = solved[panel + 1].astype(BF)
+        if panel == 0:
+            message, totals[0] = lax.optimization_barrier((message, totals[0]))
         got = exchange(message)
         if panel:
             part = dot(rounded[last], factors[last, panel - 1], 1, 0)

time: 198 us -> 196 us (0.990)
  blocking collectives: 0 us -> 13.9 us
  waiting for transfers between devices: 77.1 us -> 67.4 us
  starting transfers between devices: 69.5 us -> 65.8 us
    all_to_all x0 -> x1, blocking collectives: none -> 13.9 us  [exchange(): lax.all_to_all(blocks, 'row', split_axis=0, concat_axis=0, tiled=True, ax...]
    all_to_all x9 -> x8, waiting for transfers between devices: 68.2 us -> 58.4 us  [exchange(): lax.all_to_all(blocks, 'row', split_axis=0, concat_axis=0, tiled=True, ax...]
    all_to_all x9 -> x8, starting transfers between devices: 32.5 us -> 28.9 us  [exchange(): lax.all_to_all(blocks, 'row', split_axis=0, concat_axis=0, tiled=True, ax...]
  transfers between devices with their start and end apart: 14 -> 13, of which waited for: 12 -> 11; matrix products, arithmetic and copies ran while one was open for 16% -> 15% of each run, Pallas kernels for 1% -> 1%
where the time goes in v6:
time: 196 us; the launch traced here: 195 us
  waiting for transfers between devices  67.4 us (34%)
  starting transfers between devices  65.8 us (34%)
  matrix products  16.6 us (8%)
  local copies, waits for them, and re-layouts  15.6 us (8%)
  Pallas kernels  14.1 us (7%)
  blocking collectives  13.9 us (7%)
    all_to_all x8, waiting for transfers between devices, exchange(): lax.all_to_all(blocks, 'row', split_axis=0, concat_axis=0, tiled=True, ax...  58.4 us
    all_to_all x8, starting transfers between devices, exchange(): lax.all_to_all(blocks, 'row', split_axis=0, concat_axis=0, tiled=True, ax...  28.9 us
    ppermute x4, starting transfers between devices, swap(): return lax.ppermute(value, 'row', pairs)  26.2 us
    dot_general x16, matrix products, dot(): lax.dot_general(left, right, (((left_dim,), (right_dim,)), ((), ())), pre...  16.6 us
    all_to_all x1, blocking collectives, exchange(): lax.all_to_all(blocks, 'row', split_axis=0, concat_axis=0, tiled=True, ax...  13.9 us
    all_to_all x1, starting transfers between devices, shards(): lax.all_to_all(table, 'src', split_axis=0, concat_axis=0, tiled=True)  10.8 us
    pallas_call x1, Pallas kernels, weigh(): pl.pallas_call(weigh_kernel, out_shape=jax.ShapeDtypeStruct((panels, tabl...  7.71 us
    all_to_all x1, waiting for transfers between devices, shards(): lax.all_to_all(table, 'src', split_axis=0, concat_axis=0, tiled=True)  6.57 us
  transfers between devices with their start and end apart: 13, of which 11 were waited for; matrix products, arithmetic and copies ran while one was open for 15% of the time, Pallas kernels for 1%

profile of v6, /device:TPU:1, one launch (start us, length us, event | category | flops | bytes accessed | tf_op | source)
XLA Modules:
  0.0 194.9 jit_solution(5337387244732767926)
XLA Ops:
  0.6 8.8 %collective-permute-start.1 = (bf16[10,64,2048]{2,1,0:T(8,128)(2,1)}, bf16[10,64,2048]{2,1,0:T(8,128)(2,1)}, u32[]{:S(2)}, u32[]{:S(2)}) collective-permute-start(bf16[10,64,2048]{2,1,0:T(8,128)(2,1)} %param.6), channel_id=1, source_target_pairs={{0,1},{1,0},{2,3},{3,2},{4,5},{5,4},{6,7},{7,6},{8,9},{9,8},{10,11... | collective-permute-start | bytes 7864328 | tf_op jit(solution)/shard_map/ppermute | solution.py:156
  10.7 1.9 collective-permute-start
  14.9 4.0 %all-to-all-start = ((bf16[16,64,128]{2,1,0:T(8,128)(2,1)}), bf16[16,64,128]{2,1,0:T(8,128)(2,1)S(1)}, u32[]{:S(2)}, u32[]{:S(2)}) async-start(bf16[16,64,128]{2,1,0:T(8,128)(2,1)} %broadcast_in_dim.8), calls=%async_computation | async-start | bytes 524288 | tf_op jit(solution)/shard_map/all_to_all | solution.py:166
  19.0 2.8 %slice_bitcast_fusion.17 = (bf16[64,2048]{1,0:T(8,128)(2,1)S(1)}, bf16[64,2048]{1,0:T(8,128)(2,1)}, bf16[64,2048]{1,0:T(8,128)(2,1)}, bf16[64,2048]{1,0:T(8,128)...) fusion(bf16[10,64,2048]{2,1,0:T(8,128)(2,1)} %param.6), kind=kLoop, calls=%fused_computation.78 | loop fusion | bytes 5242880 | tf_op jit(solution)/shard_map/squeeze | solution.py:200
  21.7 2.9 %slice_bitcast_fusion.2 = (bf16[64,2048]{1,0:T(8,128)(2,1)S(1)}, bf16[64,2048]{1,0:T(8,128)(2,1)}, bf16[64,2048]{1,0:T(8,128)(2,1)}, bf16[64,2048]{1,0:T(8,128)(...) fusion(bf16[10,64,2048]{2,1,0:T(8,128)(2,1)} %collective-permut, ...), kind=kLoop, calls=%fused_computation.63 | loop fusion | bytes 5242880 | tf_op jit(solution)/shard_map/squeeze | solution.py:200
  24.7 7.0 %all-to-all-done.got_ref = bf16[16,64,128]{2,1,0:T(8,128)(2,1)S(1)} async-done(((bf16[16,64,128]{2,1,0:T(8,128)(2,1)}), bf16[16,64,128]{2,1,0:T(8,128)(2,1)S(1)}, u32[]{:S(2)}, u32[]{:S(2)}) %all-to-all-start) | async-done | bytes 262176 | tf_op jit(solution)/shard_map/all_to_all | solution.py:166
  32.7 3.6 %all-to-all-start.1 = ((bf16[16,64,128]{2,1,0:T(8,128)(2,1)}), bf16[16,64,128]{2,1,0:T(8,128)(2,1)S(1)}, u32[]{:S(2)}, u32[]{:S(2)}) async-start(bf16[16,64,128]{2,1,0:T(8,128)(2,1)} %shard_map.68), calls=%async_computation.1 | async-start | bytes 524288 | tf_op jit(solution)/shard_map/all_to_all | solution.py:166
  36.3 3.2 %collective-permute-start.2 = (bf16[5,64,2048]{2,1,0:T(8,128)(2,1)}, bf16[5,64,2048]{2,1,0:T(8,128)(2,1)}, u32[]{:S(2)}, u32[]{:S(2)}) collective-permute-start(bf16[5,64,2048]{2,1,0:T(8,128)(2,1)} %param.7), channel_id=1, source_target_pairs={{0,1},{1,0},{2,3},{3,2},{4,5},{5,4},{6,7},{7,6},{8,9},{9,8},{10,11... | collective-permute-start | bytes 3932168 | tf_op jit(solution)/shard_map/ppermute | solution.py:156
  40.8 7.4 %all-to-all-done.1.got_ref = bf16[16,64,128]{2,1,0:T(8,128)(2,1)S(1)} async-done(((bf16[16,64,128]{2,1,0:T(8,128)(2,1)}), bf16[16,64,128]{2,1,0:T(8,128)(2,1)S(1)}, u32[]{:S(2)}, u32[]{:S(2)}) %all-to-all-start.1) | async-done | bytes 262176 | tf_op jit(solution)/shard_map/all_to_all | solution.py:166
  49.3 3.5 %all-to-all-start.2 = ((bf16[16,64,128]{2,1,0:T(8,128)(2,1)}), bf16[16,64,128]{2,1,0:T(8,128)(2,1)S(1)}, u32[]{:S(2)}, u32[]{:S(2)}) async-start(bf16[16,64,128]{2,1,0:T(8,128)(2,1)} %shard_map.69), calls=%async_computation.2 | async-start | bytes 524288 | tf_op jit(solution)/shard_map/all_to_all | solution.py:166
  52.9 2.3 %slice_bitcast_fusion.15 = (bf16[64,2048]{1,0:T(8,128)(2,1)}, bf16[64,2048]{1,0:T(8,128)(2,1)}, bf16[64,2048]{1,0:T(8,128)(2,1)}, bf16[64,2048]{1,0:T(8,128)(2,1)}, bf16[64,2048]{1,0:T(8,128)(2,1)S(1)}) fusion(bf16[5,64,2048]{2,1,0:T(8,128)(2,1)} %param.7), kind=kLoop, calls=%fused_computation.76 | loop fusion | bytes 2621440 | tf_op jit(solution)/shard_map/squeeze | solution.py:196
  56.9 6.7 %all-to-all-done.2.got_ref = bf16[16,64,128]{2,1,0:T(8,128)(2,1)S(1)} async-done(((bf16[16,64,128]{2,1,0:T(8,128)(2,1)}), bf16[16,64,128]{2,1,0:T(8,128)(2,1)S(1)}, u32[]{:S(2)}, u32[]{:S(2)}) %all-to-all-start.2) | async-done | bytes 262176 | tf_op jit(solution)/shard_map/all_to_all | solution.py:166
  64.7 3.5 %all-to-all-start.3 = ((bf16[16,64,128]{2,1,0:T(8,128)(2,1)}), bf16[16,64,128]{2,1,0:T(8,128)(2,1)S(1)}, u32[]{:S(2)}, u32[]{:S(2)}) async-start(bf16[16,64,128]{2,1,0:T(8,128)(2,1)} %copy-done.4), calls=%async_computation.3 | async-start | bytes 524288 | tf_op jit(solution)/shard_map/all_to_all | solution.py:166
  68.2 1.5 convolution_subtract_fusion.2
  71.6 7.1 %all-to-all-done.3.got_ref = bf16[16,64,128]{2,1,0:T(8,128)(2,1)S(1)} async-done(((bf16[16,64,128]{2,1,0:T(8,128)(2,1)}), bf16[16,64,128]{2,1,0:T(8,128)(2,1)S(1)}, u32[]{:S(2)}, u32[]{:S(2)}) %all-to-all-start.3) | async-done | bytes 262176 | tf_op jit(solution)/shard_map/all_to_all | solution.py:166
  79.8 3.5 %all-to-all-start.4 = ((bf16[16,64,128]{2,1,0:T(8,128)(2,1)}), bf16[16,64,128]{2,1,0:T(8,128)(2,1)S(1)}, u32[]{:S(2)}, u32[]{:S(2)}) async-start(bf16[16,64,128]{2,1,0:T(8,128)(2,1)} %shard_map.71), calls=%async_computation.4 | async-start | bytes 524288 | tf_op jit(solution)/shard_map/all_to_all | solution.py:166
  83.4 2.2 %slice_bitcast_fusion = (bf16[64,2048]{1,0:T(8,128)(2,1)S(1)}, bf16[64,2048]{1,0:T(8,128)(2,1)S(1)}, bf16[64,2048]{1,0:T(8,128)(2,1)}, bf16[64,2048]{1,0:T(8,128)(2,1)}, bf16[64,2048]{1,0:T(8,128)(2,1)S(1)}) fusion(bf16[5,64,2048]{2,1,0:T(8,128)(2,1)} %collective-permute-done.2), kind=kLoop, calls=%fused_computation.61 | loop fusion | bytes 2621440 | tf_op jit(solution)/shard_map/squeeze | solution.py:196
  87.3 6.5 %all-to-all-done.4.got_ref = bf16[16,64,128]{2,1,0:T(8,128)(2,1)S(1)} async-done(((bf16[16,64,128]{2,1,0:T(8,128)(2,1)}), bf16[16,64,128]{2,1,0:T(8,128)(2,1)S(1)}, u32[]{:S(2)}, u32[]{:S(2)}) %all-to-all-start.4) | async-done | bytes 262176 | tf_op jit(solution)/shard_map/all_to_all | solution.py:166
  95.1 3.7 %all-to-all-start.5 = ((bf16[16,64,128]{2,1,0:T(8,128)(2,1)}), bf16[16,64,128]{2,1,0:T(8,128)(2,1)S(1)}, u32[]{:S(2)}, u32[]{:S(2)}) async-start(bf16[16,64,128]{2,1,0:T(8,128)(2,1)} %copy-done.6), calls=%async_computation.5 | async-start | bytes 524288 | tf_op jit(solution)/shard_map/all_to_all | solution.py:166
  98.8 1.5 fusion.6.base_ref
  101.0 8.9 %all-to-all-done.5.got_ref = bf16[16,64,128]{2,1,0:T(8,128)(2,1)S(1)} async-done(((bf16[16,64,128]{2,1,0:T(8,128)(2,1)}), bf16[16,64,128]{2,1,0:T(8,128)(2,1)S(1)}, u32[]{:S(2)}, u32[]{:S(2)}) %all-to-all-start.5) | async-done | bytes 262176 | tf_op jit(solution)/shard_map/all_to_all | solution.py:166
  111.0 3.5 %all-to-all-start.6 = ((bf16[16,64,128]{2,1,0:T(8,128)(2,1)}), bf16[16,64,128]{2,1,0:T(8,128)(2,1)S(1)}, u32[]{:S(2)}, u32[]{:S(2)}) async-start(bf16[16,64,128]{2,1,0:T(8,128)(2,1)} %get-tuple-element.18), calls=%async_computation.6 | async-start | bytes 524288 | tf_op jit(solution)/shard_map/all_to_all | solution.py:166
  114.5 2.1 %fusion.51 = f32[64,2048]{1,0:T(8,128)} fusion(bf16[64,2048]{1,0:T(8,128)(2,1)} %get-tuple-element.37, bf16[64,2048]{1,0:T(8,128)(2,1)S(1)} %copy-done.16, pred[]{:T(512)S(6)} %eq.4, f32[64,128]{1,0:T(8,128)S(1)} %get-tuple-element.17), kind=kOutput, calls=%fused_computation.102 | convolution fusion | flops 35921920 | bytes 1081345 | tf_op jit(solution)/shard_map/dot_general | solution.py:17
  118.0 1.5 convolution_add_fusion.2.part_ref
  119.5 5.5 %all-to-all-done.6.got_ref = bf16[16,64,128]{2,1,0:T(8,128)(2,1)S(1)} async-done(((bf16[16,64,128]{2,1,0:T(8,128)(2,1)}), bf16[16,64,128]{2,1,0:T(8,128)(2,1)S(1)}, u32[]{:S(2)}, u32[]{:S(2)}) %all-to-all-start.6) | async-done | bytes 262176 | tf_op jit(solution)/shard_map/all_to_all | solution.py:166
  126.0 3.5 %all-to-all-start.7 = ((bf16[16,64,128]{2,1,0:T(8,128)(2,1)}), bf16[16,64,128]{2,1,0:T(8,128)(2,1)S(1)}, u32[]{:S(2)}, u32[]{:S(2)}) async-start(bf16[16,64,128]{2,1,0:T(8,128)(2,1)} %get-tuple-element.20), calls=%async_computation.7 | async-start | bytes 524288 | tf_op jit(solution)/shard_map/all_to_all | solution.py:166
  131.2 9.2 %all-to-all-done.7.got_ref = bf16[16,64,128]{2,1,0:T(8,128)(2,1)S(1)} async-done(((bf16[16,64,128]{2,1,0:T(8,128)(2,1)}), bf16[16,64,128]{2,1,0:T(8,128)(2,1)S(1)}, u32[]{:S(2)}, u32[]{:S(2)}) %all-to-all-start.7) | async-done | bytes 262176 | tf_op jit(solution)/shard_map/all_to_all | solution.py:166
  140.7 13.9 %all_to_all.50 = bf16[16,64,128]{2,1,0:T(8,128)(2,1)S(1)} all-to-all(bf16[16,64,128]{2,1,0:T(8,128)(2,1)S(1)} %get-tuple-element.24), channel_id=1, replica_groups={{0,2,4,6,8,10,12,14,16,18,20,22,24,26,28,30},{1,3,5,7,9,11,13,15,17,19,..., dimensions={0} | all-to-all | bytes 524288 | tf_op jit(solution)/shard_map/all_to_all | solution.py:166
  154.8 12.2 %collective-permute-start.3 = (f32[5,64,64]{2,1,0:T(8,128)S(1)}, f32[5,64,64]{2,1,0:T(8,128)S(1)}, u32[]{:S(2)}, u32[]{:S(2)}) collective-permute-start(f32[5,64,64]{2,1,0:T(8,128)S(1)} %get-tuple-element.64), channel_id=1, source_target_pairs={{0,1},{1,0},{2,3},{3,2},{4,5},{5,4},{6,7},{7,6},{8,9},{9,8},{10,11... | collective-permute-start | bytes 245768 | tf_op jit(solution)/shard_map/ppermute | solution.py:156
  169.0 10.8 %all-to-all-start.9 = ((bf16[16,20,128]{2,1,0:T(8,128)(2,1)}), bf16[16,20,128]{2,1,0:T(8,128)(2,1)S(1)}, u32[]{:S(2)}, u32[]{:S(2)}) async-start(bf16[16,20,128]{2,1,0:T(8,128)(2,1)} %copy.29), calls=%async_computation.9 | async-start | bytes 196608 | tf_op jit(solution)/shard_map/all_to_all | solution.py:243
  180.6 6.6 %all-to-all-done.9.table_ref = bf16[16,20,128]{2,1,0:T(8,128)(2,1)S(1)} async-done(((bf16[16,20,128]{2,1,0:T(8,128)(2,1)}), bf16[16,20,128]{2,1,0:T(8,128)(2,1)S(1)}, u32[]{:S(2)}, u32[]{:S(2)}) %all-to-all-start.9) | async-done | bytes 81952 | tf_op jit(solution)/shard_map/all_to_all | solution.py:243
  187.2 7.7 %shard_map.76 = f32[5,4,16]{2,1,0:T(4,128)} custom-call(bf16[16,20,128]{2,1,0:T(8,128)(2,1)S(1)} %all-to-all-done.9.table_ref, s32[16,4,1024]{2,1,0:T(4,128)S(1)} %bitcast.166, f32[16,1024]{1,0:T(8,128)S(1)} %copy-done.7), custom_call_target="tpu_custom_call" | custom-call | tf_op jit(solution)/shard_map/pallas_call | solution.py:135
  (92 shorter events, 24.2 us)
Async XLA Ops:
  0.6 21.1 %collective-permute-start.1 = (bf16[10,64,2048]{2,1,0:T(8,128)(2,1)}, bf16[10,64,2048]{2,1,0:T(8,128)(2,1)}, u32[]{:S(2)}, u32[]{:S(2)}) collective-permute-start(bf16[10,64,2048]{2,1,0:T(8,128)(2,1)} %param.6), channel_id=1, source_target_pairs={{0,1},{1,0},{2,3},{3,2},{4,5},{5,4},{6,7},{7,6},{8,9},{9,8},{10,11... | collective-permute-start | bytes 7864328 | tf_op jit(solution)/shard_map/ppermute | solution.py:156
  10.7 3.4 %collective-permute-start = (bf16[5,64,64]{2,1,0:T(8,128)(2,1)S(1)}, bf16[5,64,64]{2,1,0:T(8,128)(2,1)S(1)}, u32[]{:S(2)}, u32[]{:S(2)}) collective-permute-start(bf16[5,64,64]{2,1,0:T(8,128)(2,1)S(1)} %bitcast.170), channel_id=1, source_target_pairs={{0,1},{1,0},{2,3},{3,2},{4,5},{5,4},{6,7},{7,6},{8,9},{9,8},{10,11... | collective-permute-start | bytes 122888 | tf_op jit(solution)/shard_map/ppermute | solution.py:156
  14.9 16.7 %all-to-all-start = ((bf16[16,64,128]{2,1,0:T(8,128)(2,1)}), bf16[16,64,128]{2,1,0:T(8,128)(2,1)S(1)}, u32[]{:S(2)}, u32[]{:S(2)}) async-start(bf16[16,64,128]{2,1,0:T(8,128)(2,1)} %broadcast_in_dim.8), calls=%async_computation | async-start | bytes 524288 | tf_op jit(solution)/shard_map/all_to_all | solution.py:166
  21.7 17.8 %copy-start.8 = (bf16[64,2048]{1,0:T(8,128)(2,1)}, bf16[64,2048]{1,0:T(8,128)(2,1)S(1)}, u32[]{:S(2)}) copy-start(bf16[64,2048]{1,0:T(8,128)(2,1)S(1)} %get-tuple-element.52) | copy-start | bytes 786436
  32.7 15.6 %all-to-all-start.1 = ((bf16[16,64,128]{2,1,0:T(8,128)(2,1)}), bf16[16,64,128]{2,1,0:T(8,128)(2,1)S(1)}, u32[]{:S(2)}, u32[]{:S(2)}) async-start(bf16[16,64,128]{2,1,0:T(8,128)(2,1)} %shard_map.68), calls=%async_computation.1 | async-start | bytes 524288 | tf_op jit(solution)/shard_map/all_to_all | solution.py:166
  36.3 47.1 %collective-permute-start.2 = (bf16[5,64,2048]{2,1,0:T(8,128)(2,1)}, bf16[5,64,2048]{2,1,0:T(8,128)(2,1)}, u32[]{:S(2)}, u32[]{:S(2)}) collective-permute-start(bf16[5,64,2048]{2,1,0:T(8,128)(2,1)} %param.7), channel_id=1, source_target_pairs={{0,1},{1,0},{2,3},{3,2},{4,5},{5,4},{6,7},{7,6},{8,9},{9,8},{10,11... | collective-permute-start | bytes 3932168 | tf_op jit(solution)/shard_map/ppermute | solution.py:156
  40.8 14.4 %copy-start.10 = (bf16[64,2048]{1,0:T(8,128)(2,1)S(1)}, bf16[64,2048]{1,0:T(8,128)(2,1)}, u32[]{:S(2)}) copy-start(bf16[64,2048]{1,0:T(8,128)(2,1)} %get-tuple-element.50) | copy-start | bytes 786436
  48.3 21.5 %copy-start = (bf16[16,64,128]{2,1,0:T(8,128)(2,1)}, bf16[16,64,128]{2,1,0:T(8,128)(2,1)S(1)}, u32[]{:S(2)}) copy-start(bf16[16,64,128]{2,1,0:T(8,128)(2,1)S(1)} %all-to-all-done.1.got_ref) | copy-start | bytes 786436
  49.3 14.3 %all-to-all-start.2 = ((bf16[16,64,128]{2,1,0:T(8,128)(2,1)}), bf16[16,64,128]{2,1,0:T(8,128)(2,1)S(1)}, u32[]{:S(2)}, u32[]{:S(2)}) async-start(bf16[16,64,128]{2,1,0:T(8,128)(2,1)} %shard_map.69), calls=%async_computation.2 | async-start | bytes 524288 | tf_op jit(solution)/shard_map/all_to_all | solution.py:166
  52.9 3.7 %copy-start.14 = (bf16[64,2048]{1,0:T(8,128)(2,1)S(1)}, bf16[64,2048]{1,0:T(8,128)(2,1)}, u32[]{:S(2)}) copy-start(bf16[64,2048]{1,0:T(8,128)(2,1)} %get-tuple-element.49) | copy-start | bytes 786436
  52.9 3.7 %copy-start.17 = (bf16[64,2048]{1,0:T(8,128)(2,1)S(1)}, bf16[64,2048]{1,0:T(8,128)(2,1)}, u32[]{:S(2)}) copy-start(bf16[64,2048]{1,0:T(8,128)(2,1)} %get-tuple-element.39) | copy-start | bytes 786436
  64.7 14.1 %all-to-all-start.3 = ((bf16[16,64,128]{2,1,0:T(8,128)(2,1)}), bf16[16,64,128]{2,1,0:T(8,128)(2,1)S(1)}, u32[]{:S(2)}, u32[]{:S(2)}) async-start(bf16[16,64,128]{2,1,0:T(8,128)(2,1)} %copy-done.4), calls=%async_computation.3 | async-start | bytes 524288 | tf_op jit(solution)/shard_map/all_to_all | solution.py:166
  68.2 3.1 %copy-start.18 = (bf16[64,2048]{1,0:T(8,128)(2,1)S(1)}, bf16[64,2048]{1,0:T(8,128)(2,1)}, u32[]{:S(2)}) copy-start(bf16[64,2048]{1,0:T(8,128)(2,1)} %get-tuple-element.45) | copy-start | bytes 786436
  79.8 14.0 %all-to-all-start.4 = ((bf16[16,64,128]{2,1,0:T(8,128)(2,1)}), bf16[16,64,128]{2,1,0:T(8,128)(2,1)S(1)}, u32[]{:S(2)}, u32[]{:S(2)}) async-start(bf16[16,64,128]{2,1,0:T(8,128)(2,1)} %shard_map.71), calls=%async_computation.4 | async-start | bytes 524288 | tf_op jit(solution)/shard_map/all_to_all | solution.py:166
  83.4 3.6 %copy-start.1 = (bf16[16,64,128]{2,1,0:T(8,128)(2,1)S(1)}, bf16[16,64,128]{2,1,0:T(8,128)(2,1)}, u32[]{:S(2)}) copy-start(bf16[16,64,128]{2,1,0:T(8,128)(2,1)} %copy-done) | copy-start | bytes 786436
  83.4 3.6 %copy-start.23 = (bf16[64,2048]{1,0:T(8,128)(2,1)S(1)}, bf16[64,2048]{1,0:T(8,128)(2,1)}, u32[]{:S(2)}) copy-start(bf16[64,2048]{1,0:T(8,128)(2,1)} %get-tuple-element.57) | copy-start | bytes 786436
  87.3 13.1 %copy-start.3 = (bf16[16,64,128]{2,1,0:T(8,128)(2,1)S(1)}, bf16[16,64,128]{2,1,0:T(8,128)(2,1)}, u32[]{:S(2)}) copy-start(bf16[16,64,128]{2,1,0:T(8,128)(2,1)} %copy-done.2) | copy-start | bytes 786436
  95.1 5.3 %copy-start.22 = (bf16[64,2048]{1,0:T(8,128)(2,1)S(1)}, bf16[64,2048]{1,0:T(8,128)(2,1)}, u32[]{:S(2)}) copy-start(bf16[64,2048]{1,0:T(8,128)(2,1)} %get-tuple-element.55) | copy-start | bytes 786436
  95.1 5.3 %copy-start.24 = (bf16[64,2048]{1,0:T(8,128)(2,1)S(1)}, bf16[64,2048]{1,0:T(8,128)(2,1)}, u32[]{:S(2)}) copy-start(bf16[64,2048]{1,0:T(8,128)(2,1)} %get-tuple-element.61) | copy-start | bytes 786436
  95.1 14.8 %all-to-all-start.5 = ((bf16[16,64,128]{2,1,0:T(8,128)(2,1)}), bf16[16,64,128]{2,1,0:T(8,128)(2,1)S(1)}, u32[]{:S(2)}, u32[]{:S(2)}) async-start(bf16[16,64,128]{2,1,0:T(8,128)(2,1)} %copy-done.6), calls=%async_computation.5 | async-start | bytes 524288 | tf_op jit(solution)/shard_map/all_to_all | solution.py:166
  100.4 14.1 %copy-start.16 = (bf16[64,2048]{1,0:T(8,128)(2,1)S(1)}, bf16[64,2048]{1,0:T(8,128)(2,1)}, u32[]{:S(2)}) copy-start(bf16[64,2048]{1,0:T(8,128)(2,1)} %get-tuple-element.47) | copy-start | bytes 786436
  100.8 15.8 %copy-start.15 = (bf16[64,2048]{1,0:T(8,128)(2,1)S(1)}, bf16[64,2048]{1,0:T(8,128)(2,1)}, u32[]{:S(2)}) copy-start(bf16[64,2048]{1,0:T(8,128)(2,1)} %get-tuple-element.46) | copy-start | bytes 786436
  111.0 14.0 %all-to-all-start.6 = ((bf16[16,64,128]{2,1,0:T(8,128)(2,1)}), bf16[16,64,128]{2,1,0:T(8,128)(2,1)S(1)}, u32[]{:S(2)}, u32[]{:S(2)}) async-start(bf16[16,64,128]{2,1,0:T(8,128)(2,1)} %get-tuple-element.18), calls=%async_computation.6 | async-start | bytes 524288 | tf_op jit(solution)/shard_map/all_to_all | solution.py:166
  116.6 12.9 %copy-start.11 = (bf16[64,2048]{1,0:T(8,128)(2,1)S(1)}, bf16[64,2048]{1,0:T(8,128)(2,1)}, u32[]{:S(2)}) copy-start(bf16[64,2048]{1,0:T(8,128)(2,1)} %get-tuple-element.50) | copy-start | bytes 786436
  116.6 12.9 %copy-start.13 = (bf16[64,2048]{1,0:T(8,128)(2,1)S(1)}, bf16[64,2048]{1,0:T(8,128)(2,1)}, u32[]{:S(2)}) copy-start(bf16[64,2048]{1,0:T(8,128)(2,1)} %get-tuple-element.40) | copy-start | bytes 786436
  118.0 12.9 %copy-start.9 = (bf16[64,2048]{1,0:T(8,128)(2,1)S(1)}, bf16[64,2048]{1,0:T(8,128)(2,1)}, u32[]{:S(2)}) copy-start(bf16[64,2048]{1,0:T(8,128)(2,1)} %copy-done.8) | copy-start | bytes 786436
  118.0 12.9 %copy-start.12 = (bf16[64,2048]{1,0:T(8,128)(2,1)S(1)}, bf16[64,2048]{1,0:T(8,128)(2,1)}, u32[]{:S(2)}) copy-start(bf16[64,2048]{1,0:T(8,128)(2,1)} %get-tuple-element.42) | copy-start | bytes 786436
  126.0 14.4 %all-to-all-start.7 = ((bf16[16,64,128]{2,1,0:T(8,128)(2,1)}), bf16[16,64,128]{2,1,0:T(8,128)(2,1)S(1)}, u32[]{:S(2)}, u32[]{:S(2)}) async-start(bf16[16,64,128]{2,1,0:T(8,128)(2,1)} %get-tuple-element.20), calls=%async_computation.7 | async-start | bytes 524288 | tf_op jit(solution)/shard_map/all_to_all | solution.py:166
  131.1 56.0 %copy-start.5 = (s32[16,1024,4]{1,2,0:T(4,128)S(1)}, s32[16,1024,4]{1,2,0:T(4,128)}, u32[]{:S(2)}) copy-start(s32[16,1024,4]{1,2,0:T(4,128)} %param.8) | copy-start | bytes 786436
  131.1 56.0 %copy-start.7 = (f32[16,1024]{1,0:T(8,128)S(1)}, f32[16,1024]{1,0:T(8,128)}, u32[]{:S(2)}) copy-start(f32[16,1024]{1,0:T(8,128)} %weights_ref.1) | copy-start | bytes 196612
  154.8 13.3 %collective-permute-start.3 = (f32[5,64,64]{2,1,0:T(8,128)S(1)}, f32[5,64,64]{2,1,0:T(8,128)S(1)}, u32[]{:S(2)}, u32[]{:S(2)}) collective-permute-start(f32[5,64,64]{2,1,0:T(8,128)S(1)} %get-tuple-element.64), channel_id=1, source_target_pairs={{0,1},{1,0},{2,3},{3,2},{4,5},{5,4},{6,7},{7,6},{8,9},{9,8},{10,11... | collective-permute-start | bytes 245768 | tf_op jit(solution)/shard_map/ppermute | solution.py:156
  169.0 18.2 %all-to-all-start.9 = ((bf16[16,20,128]{2,1,0:T(8,128)(2,1)}), bf16[16,20,128]{2,1,0:T(8,128)(2,1)S(1)}, u32[]{:S(2)}, u32[]{:S(2)}) async-start(bf16[16,20,128]{2,1,0:T(8,128)(2,1)} %copy.29), calls=%async_computation.9 | async-start | bytes 196608 | tf_op jit(solution)/shard_map/all_to_all | solution.py:243
  (6 other events, 9.4 us)
